TPU v7x, 32 devices: a whole 2x2x4 slice. The times are simulated.
32 devices in a mesh: dp: 8 (over z, y), blk: 4 (over x, core).
Axes of the slice: x: 2, y: 2, z: 4, core: 2. Of those that a mesh axis runs over, the one named last changes fastest.
Arguments:
- frames: bfloat16 [8, 1024, 1024], P('dp', 'blk'), may hold values from -6 to 6
- skip_frames: bfloat16 [8, 1024, 1024], P('dp', 'blk'), may hold values from -6 to 6
- cotangent: bfloat16 [8, 1024, 1024], P('dp', 'blk'), may hold values from -6 to 6
- seg_ids: int32 [8, 1024], P('dp', 'blk'), may hold values from 0 to 31, as said below
- positions: int32 [8, 1024], P('dp', 'blk'), may hold values from 0 to 511, as said below
- w_skip: float32 [2048, 1024], P('dp'), may hold values from -0.125 to 0.125
- b_skip: float32 [1024], P('dp'), may hold values from -1 to 1
- gain_attn: float32 [1024], P('dp'), may hold values from 0.25 to 1.75
- bias_attn: float32 [1024], P('dp'), may hold values from -1 to 1
- w_qkv: float32 [1024, 3072], P('dp'), may hold values from -0.1875 to 0.1875
- w_out: float32 [1024, 1024], P('dp'), may hold values from -0.375 to 0.375
- gain_ffn: float32 [1024], P('dp'), may hold values from 0.25 to 1.75
- bias_ffn: float32 [1024], P('dp'), may hold values from -1 to 1
- w_up: float32 [1024, 4096], P('dp'), may hold values from -0.1875 to 0.1875
- b_up: float32 [4096], P('dp'), may hold values from -1 to 1
- w_down: float32 [4096, 1024], P('dp'), may hold values from -0.09375 to 0.09375
- b_down: float32 [1024], P('dp'), may hold values from -1 to 1
Outputs:
- output: bfloat16 [8, 1024, 1024], P('dp', 'blk')
- grad_frames: bfloat16 [8, 1024, 1024], P('dp', 'blk')
- grad_skip: bfloat16 [8, 1024, 1024], P('dp', 'blk')
- grad_w_skip: float32 [2048, 1024], P('dp')
- grad_b_skip: float32 [1024], P('dp')
- grad_gain_attn: float32 [1024], P('dp')
- grad_bias_attn: float32 [1024], P('dp')
- grad_w_qkv: float32 [1024, 3072], P('dp')
- grad_w_out: float32 [1024, 1024], P('dp')
- grad_gain_ffn: float32 [1024], P('dp')
- grad_bias_ffn: float32 [1024], P('dp')
- grad_w_up: float32 [1024, 4096], P('dp')
- grad_b_up: float32 [4096], P('dp')
- grad_w_down: float32 [4096, 1024], P('dp')
- grad_b_down: float32 [1024], P('dp')
Inputs may be any that keep to these rules, and one draw needn't show every extreme that they name: `seg_ids`: each row holds exactly 32 items, packed back to back in a drawn order and numbered 0, 1, 2, ... in that order; frame v of the packed order (v from 0) lies at slot (v % 4) * 256 + v // 4 of the row. `positions`: positions count from 0 within an item along the packed order; every row holds exactly one item of 512 frames.
All inputs are finite; a program needn't handle non-finite values.
Results may differ from a plain program's by a relative error of at most 0.025.
Values may be sent and summed in bfloat16 or wider, within the bound.
A program may use at most 256 MiB of HBM per device.

v0:
```python
import math

import jax
import jax.numpy as jnp
from jax import lax
from jax.sharding import PartitionSpec as P

H = 16


EPSILON = 1e-05


def layer_norm(hidden, gain, offset):
    centred = hidden - jnp.mean(hidden, axis=-1, keepdims=True)
    spread = jnp.mean(centred * centred, axis=-1, keepdims=True)
    return centred * lax.rsqrt(spread + EPSILON) * gain + offset


def alibi_slopes(head_count):
    return 2.0 ** (-8.0 * (jnp.arange(head_count) + 1.0) / head_count)


def gelu_exact(pre_act):
    return jax.nn.gelu(pre_act, approximate=False)


def exp_scores(query_blk, key_blk, shift_blk, seg_q, pos_q, seg_k, pos_k, slopes):
    raw_scores = (
        jnp.einsum("qhd,khd->hqk", query_blk, key_blk, preferred_element_type=jnp.float32) * 0.125
    )
    distance = jnp.abs(pos_q[:, None] - pos_k[None, :]).astype(jnp.float32)
    raw_scores = raw_scores - slopes[:, None, None] * distance[None]
    same_item = (seg_q[:, None] == seg_k[None, :])[None]
    return jnp.where(
        same_item, jnp.exp(jnp.where(same_item, raw_scores - shift_blk[:, :, None], 0.0)), 0.0
    )


def grad_terms(exp_terms, scaled_blk, value_blk, total_blk):
    grad_exp = jnp.einsum("qhd,khd->hqk", scaled_blk, value_blk, preferred_element_type=jnp.float32)
    return exp_terms * (grad_exp + total_blk[:, :, None])


def over_blocks(row_count, step_fn, state_init):
    block_size = math.gcd(row_count, 512)

    def visit(block_index, state_now):
        return step_fn(state_now, block_index * block_size, block_size)

    return lax.fori_loop(0, row_count // block_size, visit, state_init)


def col_product(left_rows, right_rows):
    return jnp.einsum("rk,rn->kn", left_rows, right_rows, preferred_element_type=jnp.float32)


def per_device(
    frames,
    skip_frames,
    cotangent,
    seg_ids,
    positions,
    w_skip,
    b_skip,
    gain_attn,
    bias_attn,
    w_qkv,
    w_out,
    gain_ffn,
    bias_ffn,
    w_up,
    b_up,
    w_down,
    b_down,
):
    low_type = jnp.bfloat16
    seg_own = seg_ids[0]
    pos_own = positions[0]
    seg_all, pos_all = (
        lax.all_gather(seg_own, "blk", axis=0, tiled=True),
        lax.all_gather(pos_own, "blk", axis=0, tiled=True),
    )
    (
        ws_full,
        bs_full,
        ga_full,
        ba_full,
        wqkv_full,
        wout_full,
        gf_full,
        bf_full,
        wup_full,
        bup_full,
        wdown_full,
        bdown_full,
    ) = (
        lax.all_gather(w_skip.astype(low_type), "dp", axis=0, tiled=True),
        lax.all_gather(b_skip.astype(low_type), "dp", axis=0, tiled=True),
        lax.all_gather(gain_attn.astype(low_type), "dp", axis=0, tiled=True),
        lax.all_gather(bias_attn.astype(low_type), "dp", axis=0, tiled=True),
        lax.all_gather(w_qkv.astype(low_type), "dp", axis=0, tiled=True),
        lax.all_gather(w_out.astype(low_type), "dp", axis=0, tiled=True),
        lax.all_gather(gain_ffn.astype(low_type), "dp", axis=0, tiled=True),
        lax.all_gather(bias_ffn.astype(low_type), "dp", axis=0, tiled=True),
        lax.all_gather(w_up.astype(low_type), "dp", axis=0, tiled=True),
        lax.all_gather(b_up.astype(low_type), "dp", axis=0, tiled=True),
        lax.all_gather(w_down.astype(low_type), "dp", axis=0, tiled=True),
        lax.all_gather(b_down.astype(low_type), "dp", axis=0, tiled=True),
    )
    skip_bias = bs_full.astype(jnp.float32)
    attn_gain = ga_full.astype(jnp.float32)
    attn_bias = ba_full.astype(jnp.float32)
    ffn_gain = gf_full.astype(jnp.float32)
    ffn_bias = bf_full.astype(jnp.float32)
    up_bias = bup_full.astype(jnp.float32)
    down_bias = bdown_full.astype(jnp.float32)
    slopes = alibi_slopes(H)
    frame_rows = frames[0]
    skip_rows = skip_frames[0]
    grad_rows = cotangent[0]
    joined = jnp.concatenate([frame_rows, skip_rows], axis=1)
    merged = jnp.dot(joined, ws_full, preferred_element_type=jnp.float32) + skip_bias
    normed_low = layer_norm(merged, attn_gain, attn_bias).astype(low_type)
    mixed = jnp.dot(normed_low, wqkv_full, preferred_element_type=jnp.float32).astype(low_type)
    local_rows, model_width = merged.shape
    queries = mixed[:, :model_width].reshape(local_rows, H, -1)
    key_vals = mixed[:, model_width:]
    keys_own = key_vals[:, :model_width].reshape(local_rows, H, -1)
    self_shift = (
        jnp.sum(queries.astype(jnp.float32) * keys_own.astype(jnp.float32), axis=-1) * 0.125
    ).T
    head_zeros = jnp.zeros((local_rows, H, model_width // H), jnp.float32)
    key_piece = lax.all_gather(key_vals, "blk", axis=0, tiled=True)

    def forward_step(state_in, offset, block_size):
        totals_in, summed_in = state_in
        key_block = lax.dynamic_slice_in_dim(key_piece, offset, block_size, 0)
        key_blk = key_block[:, :model_width].reshape(block_size, H, -1)
        value_blk = key_block[:, model_width:].reshape(block_size, H, -1)
        seg_k = lax.dynamic_slice_in_dim(seg_all, offset, block_size, 0)
        pos_k = lax.dynamic_slice_in_dim(pos_all, offset, block_size, 0)
        exp_terms = exp_scores(queries, key_blk, self_shift, seg_own, pos_own, seg_k, pos_k, slopes)
        added = jnp.einsum(
            "hqk,khd->qhd",
            exp_terms.astype(low_type),
            value_blk,
            preferred_element_type=jnp.float32,
        )
        return (totals_in + jnp.sum(exp_terms, axis=-1), summed_in + added)

    totals, summed = over_blocks(
        key_piece.shape[0], forward_step, (jnp.zeros((H, local_rows), jnp.float32), head_zeros)
    )
    attended_f = summed / totals.T[:, :, None]
    attended = attended_f.reshape(local_rows, model_width).astype(low_type)
    middle = merged + jnp.dot(attended, wout_full, preferred_element_type=jnp.float32)
    second = layer_norm(middle, ffn_gain, ffn_bias).astype(low_type)
    hidden = jnp.dot(second, wup_full, preferred_element_type=jnp.float32) + up_bias
    active = gelu_exact(hidden).astype(low_type)
    output = (
        middle + jnp.dot(active, wdown_full, preferred_element_type=jnp.float32) + down_bias
    ).astype(low_type)
    grad_w_down = col_product(active, grad_rows)
    grad_b_down = jnp.sum(grad_rows.astype(jnp.float32), axis=0)
    grad_active = jnp.dot(grad_rows, wdown_full.T, preferred_element_type=jnp.float32)
    _, gelu_pull = jax.vjp(gelu_exact, hidden)
    grad_hidden = gelu_pull(grad_active)[0].astype(low_type)
    grad_w_up = col_product(second, grad_hidden)
    grad_b_up = jnp.sum(grad_hidden.astype(jnp.float32), axis=0)
    grad_second = jnp.dot(grad_hidden, wup_full.T, preferred_element_type=jnp.float32)
    _, ffn_pull = jax.vjp(layer_norm, middle, ffn_gain, ffn_bias)
    grad_middle, grad_gain_ffn, grad_bias_ffn = ffn_pull(grad_second)
    grad_middle = grad_middle + grad_rows.astype(jnp.float32)
    grad_branch = grad_middle.astype(low_type)
    grad_w_out = col_product(attended, grad_branch)
    grad_attended = jnp.dot(grad_branch, wout_full.T, preferred_element_type=jnp.float32).astype(
        low_type
    )
    grad_attended = grad_attended.astype(jnp.float32).reshape(local_rows, H, -1)
    grad_scaled = (grad_attended / totals.T[:, :, None]).astype(low_type)
    grad_total = -jnp.sum(grad_attended * attended_f, axis=-1).T / totals
    fold_init = (
        head_zeros,
        jnp.zeros((H, local_rows), jnp.float32),
        jnp.zeros((seg_all.shape[0], 2 * model_width), jnp.float32),
    )
    backward_key_piece = lax.all_gather(key_vals, "blk", axis=0, tiled=True)

    def backward_step(state_in, offset, block_size):
        key_block = lax.dynamic_slice_in_dim(backward_key_piece, offset, block_size, 0)
        key_blk = key_block[:, :model_width].reshape(block_size, H, -1)
        value_blk = key_block[:, model_width:].reshape(block_size, H, -1)
        seg_k = lax.dynamic_slice_in_dim(seg_all, offset, block_size, 0)
        pos_k = lax.dynamic_slice_in_dim(pos_all, offset, block_size, 0)
        exp_terms = exp_scores(queries, key_blk, self_shift, seg_own, pos_own, seg_k, pos_k, slopes)
        grad_score = grad_terms(exp_terms, grad_scaled, value_blk, grad_total)
        grad_low = grad_score.astype(low_type)
        grad_query = state_in[0] + 0.125 * jnp.einsum(
            "hqk,khd->qhd", grad_low, key_blk, preferred_element_type=jnp.float32
        )
        shift_grad = state_in[1] - jnp.sum(grad_score, axis=-1)
        grad_keys = 0.125 * jnp.einsum(
            "hqk,qhd->khd", grad_low, queries, preferred_element_type=jnp.float32
        )
        grad_values = jnp.einsum(
            "hqk,qhd->khd",
            exp_terms.astype(low_type),
            grad_scaled,
            preferred_element_type=jnp.float32,
        )
        joined_grads = jnp.concatenate(
            [
                grad_keys.reshape(block_size, model_width),
                grad_values.reshape(block_size, model_width),
            ],
            axis=1,
        )
        current = lax.dynamic_slice_in_dim(state_in[2], offset, block_size, 0)
        updated = lax.dynamic_update_slice_in_dim(state_in[2], current + joined_grads, offset, 0)
        return (grad_query, shift_grad, updated)

    folded = over_blocks(backward_key_piece.shape[0], backward_step, fold_init)
    key_sums = lax.psum_scatter(
        folded[2].astype(jnp.bfloat16), "blk", scatter_dimension=0, tiled=True
    ).astype(jnp.float32)
    grad_keys_own = key_sums[:, :model_width].reshape(local_rows, H, -1)
    grad_values_own = key_sums[:, model_width:].reshape(local_rows, H, -1)
    shift_col = folded[1].T[:, :, None]
    grad_query_all = folded[0] + 0.125 * shift_col * keys_own.astype(jnp.float32)
    grad_keys_all = grad_keys_own + 0.125 * shift_col * queries.astype(jnp.float32)
    grad_mixed = jnp.concatenate(
        [
            grad_query_all.reshape(local_rows, model_width),
            grad_keys_all.reshape(local_rows, model_width),
            grad_values_own.reshape(local_rows, model_width),
        ],
        axis=1,
    ).astype(low_type)
    grad_w_qkv = col_product(normed_low, grad_mixed)
    grad_normed = jnp.dot(grad_mixed, wqkv_full.T, preferred_element_type=jnp.float32)
    _, attn_pull = jax.vjp(layer_norm, merged, attn_gain, attn_bias)
    grad_merged_part, grad_gain_attn, grad_bias_attn = attn_pull(grad_normed)
    grad_merged = (grad_merged_part + grad_middle).astype(low_type)
    grad_w_skip = col_product(joined, grad_merged)
    grad_b_skip = jnp.sum(grad_merged.astype(jnp.float32), axis=0)
    grad_joined = jnp.dot(grad_merged, ws_full.T, preferred_element_type=jnp.float32).astype(
        low_type
    )
    grad_frames = grad_joined[:, :model_width][None]
    grad_skip = grad_joined[:, model_width:][None]
    shards = (
        lax.psum_scatter(
            grad_w_skip.astype(jnp.bfloat16), "dp", scatter_dimension=0, tiled=True
        ).astype(jnp.float32),
        lax.psum_scatter(
            grad_b_skip.astype(jnp.bfloat16), "dp", scatter_dimension=0, tiled=True
        ).astype(jnp.float32),
        lax.psum_scatter(
            grad_gain_attn.astype(jnp.bfloat16), "dp", scatter_dimension=0, tiled=True
        ).astype(jnp.float32),
        lax.psum_scatter(
            grad_bias_attn.astype(jnp.bfloat16), "dp", scatter_dimension=0, tiled=True
        ).astype(jnp.float32),
        lax.psum_scatter(
            grad_w_qkv.astype(jnp.bfloat16), "dp", scatter_dimension=0, tiled=True
        ).astype(jnp.float32),
        lax.psum_scatter(
            grad_w_out.astype(jnp.bfloat16), "dp", scatter_dimension=0, tiled=True
        ).astype(jnp.float32),
        lax.psum_scatter(
            grad_gain_ffn.astype(jnp.bfloat16), "dp", scatter_dimension=0, tiled=True
        ).astype(jnp.float32),
        lax.psum_scatter(
            grad_bias_ffn.astype(jnp.bfloat16), "dp", scatter_dimension=0, tiled=True
        ).astype(jnp.float32),
        lax.psum_scatter(
            grad_w_up.astype(jnp.bfloat16), "dp", scatter_dimension=0, tiled=True
        ).astype(jnp.float32),
        lax.psum_scatter(
            grad_b_up.astype(jnp.bfloat16), "dp", scatter_dimension=0, tiled=True
        ).astype(jnp.float32),
        lax.psum_scatter(
            grad_w_down.astype(jnp.bfloat16), "dp", scatter_dimension=0, tiled=True
        ).astype(jnp.float32),
        lax.psum_scatter(
            grad_b_down.astype(jnp.bfloat16), "dp", scatter_dimension=0, tiled=True
        ).astype(jnp.float32),
    )
    reduced = (
        lax.psum(shards[0].astype(jnp.bfloat16), "blk").astype(jnp.float32),
        lax.psum(shards[1].astype(jnp.bfloat16), "blk").astype(jnp.float32),
        lax.psum(shards[2].astype(jnp.bfloat16), "blk").astype(jnp.float32),
        lax.psum(shards[3].astype(jnp.bfloat16), "blk").astype(jnp.float32),
        lax.psum(shards[4].astype(jnp.bfloat16), "blk").astype(jnp.float32),
        lax.psum(shards[5].astype(jnp.bfloat16), "blk").astype(jnp.float32),
        lax.psum(shards[6].astype(jnp.bfloat16), "blk").astype(jnp.float32),
        lax.psum(shards[7].astype(jnp.bfloat16), "blk").astype(jnp.float32),
        lax.psum(shards[8].astype(jnp.bfloat16), "blk").astype(jnp.float32),
        lax.psum(shards[9].astype(jnp.bfloat16), "blk").astype(jnp.float32),
        lax.psum(shards[10].astype(jnp.bfloat16), "blk").astype(jnp.float32),
        lax.psum(shards[11].astype(jnp.bfloat16), "blk").astype(jnp.float32),
    )
    return (
        output[None],
        grad_frames,
        grad_skip,
        reduced[0],
        reduced[1],
        reduced[2],
        reduced[3],
        reduced[4],
        reduced[5],
        reduced[6],
        reduced[7],
        reduced[8],
        reduced[9],
        reduced[10],
        reduced[11],
    )


def solution(mesh):
    in_specs = (
        P("dp", "blk", None),
        P("dp", "blk", None),
        P("dp", "blk", None),
        P("dp", "blk"),
        P("dp", "blk"),
        P("dp", None),
        P("dp"),
        P("dp"),
        P("dp"),
        P("dp", None),
        P("dp", None),
        P("dp"),
        P("dp"),
        P("dp", None),
        P("dp"),
        P("dp", None),
        P("dp"),
    )
    out_specs = (
        P("dp", "blk", None),
        P("dp", "blk", None),
        P("dp", "blk", None),
        P("dp", None),
        P("dp"),
        P("dp"),
        P("dp"),
        P("dp", None),
        P("dp", None),
        P("dp"),
        P("dp"),
        P("dp", None),
        P("dp"),
        P("dp", None),
        P("dp"),
    )
    return jax.shard_map(
        per_device, mesh=mesh, in_specs=in_specs, out_specs=out_specs, check_vma=False
    )
```

profile of v0, /device:TPU:0, one launch (start us, length us, event | category | flops | bytes accessed | tf_op | source)
XLA Modules:
  0.0 1375.8 jit_solution(661847647690635217)
XLA Ops:
  12.0 22.3 %all-gather.2 = bf16[8,1,128]{2,1,0:T(2,128)(2,1)S(1)} all-gather(bf16[1,1,128]{2,1,0:T(2,128)(2,1)S(1)} %convert_bitcast_fusion.5), channel_id=1, replica_groups=mesh['dp'=8,'blk'=4] {'dp'}, dimensions={0}, use_global_device_ids=true | all-gather | bytes 2304 | tf_op jit(solution)/shard_map/all_gather | solution.py:99
  34.3 16.3 %all-gather.4 = bf16[8,1,128]{2,1,0:T(2,128)(2,1)S(1)} all-gather(bf16[1,1,128]{2,1,0:T(2,128)(2,1)S(1)} %convert_bitcast_fusion.3), channel_id=1, replica_groups=mesh['dp'=8,'blk'=4] {'dp'}, dimensions={0}, use_global_device_ids=true | all-gather | bytes 2304 | tf_op jit(solution)/shard_map/all_gather | solution.py:101
  50.6 18.3 %all-gather.3 = bf16[8,1,128]{2,1,0:T(2,128)(2,1)S(1)} all-gather(bf16[1,1,128]{2,1,0:T(2,128)(2,1)S(1)} %convert_bitcast_fusion.4), channel_id=1, replica_groups=mesh['dp'=8,'blk'=4] {'dp'}, dimensions={0}, use_global_device_ids=true | all-gather | bytes 2304 | tf_op jit(solution)/shard_map/all_gather | solution.py:100
  69.0 18.1 %all-gather.16.cloned.1.call-done = bf16[2048,1024]{1,0:T(8,128)(2,1)} async-done(((bf16[256,1024]{1,0:T(8,128)(2,1)}), bf16[2048,1024]{1,0:T(8,128)(2,1)}) %all-gather.16.cloned.1.call-update) | async-done | bytes 4194320 | tf_op jit(solution)/shard_map/all_gather | solution.py:98
  90.8 96.2 %all-gather.18.cloned.1.call-done = bf16[1024,3072]{1,0:T(8,128)(2,1)} async-done(((bf16[128,3072]{1,0:T(8,128)(2,1)}), bf16[1024,3072]{1,0:T(8,128)(2,1)}) %all-gather.18.cloned.1.call-update) | async-done | bytes 6291472 | tf_op jit(solution)/shard_map/all_gather | solution.py:102
  201.0 26.0 %all-gather.7 = bf16[8,1,512]{2,1,0:T(2,128)(2,1)S(1)} all-gather(bf16[1,1,512]{2,1,0:T(2,128)(2,1)S(1)} %reshape.315), channel_id=1, replica_groups=mesh['dp'=8,'blk'=4] {'dp'}, dimensions={0}, use_global_device_ids=true | all-gather | bytes 9216 | tf_op jit(solution)/shard_map/all_gather | solution.py:107
  227.1 16.3 %all-gather.6 = bf16[8,1,128]{2,1,0:T(2,128)(2,1)S(1)} all-gather(bf16[1,1,128]{2,1,0:T(2,128)(2,1)S(1)} %convert_bitcast_fusion.1), channel_id=1, replica_groups=mesh['dp'=8,'blk'=4] {'dp'}, dimensions={0}, use_global_device_ids=true | all-gather | bytes 2304 | tf_op jit(solution)/shard_map/all_gather | solution.py:105
  243.4 18.1 %all-gather.5 = bf16[8,1,128]{2,1,0:T(2,128)(2,1)S(1)} all-gather(bf16[1,1,128]{2,1,0:T(2,128)(2,1)S(1)} %convert_bitcast_fusion.2), channel_id=1, replica_groups=mesh['dp'=8,'blk'=4] {'dp'}, dimensions={0}, use_global_device_ids=true | all-gather | bytes 2304 | tf_op jit(solution)/shard_map/all_gather | solution.py:104
  281.4 30.2 %while.34 = (s32[]{:T(128)}, f32[16,256]{1,0:T(8,128)S(1)}, f32[256,16,64]{0,2,1:T(8,128)}, s32[1,256]{1,0:T(1,128)S(1)}, s32[1024]{0:T(1024)S(1)}, /*index=5*/b...) while((s32[]{:T(128)}, f32[16,256]{1,0:T(8,128)S(1)}, ...), condition=%wide.region_5.6_spmd.clone, body=%wide.region_3.5_spmd.clone.sunk | while | flops 567283776 | bytes 27769256 | solution.py:51
  316.1 88.1 %all-gather.24.cloned.1.call-done = bf16[1024,4096]{1,0:T(8,128)(2,1)} async-done(((bf16[128,4096]{1,0:T(8,128)(2,1)}), bf16[1024,4096]{1,0:T(8,128)(2,1)}) %all-gather.24.cloned.1.call-update) | async-done | bytes 8388624 | tf_op jit(solution)/shard_map/all_gather | solution.py:106
  404.2 16.1 %multiply_convert_fusion = (bf16[256,4096]{1,0:T(8,128)(2,1)}, f32[256,4096]{1,0:T(8,128)}, f32[256,4096]{1,0:T(8,128)}) fusion(f32[4096]{0:T(1024)S(1)} %bitcast.234, bf16[1024,4096]{1,0:T(8,128)(2,1)} %all-gather.24.cloned.1.call-done, f32[256,1024]{1,0:T(8,128)S(1)} %get-tuple-element.680, f32[1024]{0:T(1024)S(1)} %bitcast.228, f32[1024]{0:T(1024)S(1)} %bitcast.218, ...), kind=kOutput, calls=%fused_computation.52 | convolution fusion | flops 2218000384 | bytes 19949568 | tf_op jit(solution)/shard_map/dot_general | solution.py:159
  420.3 109.0 %all-gather.26.cloned.1.call-done = bf16[4096,1024]{1,0:T(8,128)(2,1)} async-done(((bf16[512,1024]{1,0:T(8,128)(2,1)}), bf16[4096,1024]{1,0:T(8,128)(2,1)}) %all-gather.26.cloned.1.call-update) | async-done | bytes 8388624 | tf_op jit(solution)/shard_map/all_gather | solution.py:108
  529.4 12.4 fusion.78
  556.4 86.2 %while.35 = (s32[]{:T(128)}, f32[256,16,64]{0,2,1:T(8,128)S(1)}, f32[16,256]{1,0:T(8,128)S(1)}, f32[1024,2048]{1,0:T(8,128)}, bf16[1024,2048]{0,1:T(8,128)(2,1)}...) while((s32[]{:T(128)}, f32[256,16,64]{0,2,1:T(8,128)S(1)}, ...), condition=%wide.region_13.14_spmd.clone, body=%wide.region_11.0_spmd.clone.sunk | while | flops 1381765120 | bytes 173013600 | solution.py:51
  655.2 36.2 %reduce-scatter.7.cloned.1.call-done = bf16[256,2048]{1,0:T(8,128)(2,1)} async-done(((bf16[1024,2048]{1,0:T(8,128)(2,1)}), bf16[256,2048]{1,0:T(8,128)(2,1)}) %reduce-scatter.7.cloned.1.call-update) | async-done | bytes 1048592 | tf_op jit(solution)/shard_map/reduce_scatter | solution.py:224
  705.7 7.4 convolution_convert_fusion.1
  727.6 36.2 %reduce-scatter.13.cloned.1.call-done = bf16[128,1024]{1,0:T(8,128)(2,1)} async-done(((bf16[1024,1024]{1,0:T(8,128)(2,1)}), bf16[128,1024]{1,0:T(8,128)(2,1)}) %reduce-scatter.13.cloned.1.call-update) | async-done | bytes 262160 | tf_op jit(solution)/shard_map/reduce_scatter | solution.py:268
  763.8 91.1 %reduce-scatter.9.cloned.1.call-done = bf16[256,1024]{1,0:T(8,128)(2,1)} async-done(((bf16[2048,1024]{1,0:T(8,128)(2,1)}), bf16[256,1024]{1,0:T(8,128)(2,1)}) %reduce-scatter.9.cloned.1.call-update) | async-done | bytes 524304 | tf_op jit(solution)/shard_map/reduce_scatter | solution.py:253
  854.9 152.3 %reduce-scatter.15.cloned.1.call-done = bf16[128,4096]{1,0:T(8,128)(2,1)} async-done(((bf16[1024,4096]{1,0:T(8,128)(2,1)}), bf16[128,4096]{1,0:T(8,128)(2,1)}) %reduce-scatter.15.cloned.1.call-update) | async-done | bytes 1048592 | tf_op jit(solution)/shard_map/reduce_scatter | solution.py:277
  1007.2 152.1 %reduce-scatter.17.cloned.1.call-done = bf16[512,1024]{1,0:T(8,128)(2,1)} async-done(((bf16[4096,1024]{1,0:T(8,128)(2,1)}), bf16[512,1024]{1,0:T(8,128)(2,1)}) %reduce-scatter.17.cloned.1.call-update) | async-done | bytes 1048592 | tf_op jit(solution)/shard_map/reduce_scatter | solution.py:283
  1159.3 120.4 %reduce-scatter.11.cloned.1.call-done = bf16[128,3072]{1,0:T(8,128)(2,1)} async-done(((bf16[1024,3072]{1,0:T(8,128)(2,1)}), bf16[128,3072]{1,0:T(8,128)(2,1)}) %reduce-scatter.11.cloned.1.call-update) | async-done | bytes 786448 | tf_op jit(solution)/shard_map/reduce_scatter | solution.py:265
  1279.8 18.8 %all-gather.8 = bf16[8,1,128]{2,1,0:T(2,128)(2,1)S(1)} all-gather(bf16[1,1,128]{2,1,0:T(2,128)(2,1)S(1)} %convert_bitcast_fusion), channel_id=1, replica_groups=mesh['dp'=8,'blk'=4] {'dp'}, dimensions={0}, use_global_device_ids=true | all-gather | bytes 2304 | tf_op jit(solution)/shard_map/all_gather | solution.py:109
  1300.7 7.3 fusion.54
  1308.0 33.0 %all-reduce.7 = (bf16[1024]{0:T(1024)(128)(2,1)S(1)}, bf16[1024]{0:T(1024)(128)(2,1)S(1)}, bf16[1024]{0:T(1024)(128)(2,1)S(1)}, bf16[1024]{0:T(1024)(128)(2,1)S(...) all-reduce(bf16[1024]{0:T(1024)(128)(2,1)S(1)} %get-tuple-element.6, ...), channel_id=6, replica_groups=mesh['dp'=8,'blk'=4] {'dp'}, use_global_device_ids=true, to_apply=%region_20.21.clone | all-reduce | flops 10240 | bytes 40960
  (321 shorter events, 246.7 us)
Async XLA Ops:
  7.2 79.8 %all-gather.16.cloned.1.call-start = ((), (), s32[]{:S(2)}) async-start(), calls=%async_computation.6 | async-start | bytes 4718592 | tf_op jit(solution)/shard_map/all_gather | solution.py:98
  9.5 177.6 %all-gather.18.cloned.1.call-start = ((), (), s32[]{:S(2)}) async-start(), calls=%async_computation.7 | async-start | bytes 7077888 | tf_op jit(solution)/shard_map/all_gather | solution.py:102
  11.9 262.8 %all-gather.20.cloned.1.call-start = ((), (), s32[]{:S(2)}) async-start(), calls=%async_computation.8 | async-start | bytes 5242880 | tf_op jit(solution)/shard_map/all_gather | solution.py:134
  50.6 136.5 %copy-start.51 = (f32[8,1,128]{2,1,0:T(1,128)}, f32[8,1,128]{2,1,0:T(1,128)S(1)}, u32[]{:S(2)}) copy-start(f32[8,1,128]{2,1,0:T(1,128)S(1)} %convert_element_type.323) | copy-start | bytes 12292
  69.0 118.1 %copy-start.40 = (f32[8,1,128]{2,1,0:T(1,128)}, f32[8,1,128]{2,1,0:T(1,128)S(1)}, u32[]{:S(2)}) copy-start(f32[8,1,128]{2,1,0:T(1,128)S(1)} %convert_element_type.322) | copy-start | bytes 12292
  90.5 101.3 %copy-start.5 = (f32[256,1024]{1,0:T(8,128)}, f32[256,1024]{1,0:T(8,128)S(1)}, u32[]{:S(2)}) copy-start(f32[256,1024]{1,0:T(8,128)S(1)} %get-tuple-element.678) | copy-start | bytes 3145732
  194.1 118.8 %all-gather.22.cloned.1.call-start = ((), (), s32[]{:S(2)}) async-start(), calls=%async_computation.9 | async-start | bytes 2359296 | tf_op jit(solution)/shard_map/all_gather | solution.py:103
  195.0 209.2 %all-gather.24.cloned.1.call-start = ((), (), s32[]{:S(2)}) async-start(), calls=%async_computation.10 | async-start | bytes 9437184 | tf_op jit(solution)/shard_map/all_gather | solution.py:106
  197.9 331.5 %all-gather.26.cloned.1.call-start = ((), (), s32[]{:S(2)}) async-start(), calls=%async_computation.11 | async-start | bytes 9437184 | tf_op jit(solution)/shard_map/all_gather | solution.py:108
  200.9 490.6 %reduce-scatter.7.cloned.1.call-start = ((), (), s32[]{:S(2)}) async-start(), calls=%async_computation.12 | async-start | bytes 5242880 | tf_op jit(solution)/shard_map/reduce_scatter | solution.py:224
  243.3 160.9 %copy-start.34 = (f32[8,1,128]{2,1,0:T(1,128)}, f32[8,1,128]{2,1,0:T(1,128)S(1)}, u32[]{:S(2)}) copy-start(f32[8,1,128]{2,1,0:T(1,128)S(1)} %convert_element_type.325) | copy-start | bytes 12292
  261.5 283.5 %copy-start.30 = (f32[8,1,128]{2,1,0:T(1,128)}, f32[8,1,128]{2,1,0:T(1,128)S(1)}, u32[]{:S(2)}) copy-start(f32[8,1,128]{2,1,0:T(1,128)S(1)} %convert_element_type.324) | copy-start | bytes 12292
  315.8 229.2 %copy-start.3 = (f32[256,1024]{1,0:T(8,128)}, f32[256,1024]{1,0:T(8,128)S(1)}, u32[]{:S(2)}) copy-start(f32[256,1024]{1,0:T(8,128)S(1)} %get-tuple-element.680) | copy-start | bytes 3145732
  315.8 229.2 %copy-start.36 = (f32[256]{0:T(256)}, f32[256]{0:T(256)S(1)}, u32[]{:S(2)}) copy-start(f32[256]{0:T(256)S(1)} %broadcast_multiply_fusion) | copy-start | bytes 3076
  316.1 228.9 %copy-start.38 = (f32[256]{0:T(256)}, f32[256]{0:T(256)S(1)}, u32[]{:S(2)}) copy-start(f32[256]{0:T(256)S(1)} %fusion.64) | copy-start | bytes 3076
  404.2 125.1 %copy-start.11 = (bf16[1,256,1024]{2,1,0:T(8,128)(2,1)S(1)}, bf16[1,256,1024]{2,1,0:T(8,128)(2,1)}, u32[]{:S(2)}) copy-start(bf16[1,256,1024]{2,1,0:T(8,128)(2,1)} %param.23) | copy-start | bytes 1572868
  648.6 115.2 %reduce-scatter.13.cloned.1.call-start = ((), (), s32[]{:S(2)}) async-start(), calls=%async_computation.15 | async-start | bytes 2359296 | tf_op jit(solution)/shard_map/reduce_scatter | solution.py:268
  651.8 203.1 %reduce-scatter.9.cloned.1.call-start = ((), (), s32[]{:S(2)}) async-start(), calls=%async_computation.13 | async-start | bytes 4718592 | tf_op jit(solution)/shard_map/reduce_scatter | solution.py:253
  704.5 302.7 %reduce-scatter.15.cloned.1.call-start = ((), (), s32[]{:S(2)}) async-start(), calls=%async_computation.16 | async-start | bytes 9437184 | tf_op jit(solution)/shard_map/reduce_scatter | solution.py:277
  713.1 446.2 %reduce-scatter.17.cloned.1.call-start = ((), (), s32[]{:S(2)}) async-start(), calls=%async_computation.17 | async-start | bytes 9437184 | tf_op jit(solution)/shard_map/reduce_scatter | solution.py:283
  720.4 559.3 %reduce-scatter.11.cloned.1.call-start = ((), (), s32[]{:S(2)}) async-start(), calls=%async_computation.14 | async-start | bytes 7077888 | tf_op jit(solution)/shard_map/reduce_scatter | solution.py:265
  727.5 552.3 %copy-start.66 = (f32[128]{0:T(128)S(1)}, f32[128]{0:T(128)}, u32[]{:S(2)}) copy-start(f32[128]{0:T(128)} %param.37) | copy-start | bytes 1540
  727.5 571.2 %copy-start.67 = (u32[32]{0:T(128)S(1)}, u32[32]{0:T(128)}, u32[]{:S(2)}) copy-start(u32[32]{0:T(128)} %constant.184) | copy-start | bytes 388
  727.5 631.9 %all-reduce.12.cloned.1.call-start = ((), (), s32[]{:S(2)}) async-start(), calls=%async_computation.18 | async-start | bytes 7340032 | tf_op jit(solution)/shard_map/psum | solution.py:291
  (62 other events, 1347.7 us)
Sparse Core Ops, SparseCore 0:
  10.8 76.1 all-gather.15
  89.8 97.2 all-gather.17
  194.2 32.6 all-gather.19
  229.5 49.2 all-gather.21
  280.8 123.4 all-gather.23
  406.2 123.1 all-gather.25
  648.7 42.6 reduce-scatter.6
  696.0 67.7 reduce-scatter.12
  767.8 87.0 reduce-scatter.8
  858.4 148.7 reduce-scatter.14
  1011.3 148.0 reduce-scatter.16
  1162.8 116.9 reduce-scatter.10
  1282.5 76.9 all-reduce.11
where the time goes:
time: 1380 us
  waiting for transfers between devices  904 us (66%)
  blocking collectives  185 us (13%)
  matrix products  144 us (10%)
  local copies, waits for them, and re-layouts  76.5 us (6%)
  other arithmetic  48.2 us (3%)
  between operations  16.3 us (1%)
    reduce_scatter x1, waiting for transfers between devices, per_device(): lax.psum_scatter(grad_w_up.astype(jnp.bfloat16), 'dp', scatter_dimension=...  152 us
    reduce_scatter x1, waiting for transfers between devices, per_device(): lax.psum_scatter(grad_w_down.astype(jnp.bfloat16), 'dp', scatter_dimensio...  152 us
    reduce_scatter x1, waiting for transfers between devices, per_device(): lax.psum_scatter(grad_w_qkv.astype(jnp.bfloat16), 'dp', scatter_dimension...  120 us
    all_gather x1, waiting for transfers between devices, per_device(): lax.all_gather(w_down.astype(low_type), 'dp', axis=0, tiled=True)  109 us
    all_gather x1, waiting for transfers between devices, per_device(): lax.all_gather(w_qkv.astype(low_type), 'dp', axis=0, tiled=True)  96.2 us
    reduce_scatter x1, waiting for transfers between devices, per_device(): lax.psum_scatter(grad_w_skip.astype(jnp.bfloat16), 'dp', scatter_dimensio...  91.1 us
    all_gather x1, waiting for transfers between devices, per_device(): lax.all_gather(w_up.astype(low_type), 'dp', axis=0, tiled=True)  88.1 us
    reduce_scatter x1, waiting for transfers between devices, per_device(): lax.psum_scatter(folded[2].astype(jnp.bfloat16), 'blk', scatter_dimension...  36.2 us
  transfers between devices with their start and end apart: 13, of which 11 were waited for; matrix products, arithmetic and copies ran while one was open for 9% of the time, Pallas kernels for 0%

commit v1 on v0

v1 whole, which is shorter than its diff:
```python
import functools
import math

import jax
import jax.numpy as jnp
from jax import lax
from jax.experimental import pallas as pl
from jax.experimental.pallas import tpu as pltpu
from jax.sharding import PartitionSpec as P

H = 16
EPSILON = 1e-05
LOW = jnp.bfloat16
F32 = jnp.float32
MESH = pl.DeviceIdType.MESH
FAR = 1e30


def dot(left, right):
    return jnp.dot(left, right, preferred_element_type=F32)


def dot_nt(left, right):
    return lax.dot_general(left, right, (((1,), (1,)), ((), ())), preferred_element_type=F32)


def loop(count, body):
    def visit(index, carry):
        body(index)
        return carry

    lax.fori_loop(0, count, visit, 0)


def aligned(start, size):
    return pl.ds(pl.multiple_of(start, size), size)


class Sizes:
    def __init__(self, mesh_shape, frames, w_up):
        self.n_dp, self.n_blk = mesh_shape["dp"], mesh_shape["blk"]
        self.nz = self.n_dp // 2
        self.groups = self.n_blk // 2
        self.rows = frames.shape[1]
        self.width = frames.shape[2]
        self.hidden = w_up.shape[1]
        self.shard = self.width // self.n_dp
        self.cols = self.width // self.groups
        self.heads = H // self.groups
        self.units = self.hidden // self.groups
        self.part = self.units // self.n_dp
        self.direct = self.part % 128 == 0
        self.up_rows = -(-self.units // self.width)


class Wires:
    def __init__(self, send_sems, recv_sems):
        self.send_sems, self.recv_sems, self.used = send_sems, recv_sems, 0

    def take(self, count=1):
        first = self.used
        self.used += count
        assert self.used <= self.send_sems.shape[0]
        return first

    def copy(self, ends, index=None):
        return Copy(self, ends, self.take() if index is None else index)


class Copy:
    def __init__(self, wires, ends, index):
        self.wires, self.ends, self.index = wires, ends, index

    def made(self):
        source, target, peer = self.ends()
        return pltpu.make_async_remote_copy(
            src_ref=source,
            dst_ref=target,
            send_sem=self.wires.send_sems.at[self.index],
            recv_sem=self.wires.recv_sems.at[self.index],
            device_id=peer,
            device_id_type=MESH,
        )

    def start(self):
        self.made().start()

    def wait_send(self):
        self.made().wait_send()

    def wait_recv(self):
        self.made().wait_recv()

    def wait(self):
        self.made().wait()


class Place:
    def __init__(self, sizes):
        self.dp, self.blk = lax.axis_index("dp"), lax.axis_index("blk")
        self.z, self.y = lax.div(self.dp, 2), lax.rem(self.dp, 2)
        self.g, self.c = lax.div(self.blk, 2), lax.rem(self.blk, 2)
        self.sizes = sizes

    def z_at(self, step):
        nz = self.sizes.nz
        return lax.rem(self.z + (step + nz), nz)

    def g_at(self, step):
        groups = self.sizes.groups
        return lax.rem(self.g + (step + groups), groups)

    def z_peer(self, step):
        return (self.z_at(step) * 2 + self.y, self.blk)

    def y_peer(self):
        return (self.z * 2 + 1 - self.y, self.blk)

    def x_peer(self, step):
        return (self.dp, self.g_at(step) * 2 + self.c)

    def c_peer(self):
        return (self.dp, self.g * 2 + 1 - self.c)


class Gather:
    def __init__(self, place, wires, ref, half, spread, whole_core=False):
        self.place, self.wires, self.ref = place, wires, ref
        self.half, self.spread, self.whole_core = half, spread, whole_core
        sizes = place.sizes
        self.nz = sizes.nz
        self.groups = sizes.groups if spread else 1
        self.z_copies, self.y_copies, self.x_copies, self.c_copies = {}, {}, {}, {}

    def piece(self, k, step=0):
        place = self.place
        z_index = place.z_at(-(k % self.nz))
        y_index = place.y if k < self.nz else 1 - place.y
        if self.whole_core:
            return self.ref.at[z_index, y_index]
        rows = aligned(place.c * self.half, self.half)
        if not self.spread:
            return self.ref.at[z_index, y_index, rows]
        cols = place.sizes.cols
        return self.ref.at[z_index, y_index, rows, aligned(place.g_at(-step) * cols, cols)]

    def send(self, copies, key, piece, peer):
        copies[key] = self.wires.copy(lambda: (piece(), piece(), peer()))
        copies[key].start()

    def start(self):
        for step in range(1, self.nz):
            self.send(
                self.z_copies, step, lambda: self.piece(0), lambda step=step: self.place.z_peer(step)
            )
        self.forward(0)

    def forward(self, k):
        def piece():
            return self.piece(k)

        if k < self.nz:
            self.send(self.y_copies, k, piece, self.place.y_peer)
        for step in range(1, self.groups):
            self.send(self.x_copies, (step, k), piece, lambda step=step: self.place.x_peer(step))
        if not self.whole_core:
            self.send(self.c_copies, (0, k), piece, self.place.c_peer)

    def z_step(self, step):
        self.z_copies[step].wait_recv()
        self.forward(step)

    def y_step(self, k):
        self.y_copies[k].wait_recv()
        self.forward(self.nz + k)

    def x_step(self, k):
        for step in range(1, self.groups):
            self.x_copies[step, k].wait_recv()
            self.send(
                self.c_copies, (step, k), lambda step=step: self.piece(k, step), self.place.c_peer
            )

    def z_steps(self):
        for step in range(1, self.nz):
            self.z_step(step)

    def y_steps(self):
        for k in range(self.nz):
            self.y_step(k)

    def x_steps(self):
        for k in range(2 * self.nz):
            self.x_step(k)

    def finish(self):
        for copy in self.c_copies.values():
            copy.wait_recv()

    def drain(self):
        for copies in (self.z_copies, self.y_copies, self.x_copies, self.c_copies):
            for copy in copies.values():
                copy.wait_send()
            copies.clear()


class Exchange:
    def __init__(self, place, wires):
        self.place, self.groups = place, place.sizes.groups
        self.wires = wires
        self.first = wires.take(self.groups)

    def copy(self, step, source, target):
        return self.wires.copy(
            lambda: (source(), target(), self.place.x_peer(step)), self.first + step
        )


class Reduce:
    def __init__(self, place, wires, grad, half, spread, core_in, x_in, y_in, z_in, out):
        self.place, self.wires, self.grad, self.half, self.spread = place, wires, grad, half, spread
        self.core_in, self.x_in, self.y_in, self.z_in, self.out = core_in, x_in, y_in, z_in, out
        self.nz, self.groups = place.sizes.nz, place.sizes.groups
        self.core_copies, self.x_copies, self.z_copies = {}, {}, {}
        self.fin_copies, self.fwd_copies = {}, {}

    def side(self, part):
        return 1 - self.place.y if part == 0 else self.place.y

    def core_send(self, part):
        def ends():
            side = self.side(part)
            rows = aligned((1 - self.place.c) * self.half, self.half)
            return self.grad.at[:, side, rows], self.core_in.at[:, side], self.place.c_peer()

        copy = self.wires.copy(ends)
        copy.start()
        self.core_copies[part] = copy

    def core_add(self, part):
        side = self.side(part)
        rows = aligned(self.place.c * self.half, self.half)
        self.core_copies[part].wait_recv()

        def body(z):
            self.core_in[z, side] = self.core_in[z, side] + self.grad[z, side, rows]

        loop(self.nz, body)
        if self.spread:
            cols = self.place.sizes.cols
            for step in range(1, self.groups):
                def ends(step=step):
                    side = self.side(part)
                    theirs = aligned(self.place.g_at(step) * cols, cols)
                    return (
                        self.core_in.at[:, side, :, theirs],
                        self.x_in.at[step - 1, :, side],
                        self.place.x_peer(step),
                    )

                copy = self.wires.copy(ends)
                copy.start()
                self.x_copies[part, step] = copy
        elif part == 0:
            self.y_send()

    def x_add(self, part):
        side = self.side(part)
        cols = self.place.sizes.cols
        mine = aligned(self.place.g * cols, cols)
        for step in range(1, self.groups):
            self.x_copies[part, step].wait_recv()

        def body(z):
            total = self.core_in[z, side, :, mine].astype(F32)
            for step in range(1, self.groups):
                total = total + self.x_in[step - 1, z, side].astype(F32)
            self.x_in[0, z, side] = total.astype(LOW)

        loop(self.nz, body)
        if part == 0:
            self.y_send()

    def held(self):
        return self.x_in.at[0] if self.spread else self.core_in

    def y_send(self):
        self.y_copy = self.wires.copy(
            lambda: (self.held().at[:, self.side(0)], self.y_in, self.place.y_peer())
        )
        self.y_copy.start()

    def y_add(self):
        self.y_copy.wait()
        side = self.side(1)
        held = self.held()

        def body(z):
            self.y_in[z] = self.y_in[z] + held[z, side]

        loop(self.nz, body)
        for step in range(1, self.nz):
            copy = self.wires.copy(
                lambda step=step: (
                    self.y_in.at[self.place.z_at(step)],
                    self.z_in.at[step - 1],
                    self.place.z_peer(step),
                )
            )
            copy.start()
            self.z_copies[step] = copy

    def z_add(self):
        place = self.place
        for step in range(1, self.nz):
            self.z_copies[step].wait_recv()

        def body(i):
            at = aligned(i * 16, 16)
            total = self.y_in[place.z, at].astype(F32)
            for step in range(1, self.nz):
                total = total + self.z_in[step - 1, at].astype(F32)
            self.out[place.g, place.c, at] = total.astype(LOW)

        loop(self.half // 16, body)
        for step in range(1, self.groups):
            self.fin_copies[step] = self.wires.copy(
                lambda step=step: self.spot(0) * 2 + (place.x_peer(step),)
            )
            self.fin_copies[step].start()
        self.forward(0)

    def spread_on(self):
        for step in range(1, self.groups):
            self.fin_copies[step].wait_recv()
            self.forward(step)

    def spot(self, step):
        return (self.out.at[self.place.g_at(-step), self.place.c],)

    def forward(self, step):
        self.fwd_copies[step] = self.wires.copy(
            lambda: self.spot(step) * 2 + (self.place.c_peer(),)
        )
        self.fwd_copies[step].start()

    def drain(self):
        for copies in (self.core_copies, self.x_copies, self.z_copies, self.fin_copies):
            for copy in copies.values():
                copy.wait_send()

    def finish(self):
        for copy in self.fwd_copies.values():
            copy.wait()


def norm_terms(held):
    centred = held - jnp.mean(held, axis=-1, keepdims=True)
    scale = lax.rsqrt(jnp.mean(centred * centred, axis=-1, keepdims=True) + EPSILON)
    return centred * scale, scale


def kernel(sizes, *refs):
    names = (
        "frames", "skip", "cot", "seg", "b_skip", "gain_a", "bias_a", "gain_f", "bias_f",
        "b_down", "b_up", "w_skip", "w_qkv", "w_out", "w_up", "w_down", "o_out", "o_frames",
        "o_skip", "p_skip", "p_qkv", "p_out", "p_up", "p_down", "o_small", "o_up", "io",
        "cot_all", "ws", "wqkv", "wout", "wup", "wdown", "small", "vecs", "bup", "segs", "segc",
        "merged", "middle", "gmid", "normed", "second", "kv", "qt", "kt", "shift", "attt", "tot",
        "att_own", "att_send", "active", "ghid", "p_send", "p_recv", "gb", "ga_in", "gm", "dkv",
        "far", "vt", "c_skip", "c_out", "c_up", "c_down", "x_skip", "x_out", "y_skip", "y_qkv",
        "y_out", "y_up", "y_down", "z_skip", "z_qkv", "z_out", "z_up", "z_down", "sums",
        "sum_in", "turned", "outp", "send_sems", "recv_sems", "local_sems",
    )
    assert len(names) == len(refs), (len(names), len(refs))
    v = dict(zip(names, refs))
    place = Place(sizes)
    wires = Wires(v["send_sems"], v["recv_sems"])
    local = v["local_sems"]
    nz, groups, n_dp, n_blk = sizes.nz, sizes.groups, sizes.n_dp, sizes.n_blk
    rows, width, cols, units = sizes.rows, sizes.width, sizes.cols, sizes.units
    heads = sizes.heads
    z, y, g, c = place.z, place.y, place.g, place.c

    barrier = pltpu.get_barrier_semaphore()
    partners = [place.z_peer(step) for step in range(1, nz)] + [place.y_peer()]
    partners += [place.x_peer(step) for step in range(1, groups)] + [place.c_peer()]
    for partner in partners:
        pl.semaphore_signal(barrier, inc=1, device_id=partner, device_id_type=MESH)

    fr_v, sk_v = v["io"].at[0], v["io"].at[1]

    def input_loads():
        return [
            pltpu.make_async_copy(v["frames"].at[0], fr_v, local.at[0]),
            pltpu.make_async_copy(v["skip"].at[0], sk_v, local.at[1]),
        ]

    loads = input_loads() + [
        pltpu.make_async_copy(v["cot"].at[0], v["cot_all"].at[g], local.at[2]),
    ]

    h_skip, h_qkv = v["ws"].shape[2] // 2, v["wqkv"].shape[2] // 2
    h_out, h_up, h_down = v["wout"].shape[2] // 2, v["wup"].shape[2] // 2, v["wdown"].shape[2] // 2

    stages = {}

    def fetch(name, start, size, buffer, top, index):
        parts = v[name].shape[1] // width
        copies = [
            pltpu.make_async_copy(
                v[name].at[aligned(start, size), part * width : (part + 1) * width],
                buffer.at[top + part * size : top + (part + 1) * size],
                local.at[index + part],
            )
            for part in range(parts)
        ]
        for copy in copies:
            copy.start()
        stages[name] = copies

    merged, middle, gmid, outp = v["merged"], v["middle"], v["gmid"], v["outp"]
    fetch("w_skip", c * h_skip, h_skip, merged, 0, 3)
    fetch("w_qkv", c * h_qkv, h_qkv, gmid, 0, 4)
    fetch("w_out", c * h_out, h_out, merged, h_skip, 7)
    fetch("w_up", c * h_up, h_up, outp, 0, 8)
    fetch("w_down", (g * 2 + c) * h_down, h_down, middle, 0, 12)
    for load in loads:
        load.start()
    ws, wqkv, wout, wup, wdown = v["ws"], v["wqkv"], v["wout"], v["wup"], v["wdown"]
    own_cols = aligned(g * cols, cols)

    def arrived(name):
        for copy in stages[name]:
            copy.wait()

    arrived("w_skip")
    ws[z, y, aligned(c * h_skip, h_skip), own_cols] = merged[0:h_skip, own_cols].astype(LOW)
    arrived("w_qkv")
    for third in range(3):
        wqkv[z, y, aligned(c * h_qkv, h_qkv), third * cols : (third + 1) * cols] = gmid[
            third * h_qkv : (third + 1) * h_qkv, own_cols
        ].astype(LOW)
    arrived("w_out")
    wout[z, y, aligned(c * h_out, h_out), own_cols] = merged[
        h_skip : h_skip + h_out, own_cols
    ].astype(LOW)
    arrived("w_up")
    up_rows = aligned(c * h_up, h_up)
    if sizes.direct:
        part = sizes.part
        per_row = width // (part * groups)
        for s in range(n_dp):
            at = (s // per_row) * h_up
            wup[z, y, up_rows, s * part : (s + 1) * part] = outp[
                at : at + h_up, aligned(g * part + s % per_row * part * groups, part)
            ].astype(LOW)
    else:
        at = pl.multiple_of(lax.div(g * units, width) * h_up, h_up)
        wup[z, y, up_rows] = outp[
            pl.ds(at, h_up), aligned(lax.rem(g * units, width), units)
        ].astype(LOW)
    arrived("w_down")
    wdown[z, y, aligned(c * h_down, h_down)] = middle[0:h_down].astype(LOW)

    small = v["small"]
    for row, name in enumerate(("b_skip", "gain_a", "bias_a", "gain_f", "bias_f", "b_down")):
        small[z, y, row : row + 1, 0 : sizes.shard] = v[name][...].astype(LOW).astype(F32)
    if sizes.direct:
        own_up = v["b_up"][:, aligned(g * sizes.part, sizes.part)]
    else:
        own_up = v["b_up"][...]
    small[z, y, 6:7, 0 : sizes.part] = own_up.astype(LOW).astype(F32)
    segs = v["segs"]
    segs[c, g] = jnp.broadcast_to(v["seg"][...].astype(F32), (8, rows))

    pl.semaphore_wait(barrier, len(partners))

    g_small = Gather(place, wires, small, 0, False, whole_core=True)
    g_skip = Gather(place, wires, v["ws"], h_skip, True)
    g_qkv = Gather(place, wires, v["wqkv"], h_qkv, False)
    g_out = Gather(place, wires, v["wout"], h_out, True)
    g_up = Gather(place, wires, v["wup"], h_up, False)
    g_down = Gather(place, wires, v["wdown"], h_down, False)
    seg_swap = Exchange(place, wires)
    seg_copies = []
    for step in range(1, groups):
        seg_copies.append(seg_swap.copy(step, lambda: segs.at[c, g], lambda: segs.at[c, g]))
        seg_copies[-1].start()
    g_small.start()
    g_skip.start()
    g_qkv.start()
    g_out.start()
    g_up.start()
    g_down.start()
    for copy in seg_copies:
        copy.wait_recv()
    seg_core = wires.copy(lambda: (segs.at[c], segs.at[c], place.c_peer()))
    seg_core.start()
    for step in range(1, nz):
        g_skip.z_step(step)
        g_small.z_step(step)
    for k in range(nz):
        g_skip.x_step(k)
        g_skip.y_step(k)
        g_small.y_step(k)
    for k in range(nz, 2 * nz):
        g_skip.x_step(k)

    for load in loads:
        load.wait()
    vecs = v["vecs"]
    for row in range(6):
        vecs[row : row + 1] = jnp.concatenate(
            [small[s // 2, s % 2, row : row + 1, 0 : sizes.shard] for s in range(n_dp)], axis=1
        )
    v["bup"][...] = jnp.concatenate(
        [small[s // 2, s % 2, 6:7, 0 : sizes.part] for s in range(n_dp)], axis=1
    )
    seg_core.wait_recv()
    segc = v["segc"]
    for core in range(2):

        def turn(block, core=core):
            turned_ids = jnp.broadcast_to(segs[core, block, 0:1], (128, rows)).T
            segc[core, block] = turned_ids.astype(LOW)

        loop(groups, turn)
    g_qkv.z_steps()
    g_skip.finish()

    tile = min(256, width)

    def merge_tile(n):
        lane = aligned(n * tile, tile)
        merged[:, lane] = (
            dot(fr_v[...], ws[0 : nz // 2, :, :, lane].reshape(width, tile))
            + dot(sk_v[...], ws[nz // 2 : nz, :, :, lane].reshape(width, tile))
            + vecs[0:1, lane]
        )

    loop(width // tile, merge_tile)
    chunk = 64

    def norm_into(held, gain_row, target):
        def body(i):
            at = aligned(i * chunk, chunk)
            unit, _ = norm_terms(held[at])
            target[at] = (
                unit * vecs[gain_row : gain_row + 1] + vecs[gain_row + 1 : gain_row + 2]
            ).astype(LOW)

        loop(rows // chunk, body)

    def norm_back(held, gain_row, incoming, finish):
        def body(i, carry):
            at = aligned(i * chunk, chunk)
            unit, scale = norm_terms(held[at])
            t = incoming(at)
            scaled = t * vecs[gain_row : gain_row + 1]
            grad = scale * (
                scaled
                - jnp.mean(scaled, axis=-1, keepdims=True)
                - unit * jnp.mean(scaled * unit, axis=-1, keepdims=True)
            )
            finish(at, grad)
            return (
                carry[0] + jnp.sum(t * unit, axis=0, keepdims=True),
                carry[1] + jnp.sum(t, axis=0, keepdims=True),
            )

        zero = jnp.zeros((1, width), F32)
        return lax.fori_loop(0, rows // chunk, body, (zero, zero))

    normed, second, cot_all = v["normed"], v["second"], v["cot_all"]

    def share(buffer):
        swap = Exchange(place, wires)
        copies = [
            swap.copy(step, lambda: buffer.at[g], lambda: buffer.at[g])
            for step in range(1, groups)
        ]
        for copy in copies:
            copy.start()
        return copies

    norm_into(merged, 1, normed.at[g])
    normed_copies = share(normed)
    cot_copies = share(cot_all)

    kv, qt, kt = v["kv"], v["qt"], v["kt"]
    shift = v["shift"]
    pick = (
        lax.broadcasted_iota(jnp.int32, (max(8, heads), cols), 1)
        // (width // H)
        == lax.broadcasted_iota(jnp.int32, (max(8, heads), cols), 0)
    ).astype(F32)
    kv_first = wires.take(groups)

    def kv_copy(block, step):
        return wires.copy(
            lambda: (kv.at[c, block], kv.at[c, block], place.c_peer()), kv_first + step
        )

    def mix(block, step):
        rows_in = normed[block]
        for third in range(3):
            value = dot(
                rows_in,
                wqkv[:, :, :, third * cols : (third + 1) * cols].reshape(width, cols),
            ).astype(LOW)
            if third == 0:
                query = value
            else:
                kv[c, block, :, (third - 1) * cols : third * cols] = value
        kv_copy(block, step).start()
        found = 0.0
        for at in range(0, cols, 128):
            part = query[:, at : at + 128].astype(F32)
            product = part * kv[c, block, :, at : at + 128].astype(F32)
            found = found + lax.dot_general(
                pick[:, at : at + 128],
                product,
                (((1,), (1,)), ((), ())),
                precision=lax.Precision.HIGHEST,
                preferred_element_type=F32,
            )
            qt[block, at : at + 128] = (part * 0.125).T.astype(LOW)
        for head in range(heads):
            shift[block, head] = found[head : head + 1] * 0.125

    g_qkv.y_steps()
    g_qkv.finish()
    mix(g, 0)
    g_out.z_steps()
    for copy in normed_copies:
        copy.wait_recv()

    def mix_other(step):
        mix(place.g_at(-step), step)

    lax.fori_loop(1, groups, lambda step, carry: (mix_other(step), carry)[1], 0)
    g_up.z_step(1)
    g_out.y_steps()

    kv_waits = [kv_copy(place.g_at(-step), step) for step in range(groups)]
    for copy in kv_waits:
        copy.wait_recv()

    def slope_row(head):
        index = jnp.full((1, rows), g * heads + head, jnp.int32).astype(F32)
        return jnp.exp2((index + 1.0) * (-8.0 / H))

    def fill_far(block):
        place_k = lax.broadcasted_iota(jnp.int32, (rows, rows), 0) * n_blk
        place_q = lax.broadcasted_iota(jnp.int32, (rows, rows), 1) * n_blk + (block * 2 + c)
        apart = place_k - place_q
        seg_q = segs[c, block, 0:1]
        for core in range(2):

            def body(b, core=core):
                seg_k = segc[core, b].astype(F32)
                same = jnp.concatenate([seg_k] * (rows // 128), axis=1) == seg_q
                distance = jnp.abs(apart + (b * 2 + core)).astype(F32)
                far[core, b] = jnp.where(same, distance, FAR)

            loop(groups, body)

    def padded(half_value, half):
        zero = jnp.zeros_like(half_value)
        return jnp.concatenate([half_value, zero] if half == 0 else [zero, half_value], axis=0)

    head_width = width // H
    pair_width = 2 * head_width
    attt, tot = v["attt"], v["tot"]

    def score_terms(pair, core, b, queries_pad, slope, moved):
        keys = kv[core, b, :, aligned(pair * pair_width, pair_width)]
        return jnp.exp(dot(keys, queries_pad) - slope * far[core, b] - moved)

    def over_keys(body, first):
        def visit(index, carry):
            return body(lax.div(index, groups), lax.rem(index, groups), carry)

        return lax.fori_loop(0, 2 * groups, visit, first)

    def head_at(pair, half):
        return aligned(pair * pair_width + half * head_width, head_width)

    far, vt = v["far"], v["vt"]

    def attend(block):
        def body(pair):
            lanes = aligned(pair * pair_width, pair_width)
            fixed = []
            for half in range(2):
                head = pair * 2 + half
                fixed.append(
                    (padded(qt[block, head_at(pair, half)], half), slope_row(head), shift[block, head])
                )

            def keys_in(core, b, carry):
                done = []
                for half in range(2):
                    total, summed = carry[half]
                    terms = score_terms(pair, core, b, *fixed[half])
                    total = total + jnp.sum(terms, axis=0, keepdims=True)
                    done.append((total, summed + dot(vt[core, b, lanes], terms.astype(LOW))))
                return tuple(done)

            start = (jnp.zeros((1, rows), F32), jnp.zeros((pair_width, rows), F32))
            found = over_keys(keys_in, (start, start))
            for half in range(2):
                total, summed = found[half]
                tot[block, pair * 2 + half] = total
                own = summed[half * head_width : (half + 1) * head_width]
                attt[block, head_at(pair, half)] = own / total

        loop(heads // 2, body)

    att_own, att_send = v["att_own"], v["att_send"]
    att_first = wires.take(groups)

    def att_copy(step, block):
        return wires.copy(
            lambda: (att_send.at[block], att_own.at[:, own_cols], place.x_peer(step)),
            att_first + step,
        )

    def attention():
        for core in range(2):

            def turn(b, core=core):
                vt[core, b] = kv[core, b, :, cols : 2 * cols].T
                kt[core, b] = kv[core, b, :, 0:cols].T

            loop(groups, turn)

        def other(step, carry):
            block = place.g_at(step)
            fill_far(block)
            attend(block)
            att_send[block] = attt[block].T.astype(LOW)
            att_copy(step, block).start()
            return carry

        lax.fori_loop(1, groups, other, 0)
        g_up.z_step(2)
        g_out.x_steps()
        fill_far(g)
        attend(g)
        att_own[:, own_cols] = attt[g].T.astype(LOW)

    attention()
    for step in range(3, nz):
        g_up.z_step(step)
    g_out.finish()
    for step in range(1, groups):
        att_copy(step, place.g_at(step)).wait_recv()

    def middle_tile(n):
        lane = aligned(n * tile, tile)
        middle[:, lane] = merged[:, lane] + dot(
            att_own[...], wout[:, :, :, lane].reshape(width, tile)
        )

    loop(width // tile, middle_tile)
    norm_into(middle, 3, second.at[g])
    second_copies = share(second)
    g_up.y_steps()
    g_down.z_steps()
    g_up.finish()
    g_down.y_steps()
    g_down.finish()

    active, ghid = v["active"], v["ghid"]
    unit_tile = 256
    shard_rows = wdown.shape[2]

    def down_rows(u):
        if shard_rows >= unit_tile:
            per = shard_rows // unit_tile
            s = lax.div(u, per)
            return wdown[lax.div(s, 2), lax.rem(s, 2), aligned(lax.rem(u, per) * unit_tile, unit_tile)]
        per = unit_tile // (2 * shard_rows)
        return wdown[pl.ds(u * per, per)].reshape(unit_tile, width)

    for copy in cot_copies:
        copy.wait_recv()

    def feed(block):
        def body(u):
            lane = aligned(u * unit_tile, unit_tile)
            pre = dot(second[block], wup[:, :, :, lane].reshape(width, unit_tile)) + v["bup"][:, lane]
            back = dot_nt(cot_all[block], down_rows(u))
            normal = 0.5 * (1.0 + lax.erf(pre * (0.5**0.5)))
            active[block, :, lane] = (pre * normal).astype(LOW)
            slope = normal + pre * (jnp.exp(-0.5 * pre * pre) * (1.0 / math.sqrt(2.0 * math.pi)))
            ghid[block, :, lane] = (back * slope).astype(LOW)

        loop(units // unit_tile, body)

    def row_chunks(ref, most=512):
        per = min(nz, max(1, most // (2 * ref.shape[2])))
        return nz // per, per, per * 2 * ref.shape[2]

    def back_product(left, weight, store):
        count, per, size = row_chunks(weight)

        def body(j):
            value = dot_nt(left[...], weight[pl.ds(j * per, per)].reshape(size, weight.shape[3]))
            store(aligned(j * size, size), value)

        loop(count, body)

    lend = groups > 2
    p_send, p_recv = v["io"] if lend else v["p_send"], v["p_recv"]

    def store_into(ref, kind):
        def store(lane, value):
            ref[:, lane] = value.astype(kind)

        return store

    feed(g)
    for copy in second_copies:
        copy.wait_recv()
    second_first = wires.take(groups)

    def part_copy(step, first):
        return wires.copy(
            lambda: (p_send.at[part_slot(step)], p_recv.at[step - 1], place.x_peer(step)),
            first + step,
        )

    def part_slot(step):
        return 0 if groups == 2 else lax.rem(step, 2)

    def send_part(step, left, weight, first):
        if groups > 3:

            @pl.when(step > 2)
            def _():
                part_copy(step - 2, first).wait_send()

        back_product(left, weight, store_into(p_send.at[part_slot(step)], LOW))
        part_copy(step, first).start()

    def parts_sent(first):
        for step in range(max(1, groups - 2), groups):
            part_copy(step, first).wait_send()

    def other_feed(step, carry):
        block = place.g_at(step)
        feed(block)
        send_part(step, ghid.at[block], wup, second_first)
        return carry

    lax.fori_loop(1, groups, other_feed, 0)
    back_product(ghid.at[g], wup, store_into(gmid, F32))

    def down_tile(left, target, n):
        lane = aligned(n * tile, tile)
        target(lane, dot(left[...], wdown[:, :, :, lane].reshape(units, tile)))

    turned = v["turned"]

    def weight_grad(left, right, grad, left_at):
        count, per, size = row_chunks(grad, turned.shape[0])
        wide = grad.shape[3]
        step_cols = min(256, wide)
        depth = left.shape[0] if len(left.shape) == 2 else left.shape[0] * left.shape[1]

        def body(j):
            lane = aligned(j * size, size)
            part = left[:, lane] if len(left.shape) == 2 else left[:, :, lane]
            turned[0:size, 0:depth] = part.reshape(depth, size).T

            def inner(n):
                out = aligned(n * step_cols, step_cols)
                part = right[:, out] if len(right.shape) == 2 else right[:, :, out]
                value = dot(turned[0:size, 0:depth], part.reshape(depth, step_cols))
                grad[pl.ds(left_at + j * per, per), :, :, out] = value.astype(LOW).reshape(
                    per, 2, size // per // 2, step_cols
                )

            loop(wide // step_cols, inner)

        if len(left.shape) == 2 and left.shape[1] < n_dp * grad.shape[2]:
            count = count * left.shape[1] // (n_dp * grad.shape[2])
        loop(count, body)

    g_up.drain()
    g_down.drain()
    weight_grad(second, ghid, wup, 0)
    r_up = Reduce(
        place, wires, wup, h_up, False, v["c_up"], None, v["y_up"], v["z_up"], v["p_up"]
    )
    r_up.core_send(0)
    r_up.core_send(1)

    for copy in second_copies:
        copy.wait_send()

    def other_down(step, carry):
        block = place.g_at(step)

        def keep(lane, value):
            second[block, :, lane] = value.astype(LOW)

        loop(width // tile, lambda n: down_tile(active.at[block], keep, n))
        return carry

    lax.fori_loop(1, groups, other_down, 0)

    def own_down(lane, value):
        outp[:, lane] = value + vecs[5:6, lane]

    loop(width // tile, lambda n: down_tile(active.at[g], own_down, n))
    weight_grad(active, cot_all, wdown, 0)
    c_down = v["c_skip"] if v["c_skip"].shape == v["wdown"].shape[:2] + (h_down, width) else v["c_down"]
    r_down = Reduce(
        place, wires, wdown, h_down, False, c_down, None, v["y_down"], v["z_down"], v["p_down"]
    )
    r_down.core_send(0)
    r_down.core_send(1)
    sums = v["sums"]
    sums[...] = jnp.zeros_like(sums)

    def column_sums(read, count, wide):
        def body(i, total):
            return total + jnp.sum(read(i).astype(F32), axis=0, keepdims=True)

        return lax.fori_loop(0, count, body, jnp.zeros((1, wide), F32))

    per_block = rows // chunk
    ghid_sum = column_sums(
        lambda i: ghid[lax.div(i, per_block), aligned(lax.rem(i, per_block) * chunk, chunk)],
        groups * per_block,
        units,
    )
    if units >= width:
        for row in range(sizes.up_rows):
            sums[6 + row : 7 + row] = ghid_sum[:, row * width : (row + 1) * width]
    else:
        sums[6:7, 0:units] = ghid_sum
    sums[5:6] = column_sums(lambda i: cot_all[g, aligned(i * chunk, chunk)], per_block, width)
    r_up.core_add(0)
    r_up.core_add(1)

    for step in range(1, groups):
        part_copy(step, second_first).wait_recv()

    def second_in(at):
        t = gmid[at]
        for step in range(1, groups):
            t = t + p_recv[step - 1, at].astype(F32)
        return t

    gb = v["gb"]

    def second_out(at, grad):
        total = grad + cot_all[g, at].astype(F32)
        gmid[at] = total
        gb[at] = total.astype(LOW)

    gain_sum, bias_sum = norm_back(middle, 3, second_in, second_out)
    sums[3:4] = gain_sum
    sums[4:5] = bias_sum

    ga_in, ga_send = v["ga_in"], att_send
    for step in range(1, groups):
        att_copy(step, place.g_at(step)).wait_send()
    ga_first = wires.take(groups)

    def ga_copy(step):
        block = place.g_at(step)
        return wires.copy(
            lambda: (ga_send.at[block], ga_in.at[g], place.x_peer(step)), ga_first + step
        )

    count, per, size = row_chunks(wout)

    def branch_back(j):
        value = dot_nt(gb[...], wout[pl.ds(j * per, per)].reshape(size, width)).astype(LOW)
        for b in range(max(1, size // cols)):
            if size >= cols:
                ga_send[j * (size // cols) + b] = value[:, b * cols : (b + 1) * cols]
            else:
                ga_send[lax.div(j, cols // size), :, aligned(lax.rem(j, cols // size) * size, size)] = value

    loop(count, branch_back)
    for step in range(1, groups):
        ga_copy(step).start()
    ga_in[g] = ga_send[g]
    out_swap = Exchange(place, wires)
    out_copies = [
        out_swap.copy(
            step, lambda step=step: second.at[place.g_at(step)], lambda: cot_all.at[g]
        )
        for step in range(1, groups)
    ]
    r_down.core_add(0)
    r_down.core_add(1)
    g_out.drain()
    weight_grad(att_own, gb, wout, 0)
    r_out = Reduce(
        place, wires, wout, h_out, True, v["c_out"], v["x_out"], v["y_out"], v["z_out"], v["p_out"]
    )
    r_out.core_send(0)
    r_out.core_send(1)

    gm = v["gm"]

    dkv = v["dkv"]
    gat, gqt, skt = vt.at[0, 0], vt.at[0, 1], vt.at[1, 0]

    def back_attend(block, first):
        gat[...] = ga_in[block].T

        def body(pair):
            lanes = aligned(pair * pair_width, pair_width)
            later = aligned(cols + pair * pair_width, pair_width)
            fixed, scores = [], []
            for half in range(2):
                head = pair * 2 + half
                at = head_at(pair, half)
                total = tot[block, head]
                grad_att = gat[at].astype(F32)
                scaled = padded(grad_att / total, half)
                grad_total = -jnp.sum(grad_att * attt[block, at], axis=0, keepdims=True) / total
                queries = qt[block, at]
                scores.append((padded(queries, half), slope_row(head), shift[block, head]))
                fixed.append(
                    (
                        scaled.astype(LOW),
                        scaled.T.astype(LOW),
                        grad_total,
                        padded(queries.astype(F32), half).T.astype(LOW),
                    )
                )

            def keys_in(core, b, carry):
                values = kv[core, b, :, later]
                key_grad, value_grad, done = 0.0, 0.0, []
                for half in range(2):
                    shift_sum, query_grad = carry[half]
                    scaled, scaled_nat, grad_total, queries_nat = fixed[half]
                    terms = score_terms(pair, core, b, *scores[half])
                    grad_score = terms * (dot(values, scaled) + grad_total)
                    shift_sum = shift_sum - jnp.sum(grad_score, axis=0, keepdims=True)
                    grad_low = grad_score.astype(LOW)
                    value_grad = value_grad + dot(terms.astype(LOW), scaled_nat)
                    key_grad = key_grad + dot(grad_low, queries_nat)
                    done.append((shift_sum, query_grad + dot(kt[core, b, lanes], grad_low)))
                for at, found in ((lanes, key_grad), (later, value_grad)):
                    if not first:
                        found = found + dkv[core, b, :, at].astype(F32)
                    dkv[core, b, :, at] = found.astype(LOW)
                return tuple(done)

            start = (jnp.zeros((1, rows), F32), jnp.zeros((pair_width, rows), F32))
            found = over_keys(keys_in, (start, start))
            for half in range(2):
                shift_sum, query_grad = found[half]
                at = head_at(pair, half)
                own = query_grad[half * head_width : (half + 1) * head_width]
                own_keys = kt[c, block, at].astype(F32)
                gqt[at] = (0.125 * (own + shift_sum * own_keys)).astype(LOW)
                skt[at] = (shift_sum * qt[block, at].astype(F32)).astype(LOW)

        loop(heads // 2, body)
        gm[block, :, 0:cols] = gqt[...].T
        dkv[c, block, :, 0:cols] = dkv[c, block, :, 0:cols] + skt[...].T

    dkv_wire = wires.take(1)

    def dkv_copy():
        return wires.copy(
            lambda: (dkv.at[1 - c], gm.at[:, :, cols : 3 * cols], place.c_peer()), dkv_wire
        )

    def back_attention():
        fill_far(g)
        back_attend(g, True)
        r_out.core_add(0)
        r_out.core_add(1)
        r_up.y_add()
        for step in range(1, groups):
            ga_copy(step).wait_recv()
        for copy in cot_copies:
            copy.wait_send()
        for copy in out_copies:
            copy.start()

        def other(step, carry):
            block = place.g_at(-step)
            fill_far(block)
            back_attend(block, False)
            return carry

        lax.fori_loop(1, groups, other, 0)

        dkv_copy().start()
        r_up.z_add()
        r_down.y_add()
        r_out.x_add(0)
        r_out.x_add(1)
        dkv_copy().wait_recv()

        def merge(b):
            gm[b, :, cols : 3 * cols] = gm[b, :, cols : 3 * cols] + dkv[c, b]

        loop(groups, merge)

    back_attention()

    parts_sent(second_first)
    mix_first = wires.take(groups)

    def other_mix(step, carry):
        block = place.g_at(step)
        send_part(step, gm.at[block], wqkv, mix_first)
        return carry

    lax.fori_loop(1, groups, other_mix, 0)
    for copy in out_copies:
        copy.wait_recv()
    ob = second.at[g]

    def out_rows(i):
        at = aligned(i * chunk, chunk)
        value = middle[at] + outp[at]
        for step in range(1, groups):
            value = value + cot_all[place.g_at(-step), at].astype(F32)
        ob[at] = value.astype(LOW)

    loop(rows // chunk, out_rows)
    stores = [pltpu.make_async_copy(ob, v["o_out"].at[0], local.at[0])]
    stores[0].start()
    back_product(gm.at[g], wqkv, store_into(middle, F32))
    g_qkv.drain()
    weight_grad(normed, gm, wqkv, 0)
    c_qkv = v["c_up"].at[:, :, :, 0 : 3 * cols]
    r_qkv = Reduce(
        place, wires, wqkv, h_qkv, False, c_qkv, None, v["y_qkv"], v["z_qkv"], v["p_qkv"]
    )
    r_qkv.core_send(0)
    r_qkv.core_send(1)
    r_down.z_add()
    r_out.y_add()
    r_qkv.core_add(0)
    r_qkv.core_add(1)
    for step in range(1, groups):
        part_copy(step, mix_first).wait_recv()

    def first_in(at):
        t = middle[at]
        for step in range(1, groups):
            t = t + p_recv[step - 1, at].astype(F32)
        return t

    def first_out(at, grad):
        gb[at] = (grad + gmid[at]).astype(LOW)

    gain_sum, bias_sum = norm_back(merged, 1, first_in, first_out)
    sums[1:2] = gain_sum
    sums[2:3] = bias_sum
    sums[0:1] = column_sums(lambda i: gb[aligned(i * chunk, chunk)], per_block, width)

    sum_in = v["sum_in"]

    def sum_swap(slot, peer):
        copy = wires.copy(lambda: (sums, sum_in.at[slot], peer))
        copy.start()
        return copy

    sum_core = sum_swap(0, place.c_peer())

    gj = cot_all

    def joined_back():
        _, _, size = row_chunks(ws)
        span = width // size

        def store(lane_index, value):
            gj[lax.div(lane_index, span), :, aligned(lax.rem(lane_index, span) * size, size)] = value

        count, per, size = row_chunks(ws)

        def body(j):
            value = dot_nt(gb[...], ws[pl.ds(j * per, per)].reshape(size, width))
            store(j, value.astype(LOW))

        loop(count, body)
        for half, name in enumerate(("o_frames", "o_skip")):
            stores.append(pltpu.make_async_copy(gj.at[half], v[name].at[0], local.at[1 + half]))
            stores[-1].start()

    if lend:
        parts_sent(mix_first)
        for store in stores:
            store.wait()
        stores.clear()
        for load in input_loads():
            load.start()
        for load in input_loads():
            load.wait()
    apart = ws.shape == wdown.shape
    grad_skip = wdown if apart else ws
    g_skip.drain()
    r_up.drain()
    r_down.drain()
    if not apart:
        joined_back()
    weight_grad(fr_v, gb, grad_skip, 0)
    weight_grad(sk_v, gb, grad_skip, nz // 2)
    r_skip = Reduce(
        place, wires, grad_skip, h_skip, True, v["c_skip"], v["x_skip"], v["y_skip"], v["z_skip"],
        v["p_skip"],
    )
    r_skip.core_send(0)
    r_skip.core_send(1)
    if apart:
        joined_back()
    r_skip.core_add(0)
    r_skip.core_add(1)
    r_qkv.y_add()
    sum_core.wait()
    sums[...] = sums[...] + sum_in[0]
    sum_x = [sum_swap(step, place.x_peer(step)) for step in range(1, groups)]
    r_out.z_add()
    r_up.spread_on()
    r_down.spread_on()
    for copy in sum_x:
        copy.wait()
    for step in range(1, groups):
        sums[0:6] = sums[0:6] + sum_in[step, 0:6]
    sum_y = sum_swap(groups, place.y_peer())
    r_qkv.z_add()
    r_skip.x_add(0)
    sum_y.wait()
    sums[...] = sums[...] + sum_in[groups]
    sum_z = [sum_swap(groups + step, place.z_peer(step)) for step in range(1, nz)]
    r_out.spread_on()
    r_skip.x_add(1)
    r_qkv.spread_on()
    for copy in sum_z:
        copy.wait()
    for step in range(1, nz):
        sums[...] = sums[...] + sum_in[groups + step]
    o_up = v["o_up"]
    o_up[g] = sums[...]
    v["o_small"][...] = sums[...]
    up_swap = Exchange(place, wires)
    up_copies = [up_swap.copy(step, lambda: o_up.at[g], lambda: o_up.at[g]) for step in range(1, groups)]
    for copy in up_copies:
        copy.start()
    r_skip.y_add()
    r_skip.z_add()
    r_skip.spread_on()

    for copy in up_copies:
        copy.wait()
    for reduced in (r_up, r_down, r_out, r_qkv, r_skip):
        reduced.finish()
    for reduced in (r_out, r_qkv, r_skip):
        reduced.drain()
    for gathered in (g_small, g_out):
        gathered.drain()
    for copy in seg_copies + [seg_core] + normed_copies + kv_waits:
        copy.wait_send()
    for copy in out_copies:
        copy.wait_send()
    for step in range(1, groups):
        ga_copy(step).wait_send()
    if not lend:
        parts_sent(mix_first)
    dkv_copy().wait_send()
    for store in stores:
        store.wait()


def per_device(sizes, *args):
    (
        frames, skip_frames, cotangent, seg_ids, positions,
        w_skip, b_skip, gain_attn, bias_attn, w_qkv, w_out,
        gain_ffn, bias_ffn, w_up, b_up, w_down, b_down,
    ) = args
    del positions
    n_dp, nz, groups = sizes.n_dp, sizes.nz, sizes.groups
    rows, width, cols, units = sizes.rows, sizes.width, sizes.cols, sizes.units
    heads, part, shard = sizes.heads, sizes.part, sizes.shard
    depth = w_up.shape[0]
    if not sizes.direct:
        w_up = (
            w_up.reshape(depth, n_dp, groups, part).transpose(0, 2, 1, 3).reshape(depth, groups * units)
        )
        group = lax.axis_index("blk") // 2
        b_up = lax.dynamic_slice_in_dim(b_up, group * part, part)
    r_skip, r_down = w_skip.shape[0], w_down.shape[0] // groups
    span = -(-max(shard, part) // 128) * 128

    def low(*shape):
        return pltpu.VMEM(shape, LOW)

    def full(*shape):
        return pltpu.VMEM(shape, F32)

    same = (r_skip, width) == (r_down, width)
    scratch = [
        low(2, rows, width), low(groups, rows, width),
        low(nz, 2, r_skip, width), low(nz, 2, depth, 3 * cols), low(nz, 2, depth, width),
        low(nz, 2, depth, units), low(nz, 2, r_down, width),
        full(nz, 2, 8, span), full(8, width), full(1, units),
        full(2, groups, 8, rows), low(2, groups, rows, 128),
        full(rows, width), full(rows, width), full(rows, width),
        low(groups, rows, width), low(groups, rows, width),
        low(2, groups, rows, 2 * cols),
        low(groups, cols, rows), low(2, groups, cols, rows),
        full(groups, heads, 1, rows), full(groups, cols, rows), full(groups, heads, 1, rows),
        low(rows, width), low(groups, rows, cols),
        low(groups, rows, units), low(groups, rows, units),
        low(1, 16, 128) if groups > 2 else low(1, rows, width),
        low(groups - 1, rows, width),
        low(rows, width), low(groups, rows, cols),
        low(groups, rows, 3 * cols),
        low(2, groups, rows, 2 * cols),
        full(2, groups, rows, rows), low(2, groups, cols, rows),
        low(nz, 2, r_skip // 2, width), low(nz, 2, depth // 2, width),
        low(nz, 2, depth // 2, units),
        low(1, 1, 16, 128) if same else low(nz, 2, r_down // 2, width),
        low(groups - 1, nz, 2, r_skip // 2, cols), low(groups - 1, nz, 2, depth // 2, cols),
        low(nz, r_skip // 2, cols), low(nz, depth // 2, 3 * cols), low(nz, depth // 2, cols),
        low(nz, depth // 2, units), low(nz, r_down // 2, width),
        low(nz - 1, r_skip // 2, cols), low(nz - 1, depth // 2, 3 * cols),
        low(nz - 1, depth // 2, cols), low(nz - 1, depth // 2, units),
        low(nz - 1, r_down // 2, width),
        full(8, width), full(groups + nz, 8, width),
        low(512 if groups * rows <= 512 else 256, groups * rows), full(rows, width),
    ]
    wires = 200 if groups * n_dp <= 16 else 1200
    scratch += [pltpu.SemaphoreType.DMA((wires,)), pltpu.SemaphoreType.DMA((wires,))]
    scratch += [pltpu.SemaphoreType.DMA((16,))]
    hbm, vmem = pl.BlockSpec(memory_space=pl.ANY), pl.BlockSpec(memory_space=pltpu.VMEM)
    whole = jax.ShapeDtypeStruct((1, rows, width), LOW)

    def piece(*shape):
        return jax.ShapeDtypeStruct((groups, 2) + shape, LOW)

    vectors = (b_skip, gain_attn, bias_attn, gain_ffn, bias_ffn, b_down, b_up)
    found = pl.pallas_call(
        functools.partial(kernel, sizes),
        out_shape=(
            whole, whole, whole,
            piece(r_skip // 2, cols), piece(depth // 2, 3 * cols), piece(depth // 2, cols),
            piece(depth // 2, units), piece(r_down // 2, width),
            jax.ShapeDtypeStruct((8, width), F32), jax.ShapeDtypeStruct((groups, 8, width), F32),
        ),
        in_specs=[hbm] * 3 + [vmem] * 8 + [hbm] * 5,
        out_specs=[hbm] * 3 + [vmem] * 7,
        scratch_shapes=scratch,
        compiler_params=pltpu.CompilerParams(
            collective_id=0, has_side_effects=True, vmem_limit_bytes=64 * 2**20
        ),
    )(
        frames, skip_frames, cotangent, seg_ids,
        *[vector.reshape(1, -1) for vector in vectors],
        w_skip, w_qkv, w_out, w_up, w_down,
    )
    output, grad_frames, grad_skip, p_skip, p_qkv, p_out, p_up, p_down, small, up = found

    def joined(pieces, inner):
        half = pieces.shape[2]
        split = pieces.reshape(groups, 2, half, inner, -1).transpose(1, 2, 3, 0, 4)
        return split.reshape(2 * half, -1).astype(F32)

    own = lax.dynamic_slice_in_dim(small, lax.axis_index("dp") * shard, shard, 1)
    flat = up[:, 6 : 6 + sizes.up_rows].reshape(groups, -1)
    own_up = lax.dynamic_slice_in_dim(flat, lax.axis_index("dp") * part, part, 1).reshape(-1)
    return (
        output, grad_frames, grad_skip,
        joined(p_skip, 1), own[0], own[1], own[2], joined(p_qkv, 3), joined(p_out, 1),
        own[3], own[4], joined(p_up, n_dp), own_up,
        p_down.reshape(-1, width).astype(F32), own[5],
    )


def solution(mesh):
    rows, lone = P("dp", None), P("dp")
    frames = P("dp", "blk", None)
    in_specs = (frames,) * 3 + (P("dp", "blk"),) * 2
    in_specs += (rows, lone, lone, lone, rows, rows, lone, lone, rows, lone, rows, lone)
    out_specs = (frames,) * 3
    out_specs += (rows, lone, lone, lone, rows, rows, lone, lone, rows, lone, rows, lone)

    def body(*args):
        return per_device(Sizes(mesh.shape, args[0], args[13]), *args)

    return jax.shard_map(
        body, mesh=mesh, in_specs=in_specs, out_specs=out_specs, check_vma=False
    )
```

time: 1380 us -> 315 us (0.23)
  waiting for transfers between devices: 904 us -> 0 us
  Pallas kernels: 0 us -> 289 us
  blocking collectives: 185 us -> 0 us
  matrix products: 144 us -> 0 us
  local copies, waits for them, and re-layouts: 76.5 us -> 21.3 us
  other arithmetic: 48.2 us -> 1.79 us
  between operations: 16.3 us -> 0.77 us
    reduce_scatter x6 -> x0, waiting for transfers between devices: 588 us -> none  [the longest x1 152 us: per_device(): lax.psum_scatter(grad_w_up.astype(jnp.bfloat16), 'dp', scatter_dimension=...]
    all_gather x6 -> x0, waiting for transfers between devices: 311 us -> none  [the longest x1 109 us: per_device(): lax.all_gather(w_down.astype(low_type), 'dp', axis=0, tiled=True)]
    pallas_call x0 -> x1, Pallas kernels: none -> 289 us  [per_device(): pl.pallas_call(functools.partial(kernel, sizes), out_shape=(whole, whole,...]
    all_gather x9 -> x0, blocking collectives: 146 us -> none  [the longest x1 26 us: per_device(): lax.all_gather(b_up.astype(low_type), 'dp', axis=0, tiled=True)]
    dot_general x29 -> x0, matrix products: 144 us -> none  [the longest x5 25.8 us: col_product(): jnp.einsum('rk,rn->kn', left_rows, right_rows, preferred_element_type=jnp...]
    unnamed x1 -> x0, blocking collectives: 33 us -> none
    convert_element_type x33 -> x3, other arithmetic: 33.7 us -> 1.79 us  [the longest x1 1.63 us: per_device(): p_down.reshape(-1, width).astype(F32)]
    dynamic_update_slice x4 -> x0, local copies, waits for them, and re-layouts: 20.2 us -> none  [backward_step(): lax.dynamic_update_slice_in_dim(state_in[2], current + joined_grads, offs...]
  transfers between devices with their start and end apart: 13 -> 0, of which waited for: 11 -> 0; matrix products, arithmetic and copies ran while one was open for 9% -> 0% of each run, Pallas kernels for 0% -> 0%
where the time goes in v1:
time: 315 us; the launch traced here: 313 us
  Pallas kernels  289 us (92%)
  local copies, waits for them, and re-layouts  21.3 us (7%)
    pallas_call x1, Pallas kernels, per_device(): pl.pallas_call(functools.partial(kernel, sizes), out_shape=(whole, whole,...  289 us
    convert_element_type x7, local copies, waits for them, and re-layouts, joined(): return split.reshape(2 * half, -1).astype(F32)  12.7 us
    unnamed x24, local copies, waits for them, and re-layouts  7.36 us

profile of v1, /device:TPU:0, one launch (start us, length us, event | category | flops | bytes accessed | tf_op | source)
XLA Modules:
  0.0 313.2 jit_solution(11202905173081949225)
XLA Ops:
  0.7 289.4 %shard_map.271 = (bf16[1,256,1024]{2,1,0:T(8,128)(2,1)}, bf16[1,256,1024]{2,1,0:T(8,128)(2,1)}, bf16[1,256,1024]{2,1,0:T(8,128)(2,1)}, bf16[2,2,128,512]{3,2,1,0...) custom-call(bf16[1,256,1024]{2,1,0:T(8,128)(2,1)} %refs_0_.1, ...), custom_call_target="tpu_custom_call" | custom-call | tf_op jit(solution)/shard_map/pallas_call | solution.py:1352
  290.0 0.7 constant_dynamic-slice_fusion
  290.7 0.5 slice_bitcast_fusion.1
  291.3 0.8 slice_bitcast_fusion
  292.1 0.6 copy.44
  292.7 1.5 copy.42
  294.2 1.6 copy.39
  295.8 0.0 copy-start.1
  295.8 2.7 reshape.96
  298.5 0.0 copy-done.1
  298.5 1.4 reshape.99
  299.9 2.4 copy.37
  302.3 3.5 %reshape.94 = f32[128,3072]{1,0:T(8,128)} reshape(f32[2,64,3,2,512]{4,3,2,1,0:T(2,128)} %copy.37) | data formatting | bytes 3145728 | tf_op jit(solution)/shard_map/convert_element_type | solution.py:1376
  305.7 0.0 copy-done.2
  305.7 0.1 convert_bitcast_fusion
  305.9 0.8 copy.36
  306.7 1.2 copy.40
  307.8 1.6 bitcast_convert_fusion
  309.5 0.0 copy-start.3
  309.6 0.4 copy.38
  310.0 0.9 copy.41
  310.9 0.8 copy.48
  311.7 0.8 copy.49
  312.5 0.8 copy.50
  (13 shorter events, 0.1 us)
Async XLA Ops:
  295.8 2.7 copy-start.1
  302.3 3.5 %copy-start.2 = (bf16[2,2,128,512]{3,2,1,0:T(8,128)(2,1)S(1)}, bf16[2,2,128,512]{3,2,1,0:T(8,128)(2,1)}, u32[]{:S(2)}) copy-start(bf16[2,2,128,512]{3,2,1,0:T(8,128)(2,1)} %get-tuple-element.28) | copy-start | bytes 1572868
  305.8 2.0 copy-start
  307.8 1.6 copy-start.6
  309.5 1.4 copy-start.5
  309.5 2.2 copy-start.4
  309.5 2.9 copy-start.3

commit v2 on v1

--- a/solution.py
+++ b/solution.py
@@ -30,6 +30,14 @@
         return carry
 
     lax.fori_loop(0, count, visit, 0)
+
+
+def loop_from(first, last, body):
+    def visit(index, carry):
+        body(index)
+        return carry
+
+    lax.fori_loop(first, last, visit, 0)
 
 
 def aligned(start, size):
@@ -50,12 +58,13 @@
         self.units = self.hidden // self.groups
         self.part = self.units // self.n_dp
         self.direct = self.part % 128 == 0
+        self.share = max(1, self.width // (self.groups + 2) // 128) * 128
         self.up_rows = -(-self.units // self.width)
 
 
 class Wires:
-    def __init__(self, send_sems, recv_sems):
-        self.send_sems, self.recv_sems, self.used = send_sems, recv_sems, 0
+    def __init__(self, place, send_sems, recv_sems):
+        self.place, self.send_sems, self.recv_sems, self.used = place, send_sems, recv_sems, 0
 
     def take(self, count=1):
         first = self.used
@@ -73,11 +82,14 @@
 
     def made(self):
         source, target, peer = self.ends()
+        index = self.index
+        if isinstance(index, tuple):
+            index = index[0] + self.wires.place.z + index[1]
         return pltpu.make_async_remote_copy(
             src_ref=source,
             dst_ref=target,
-            send_sem=self.wires.send_sems.at[self.index],
-            recv_sem=self.wires.recv_sems.at[self.index],
+            send_sem=self.wires.send_sems.at[index],
+            recv_sem=self.wires.recv_sems.at[index],
             device_id=peer,
             device_id_type=MESH,
         )
@@ -113,6 +125,15 @@
     def z_peer(self, step):
         return (self.z_at(step) * 2 + self.y, self.blk)
 
+    def z_next(self, way):
+        return ((self.z + way) * 2 + self.y, self.blk)
+
+    def if_z(self, *distances):
+        low, high = min(distances + (0,)), max(distances + (0,))
+        if low < 0 and high > 0:
+            return pl.when(jnp.logical_and(self.z >= -low, self.z < self.sizes.nz - high))
+        return pl.when(self.z >= -low if low < 0 else self.z < self.sizes.nz - high)
+
     def y_peer(self):
         return (self.z * 2 + 1 - self.y, self.blk)
 
@@ -124,84 +145,143 @@
 
 
 class Gather:
-    def __init__(self, place, wires, ref, half, spread, whole_core=False):
+    def __init__(self, place, wires, ref, half, spread=0, span=None, whole_core=False):
         self.place, self.wires, self.ref = place, wires, ref
-        self.half, self.spread, self.whole_core = half, spread, whole_core
-        sizes = place.sizes
-        self.nz = sizes.nz
-        self.groups = sizes.groups if spread else 1
-        self.z_copies, self.y_copies, self.x_copies, self.c_copies = {}, {}, {}, {}
-
-    def piece(self, k, step=0):
+        self.half, self.spread, self.span, self.whole_core = half, spread, span, whole_core
+        self.nz = place.sizes.nz
+        self.groups = place.sizes.groups if spread else 1
+        self.z_wires = {way: wires.take(self.nz) for way in (1, -1)}
+        self.y_wires = wires.take(self.nz)
+        self.x_wires = {
+            (step, far): wires.take(self.nz) for step in range(1, self.groups) for far in (0, 1)
+        }
+        self.c_wires = {
+            (step, far): 0 if whole_core else wires.take(self.nz)
+            for step in range(self.groups)
+            for far in (0, 1)
+        }
+
+    def at(self, distance, far, step=0):
         place = self.place
-        z_index = place.z_at(-(k % self.nz))
-        y_index = place.y if k < self.nz else 1 - place.y
+        z_index = place.z + distance
+        y_index = 1 - place.y if far else place.y
         if self.whole_core:
             return self.ref.at[z_index, y_index]
         rows = aligned(place.c * self.half, self.half)
+        if self.span:
+            return self.ref.at[z_index, y_index, rows, self.span[0] : self.span[1]]
         if not self.spread:
             return self.ref.at[z_index, y_index, rows]
-        cols = place.sizes.cols
-        return self.ref.at[z_index, y_index, rows, aligned(place.g_at(-step) * cols, cols)]
-
-    def send(self, copies, key, piece, peer):
-        copies[key] = self.wires.copy(lambda: (piece(), piece(), peer()))
-        copies[key].start()
+        cols = aligned(place.g_at(-step) * self.spread, self.spread)
+        return self.ref.at[z_index, y_index, rows, cols]
+
+    def copy(self, first, peer, distance, far, step=0):
+        def ends():
+            piece = self.at(distance, far, step)
+            return piece, piece, peer()
+
+        return self.wires.copy(ends, (first, distance))
+
+    def z_copy(self, way, distance):
+        return self.copy(self.z_wires[way], lambda: self.place.z_next(way), distance, 0)
+
+    def y_copy(self, distance):
+        return self.copy(self.y_wires, self.place.y_peer, distance, 0)
+
+    def y_arrival(self, distance):
+        return self.copy(self.y_wires, self.place.y_peer, distance, 1)
+
+    def x_copy(self, step, distance, far):
+        first = self.x_wires[step, far]
+        return self.copy(first, lambda: self.place.x_peer(step), distance, far)
+
+    def c_copy(self, step, distance, far):
+        return self.copy(self.c_wires[step, far], self.place.c_peer, distance, far, step)
+
+    def each(self, reach, body):
+        if reach == 0:
+            body(0)
+            return
+        for distance in (-reach, reach):
+            self.place.if_z(distance)(functools.partial(body, distance))
 
     def start(self):
-        for step in range(1, self.nz):
-            self.send(
-                self.z_copies, step, lambda: self.piece(0), lambda step=step: self.place.z_peer(step)
-            )
-        self.forward(0)
-
-    def forward(self, k):
-        def piece():
-            return self.piece(k)
-
-        if k < self.nz:
-            self.send(self.y_copies, k, piece, self.place.y_peer)
+        for way in (1, -1):
+            self.place.if_z(way)(lambda way=way: self.z_copy(way, 0).start())
+
+    def own(self):
+        self.forward(0, 0)
+
+    def forward(self, distance, far):
+        if not far:
+            self.y_copy(distance).start()
         for step in range(1, self.groups):
-            self.send(self.x_copies, (step, k), piece, lambda step=step: self.place.x_peer(step))
+            self.x_copy(step, distance, far).start()
         if not self.whole_core:
-            self.send(self.c_copies, (0, k), piece, self.place.c_peer)
-
-    def z_step(self, step):
-        self.z_copies[step].wait_recv()
-        self.forward(step)
-
-    def y_step(self, k):
-        self.y_copies[k].wait_recv()
-        self.forward(self.nz + k)
-
-    def x_step(self, k):
-        for step in range(1, self.groups):
-            self.x_copies[step, k].wait_recv()
-            self.send(
-                self.c_copies, (step, k), lambda step=step: self.piece(k, step), self.place.c_peer
-            )
+            self.c_copy(0, distance, far).start()
+
+    def z_step(self, reach):
+        def body(distance):
+            way = 1 if distance < 0 else -1
+            self.z_copy(way, distance).wait_recv()
+            self.place.if_z(way)(lambda: self.z_copy(way, distance).start())
+            self.forward(distance, 0)
+
+        self.each(reach, body)
+
+    def y_step(self, reach):
+        def body(distance):
+            self.y_arrival(distance).wait_recv()
+            self.forward(distance, 1)
+
+        self.each(reach, body)
+
+    def x_step(self, reach, far):
+        def body(distance):
+            for step in range(1, self.groups):
+                self.x_copy(step, distance, far).wait_recv()
+                self.c_copy(step, distance, far).start()
+
+        self.each(reach, body)
 
     def z_steps(self):
-        for step in range(1, self.nz):
-            self.z_step(step)
+        for reach in range(1, self.nz):
+            self.z_step(reach)
 
     def y_steps(self):
-        for k in range(self.nz):
-            self.y_step(k)
+        for reach in range(self.nz):
+            self.y_step(reach)
 
     def x_steps(self):
-        for k in range(2 * self.nz):
-            self.x_step(k)
+        for far in (0, 1):
+            for reach in range(self.nz):
+                self.x_step(reach, far)
+
+    def c_wait(self, reach, far):
+        def body(distance):
+            for step in range(self.groups):
+                self.c_copy(step, distance, far).wait_recv()
+
+        self.each(reach, body)
 
     def finish(self):
-        for copy in self.c_copies.values():
-            copy.wait_recv()
+        for far in (0, 1):
+            for reach in range(self.nz):
+                self.c_wait(reach, far)
 
     def drain(self):
-        for copies in (self.z_copies, self.y_copies, self.x_copies, self.c_copies):
-            for copy in copies.values():
-                copy.wait_send()
-            copies.clear()
+        def body(distance):
+            for way in (1, -1) if distance == 0 else (1,) if distance < 0 else (-1,):
+                self.place.if_z(way)(lambda way=way: self.z_copy(way, distance).wait_send())
+            self.y_copy(distance).wait_send()
+            for first in self.x_wires:
+                self.x_copy(first[0], distance, first[1]).wait_send()
+            if not self.whole_core:
+                for first in self.c_wires:
+                    self.c_copy(first[0], distance, first[1]).wait_send()
+
+        for reach in range(self.nz):
+            self.each(reach, body)
 
 
 class Exchange:
@@ -221,7 +301,7 @@
         self.place, self.wires, self.grad, self.half, self.spread = place, wires, grad, half, spread
         self.core_in, self.x_in, self.y_in, self.z_in, self.out = core_in, x_in, y_in, z_in, out
         self.nz, self.groups = place.sizes.nz, place.sizes.groups
-        self.core_copies, self.x_copies, self.z_copies = {}, {}, {}
+        self.core_copies, self.x_copies, self.y_copies, self.z_copies = {}, {}, {}, {}
         self.fin_copies, self.fwd_copies = {}, {}
 
     def side(self, part):
@@ -285,23 +365,23 @@
         return self.x_in.at[0] if self.spread else self.core_in
 
     def y_send(self):
-        self.y_copy = self.wires.copy(
-            lambda: (self.held().at[:, self.side(0)], self.y_in, self.place.y_peer())
-        )
-        self.y_copy.start()
-
-    def y_add(self):
-        self.y_copy.wait()
-        side = self.side(1)
-        held = self.held()
-
-        def body(z):
-            self.y_in[z] = self.y_in[z] + held[z, side]
-
-        loop(self.nz, body)
-        for step in range(1, self.nz):
+        for step in [*range(1, self.nz), 0]:
+
+            def ends(step=step):
+                z_index = self.place.z_at(step)
+                source = self.held().at[z_index, self.side(0)]
+                return source, self.y_in.at[z_index], self.place.y_peer()
+
+            self.y_copies[step] = self.wires.copy(ends)
+            self.y_copies[step].start()
+
+    def y_add(self, step):
+        self.y_copies[step].wait_recv()
+        z_index, side, held = self.place.z_at(step), self.side(1), self.held()
+        self.y_in[z_index] = self.y_in[z_index] + held[z_index, side]
+        if step:
             copy = self.wires.copy(
-                lambda step=step: (
+                lambda: (
                     self.y_in.at[self.place.z_at(step)],
                     self.z_in.at[step - 1],
                     self.place.z_peer(step),
@@ -310,6 +390,15 @@
             copy.start()
             self.z_copies[step] = copy
 
+    def y_tasks(self):
+        steps = [*range(1, self.nz), 0]
+        return [functools.partial(self.y_add, step) for step in steps]
+
+    def y_sent(self):
+        for copy in self.y_copies.values():
+            copy.wait_send()
+        self.y_copies.clear()
+
     def z_add(self):
         place = self.place
         for step in range(1, self.nz):
@@ -344,8 +433,15 @@
         )
         self.fwd_copies[step].start()
 
+    def core_sent(self):
+        for copy in self.core_copies.values():
+            copy.wait_send()
+        self.core_copies.clear()
+
     def drain(self):
-        for copies in (self.core_copies, self.x_copies, self.z_copies, self.fin_copies):
+        self.core_sent()
+        self.y_sent()
+        for copies in (self.x_copies, self.z_copies, self.fin_copies):
             for copy in copies.values():
                 copy.wait_send()
 
@@ -367,21 +463,34 @@
         "o_skip", "p_skip", "p_qkv", "p_out", "p_up", "p_down", "o_small", "o_up", "io",
         "cot_all", "ws", "wqkv", "wout", "wup", "wdown", "small", "vecs", "bup", "segs", "segc",
         "merged", "middle", "gmid", "normed", "second", "kv", "qt", "kt", "shift", "attt", "tot",
-        "att_own", "att_send", "active", "ghid", "p_send", "p_recv", "gb", "ga_in", "gm", "dkv",
+        "att_own", "att_send", "active", "ghid", "p_send", "p_recv", "gb", "ga_in", "gm",
         "far", "vt", "c_skip", "c_out", "c_up", "c_down", "x_skip", "x_out", "y_skip", "y_qkv",
-        "y_out", "y_up", "y_down", "z_skip", "z_qkv", "z_out", "z_up", "z_down", "sums",
-        "sum_in", "turned", "outp", "send_sems", "recv_sems", "local_sems",
+        "y_out", "y_up", "y_down", "z_skip", "z_qkv", "z_out", "z_up", "z_down", "joined", "gmx", "grad_down", "sums",
+        "sum_in", "turned", "send_sems", "recv_sems", "local_sems", "free_sem",
     )
     assert len(names) == len(refs), (len(names), len(refs))
     v = dict(zip(names, refs))
     place = Place(sizes)
-    wires = Wires(v["send_sems"], v["recv_sems"])
+    wires = Wires(place, v["send_sems"], v["recv_sems"])
     local = v["local_sems"]
     nz, groups, n_dp, n_blk = sizes.nz, sizes.groups, sizes.n_dp, sizes.n_blk
     rows, width, cols, units = sizes.rows, sizes.width, sizes.cols, sizes.units
     heads = sizes.heads
     z, y, g, c = place.z, place.y, place.g, place.c
 
+    def each_group(body):
+        if groups == 2:
+            body(1)
+        else:
+            loop_from(1, groups, body)
+
+    tasks = []
+
+    def work(count=None):
+        for task in tasks[:count]:
+            task()
+        del tasks[:count]
+
     barrier = pltpu.get_barrier_semaphore()
     partners = [place.z_peer(step) for step in range(1, nz)] + [place.y_peer()]
     partners += [place.x_peer(step) for step in range(1, groups)] + [place.c_peer()]
@@ -405,26 +514,28 @@
 
     stages = {}
 
-    def fetch(name, start, size, buffer, top, index):
-        parts = v[name].shape[1] // width
+    def fetch(name, start, size, tops, index):
         copies = [
             pltpu.make_async_copy(
                 v[name].at[aligned(start, size), part * width : (part + 1) * width],
-                buffer.at[top + part * size : top + (part + 1) * size],
+                buffer.at[top : top + size],
                 local.at[index + part],
             )
-            for part in range(parts)
+            for part, (buffer, top) in enumerate(tops)
         ]
         for copy in copies:
             copy.start()
         stages[name] = copies
 
-    merged, middle, gmid, outp = v["merged"], v["middle"], v["gmid"], v["outp"]
-    fetch("w_skip", c * h_skip, h_skip, merged, 0, 3)
-    fetch("w_qkv", c * h_qkv, h_qkv, gmid, 0, 4)
-    fetch("w_out", c * h_out, h_out, merged, h_skip, 7)
-    fetch("w_up", c * h_up, h_up, outp, 0, 8)
-    fetch("w_down", (g * 2 + c) * h_down, h_down, middle, 0, 12)
+    merged, middle, gmid = v["merged"], v["middle"], v["gmid"]
+    up_tops = [
+        (middle, h_down), (middle, h_down + h_up), (merged, h_skip + h_out), (gmid, 3 * h_qkv)
+    ]
+    fetch("w_skip", c * h_skip, h_skip, [(merged, 0)], 3)
+    fetch("w_qkv", c * h_qkv, h_qkv, [(gmid, third * h_qkv) for third in range(3)], 4)
+    fetch("w_out", c * h_out, h_out, [(merged, h_skip)], 7)
+    fetch("w_up", c * h_up, h_up, up_tops, 8)
+    fetch("w_down", (g * 2 + c) * h_down, h_down, [(middle, 0)], 12)
     for load in loads:
         load.start()
     ws, wqkv, wout, wup, wdown = v["ws"], v["wqkv"], v["wout"], v["wup"], v["wdown"]
@@ -435,7 +546,11 @@
             copy.wait()
 
     arrived("w_skip")
-    ws[z, y, aligned(c * h_skip, h_skip), own_cols] = merged[0:h_skip, own_cols].astype(LOW)
+    share, shared = sizes.share, groups * sizes.share
+    own_share, skip_rows = aligned(g * share, share), aligned(c * h_skip, h_skip)
+    ws[z, y, skip_rows, own_share] = merged[0:h_skip, own_share].astype(LOW)
+    if shared < width:
+        ws[z, y, skip_rows, shared:width] = merged[0:h_skip, shared:width].astype(LOW)
     arrived("w_qkv")
     for third in range(3):
         wqkv[z, y, aligned(c * h_qkv, h_qkv), third * cols : (third + 1) * cols] = gmid[
@@ -451,15 +566,17 @@
         part = sizes.part
         per_row = width // (part * groups)
         for s in range(n_dp):
-            at = (s // per_row) * h_up
-            wup[z, y, up_rows, s * part : (s + 1) * part] = outp[
-                at : at + h_up, aligned(g * part + s % per_row * part * groups, part)
-            ].astype(LOW)
+            buffer, top = up_tops[s // per_row]
+            lane = aligned(g * part + s % per_row * part * groups, part)
+            wup[z, y, up_rows, s * part : (s + 1) * part] = buffer[top : top + h_up, lane].astype(LOW)
     else:
-        at = pl.multiple_of(lax.div(g * units, width) * h_up, h_up)
-        wup[z, y, up_rows] = outp[
-            pl.ds(at, h_up), aligned(lax.rem(g * units, width), units)
-        ].astype(LOW)
+        for index, (buffer, top) in enumerate(up_tops):
+
+            @pl.when(lax.div(g * units, width) == index)
+            def _(buffer=buffer, top=top):
+                lane = aligned(lax.rem(g * units, width), units)
+                wup[z, y, up_rows] = buffer[top : top + h_up, lane].astype(LOW)
+
     arrived("w_down")
     wdown[z, y, aligned(c * h_down, h_down)] = middle[0:h_down].astype(LOW)
 
@@ -476,39 +593,69 @@
 
     pl.semaphore_wait(barrier, len(partners))
 
-    g_small = Gather(place, wires, small, 0, False, whole_core=True)
-    g_skip = Gather(place, wires, v["ws"], h_skip, True)
-    g_qkv = Gather(place, wires, v["wqkv"], h_qkv, False)
-    g_out = Gather(place, wires, v["wout"], h_out, True)
-    g_up = Gather(place, wires, v["wup"], h_up, False)
-    g_down = Gather(place, wires, v["wdown"], h_down, False)
+    g_small = Gather(place, wires, small, 0, whole_core=True)
+    g_skip = Gather(place, wires, v["ws"], h_skip, spread=share)
+    g_rest = Gather(place, wires, v["ws"], h_skip, span=(shared, width))
+    g_qkv = Gather(place, wires, v["wqkv"], h_qkv)
+    g_out = Gather(place, wires, v["wout"], h_out, spread=cols)
+    g_up = Gather(place, wires, v["wup"], h_up)
+    g_down = Gather(place, wires, v["wdown"], h_down)
+    skips = [g_skip, g_rest] if shared < width else [g_skip]
     seg_swap = Exchange(place, wires)
     seg_copies = []
     for step in range(1, groups):
         seg_copies.append(seg_swap.copy(step, lambda: segs.at[c, g], lambda: segs.at[c, g]))
         seg_copies[-1].start()
-    g_small.start()
-    g_skip.start()
-    g_qkv.start()
-    g_out.start()
-    g_up.start()
-    g_down.start()
+    for gather in [g_small] + skips:
+        gather.start()
+    for gather in skips + [g_small, g_qkv]:
+        gather.own()
+
+    joined_copies, joined_parts = [], []
+    if sizes.pair:
+        for load in loads:
+            load.wait()
+        lines = rows // 4
+        for part in range(8):
+            at = part // 4, pl.ds(part % 4 * lines, lines)
+            copy = Exchange(place, wires).copy(
+                1, lambda at=at: v["io"].at[at], lambda at=at: v["joined"].at[at]
+            )
+            joined_copies.append(copy)
+            joined_parts.append(copy)
+
+    def send_joined(count):
+        for copy in joined_parts[:count]:
+            copy.start()
+        del joined_parts[:count]
+
+    send_joined(1)
+    for reach in range(1, nz):
+        g_skip.z_step(reach)
+        if reach == nz - 1:
+            g_qkv.start()
+        if reach > 1:
+            g_skip.y_step(reach - 2)
+        g_skip.x_step(reach - 1, 0)
+        send_joined(1)
     for copy in seg_copies:
         copy.wait_recv()
     seg_core = wires.copy(lambda: (segs.at[c], segs.at[c], place.c_peer()))
     seg_core.start()
-    for step in range(1, nz):
-        g_skip.z_step(step)
-        g_small.z_step(step)
-    for k in range(nz):
-        g_skip.x_step(k)
-        g_skip.y_step(k)
-        g_small.y_step(k)
-    for k in range(nz, 2 * nz):
-        g_skip.x_step(k)
-
-    for load in loads:
-        load.wait()
+    for gather in skips[1:] + [g_small]:
+        gather.z_steps()
+    g_skip.x_step(nz - 1, 0)
+    g_skip.y_step(nz - 2)
+    g_skip.y_step(nz - 1)
+    for reach in range(nz):
+        g_skip.x_step(reach, 1)
+        for gather in skips[1:] + [g_small]:
+            gather.y_step(reach)
+    g_up.own()
+
+    if not sizes.pair:
+        for load in loads:
+            load.wait()
     vecs = v["vecs"]
     for row in range(6):
         vecs[row : row + 1] = jnp.concatenate(
@@ -526,8 +673,10 @@
             segc[core, block] = turned_ids.astype(LOW)
 
         loop(groups, turn)
-    g_qkv.z_steps()
-    g_skip.finish()
+    g_out.start()
+    g_qkv.z_step(1)
+    for gather in skips:
+        gather.finish()
 
     tile = min(256, width)
 
@@ -540,6 +689,7 @@
         )
 
     loop(width // tile, merge_tile)
+    g_qkv.z_step(2)
     chunk = 64
 
     def norm_into(held, gain_row, target):
@@ -586,7 +736,6 @@
 
     norm_into(merged, 1, normed.at[g])
     normed_copies = share(normed)
-    cot_copies = share(cot_all)
 
     kv, qt, kt = v["kv"], v["qt"], v["kt"]
     shift = v["shift"]
@@ -629,17 +778,25 @@
         for head in range(heads):
             shift[block, head] = found[head : head + 1] * 0.125
 
-    g_qkv.y_steps()
+    g_up.start()
+    for step in range(3, nz):
+        g_qkv.z_step(step)
+    g_out.own()
+    g_down.own()
+    for k in range(nz - 1):
+        g_qkv.y_step(k)
+    g_out.z_steps()
+    g_qkv.y_step(nz - 1)
     g_qkv.finish()
+    g_down.start()
     mix(g, 0)
-    g_out.z_steps()
     for copy in normed_copies:
         copy.wait_recv()
 
     def mix_other(step):
         mix(place.g_at(-step), step)
 
-    lax.fori_loop(1, groups, lambda step, carry: (mix_other(step), carry)[1], 0)
+    each_group(mix_other)
     g_up.z_step(1)
     g_out.y_steps()
 
@@ -749,11 +906,10 @@
         g_out.x_steps()
         fill_far(g)
         attend(g)
+        send_joined(1)
         att_own[:, own_cols] = attt[g].T.astype(LOW)
 
     attention()
-    for step in range(3, nz):
-        g_up.z_step(step)
     g_out.finish()
     for step in range(1, groups):
         att_copy(step, place.g_at(step)).wait_recv()
@@ -767,38 +923,37 @@
     loop(width // tile, middle_tile)
     norm_into(middle, 3, second.at[g])
     second_copies = share(second)
+    cot_copies = share(cot_all)
+    for step in range(3, nz):
+        g_up.z_step(step)
     g_up.y_steps()
-    g_down.z_steps()
+    g_down.z_step(1)
     g_up.finish()
-    g_down.y_steps()
-    g_down.finish()
 
     active, ghid = v["active"], v["ghid"]
     unit_tile = 256
     shard_rows = wdown.shape[2]
-
-    def down_rows(u):
-        if shard_rows >= unit_tile:
-            per = shard_rows // unit_tile
-            s = lax.div(u, per)
-            return wdown[lax.div(s, 2), lax.rem(s, 2), aligned(lax.rem(u, per) * unit_tile, unit_tile)]
-        per = unit_tile // (2 * shard_rows)
-        return wdown[pl.ds(u * per, per)].reshape(unit_tile, width)
-
-    for copy in cot_copies:
-        copy.wait_recv()
 
     def feed(block):
         def body(u):
             lane = aligned(u * unit_tile, unit_tile)
             pre = dot(second[block], wup[:, :, :, lane].reshape(width, unit_tile)) + v["bup"][:, lane]
-            back = dot_nt(cot_all[block], down_rows(u))
             normal = 0.5 * (1.0 + lax.erf(pre * (0.5**0.5)))
             active[block, :, lane] = (pre * normal).astype(LOW)
             slope = normal + pre * (jnp.exp(-0.5 * pre * pre) * (1.0 / math.sqrt(2.0 * math.pi)))
-            ghid[block, :, lane] = (back * slope).astype(LOW)
+            ghid[block, :, lane] = slope.astype(LOW)
 
         loop(units // unit_tile, body)
+
+    def feed_back(lane, weight):
+        def body(block):
+            back = dot_nt(cot_all[block], weight)
+            ghid[block, :, lane] = (back * ghid[block, :, lane].astype(F32)).astype(LOW)
+
+        for block in range(groups) if groups == 2 else ():
+            body(block)
+        if groups > 2:
+            loop(groups, body)
 
     def row_chunks(ref, most=512):
         per = min(nz, max(1, most // (2 * ref.shape[2])))
@@ -822,59 +977,18 @@
 
         return store
 
-    feed(g)
-    for copy in second_copies:
-        copy.wait_recv()
-    second_first = wires.take(groups)
-
-    def part_copy(step, first):
-        return wires.copy(
-            lambda: (p_send.at[part_slot(step)], p_recv.at[step - 1], place.x_peer(step)),
-            first + step,
-        )
-
-    def part_slot(step):
-        return 0 if groups == 2 else lax.rem(step, 2)
-
-    def send_part(step, left, weight, first):
-        if groups > 3:
-
-            @pl.when(step > 2)
-            def _():
-                part_copy(step - 2, first).wait_send()
-
-        back_product(left, weight, store_into(p_send.at[part_slot(step)], LOW))
-        part_copy(step, first).start()
-
-    def parts_sent(first):
-        for step in range(max(1, groups - 2), groups):
-            part_copy(step, first).wait_send()
-
-    def other_feed(step, carry):
-        block = place.g_at(step)
-        feed(block)
-        send_part(step, ghid.at[block], wup, second_first)
-        return carry
-
-    lax.fori_loop(1, groups, other_feed, 0)
-    back_product(ghid.at[g], wup, store_into(gmid, F32))
-
-    def down_tile(left, target, n):
-        lane = aligned(n * tile, tile)
-        target(lane, dot(left[...], wdown[:, :, :, lane].reshape(units, tile)))
-
     turned = v["turned"]
 
-    def weight_grad(left, right, grad, left_at):
+    def weight_grad(lefts, right, grad, left_at=0):
         count, per, size = row_chunks(grad, turned.shape[0])
-        wide = grad.shape[3]
-        step_cols = min(256, wide)
-        depth = left.shape[0] if len(left.shape) == 2 else left.shape[0] * left.shape[1]
+        step_cols = min(256, grad.shape[3])
+        depth = len(lefts) * rows
+        count = count * lefts[0].shape[1] // (n_dp * grad.shape[2])
 
         def body(j):
             lane = aligned(j * size, size)
-            part = left[:, lane] if len(left.shape) == 2 else left[:, :, lane]
-            turned[0:size, 0:depth] = part.reshape(depth, size).T
+            for b, left in enumerate(lefts):
+                turned[0:size, b * rows : (b + 1) * rows] = left[:, lane].T
 
             def inner(n):
                 out = aligned(n * step_cols, step_cols)
@@ -884,15 +998,99 @@
                     per, 2, size // per // 2, step_cols
                 )
 
-            loop(wide // step_cols, inner)
-
-        if len(left.shape) == 2 and left.shape[1] < n_dp * grad.shape[2]:
-            count = count * left.shape[1] // (n_dp * grad.shape[2])
+            loop(grad.shape[3] // step_cols, inner)
+
         loop(count, body)
+
+    def blocks(ref):
+        return [ref.at[b] for b in range(groups)]
+
+    feed(g)
+    g_down.z_step(2)
+    second_first = wires.take(groups)
+
+    def part_copy(step, first):
+        return wires.copy(
+            lambda: (p_send.at[part_slot(step)], p_recv.at[step - 1], place.x_peer(step)),
+            first + step,
+        )
+
+    def part_slot(step):
+        return 0 if groups == 2 else lax.rem(step, 2)
+
+    def send_part(step, left, weight, first):
+        if groups > 3:
+
+            @pl.when(step > 2)
+            def _():
+                part_copy(step - 2, first).wait_send()
+
+        back_product(left, weight, store_into(p_send.at[part_slot(step)], LOW))
+        part_copy(step, first).start()
+
+    def parts_sent(first):
+        for step in range(max(1, groups - 2), groups):
+            part_copy(step, first).wait_send()
+
+    for copy in second_copies:
+        copy.wait_recv()
+    each_group(lambda step: feed(place.g_at(step)))
+    send_joined(len(joined_parts))
+    early = shard_rows == unit_tile
+    grad_down = v["grad_down"] if early else wdown
+    r_down = Reduce(
+        place, wires, grad_down, h_down, False, v["c_down"], None, v["y_down"], v["z_down"],
+        v["p_down"],
+    )
+    if early:
+
+        def feed_shard(z_index, y_index):
+            lane = aligned((z_index * 2 + y_index) * unit_tile, unit_tile)
+            feed_back(lane, wdown[z_index, y_index])
+
+        for step in range(3, nz):
+            g_down.z_step(step)
+        for copy in cot_copies:
+            copy.wait_recv()
+        weight_grad(blocks(active), cot_all, grad_down)
+        r_down.core_send(0)
+        r_down.core_send(1)
+        for reach in range(nz - 1):
+            g_down.y_step(reach)
+        for reach in range(nz):
+            g_down.c_wait(reach, 0)
+        loop(nz, lambda z_index: feed_shard(z_index, y))
+        g_down.y_step(nz - 1)
+        r_down.core_add(0)
+        r_down.core_add(1)
+        for reach in range(nz):
+            g_down.c_wait(reach, 1)
+        loop(nz, lambda z_index: feed_shard(z_index, 1 - y))
+    else:
+        for step in range(3, nz):
+            g_down.z_step(step)
+        for copy in cot_copies:
+            copy.wait_recv()
+        g_down.y_steps()
+        g_down.finish()
+        per = unit_tile // (2 * shard_rows)
+
+        def feed_tile(u):
+            weight = wdown[pl.ds(u * per, per)].reshape(unit_tile, width)
+            feed_back(aligned(u * unit_tile, unit_tile), weight)
+
+        loop(units // unit_tile, feed_tile)
+
+    each_group(lambda step: send_part(step, ghid.at[place.g_at(step)], wup, second_first))
+    back_product(ghid.at[g], wup, store_into(gmid, F32))
+
+    def down_tile(left, target, n):
+        lane = aligned(n * tile, tile)
+        target(lane, dot(left[...], wdown[:, :, :, lane].reshape(units, tile)))
 
     g_up.drain()
     g_down.drain()
-    weight_grad(second, ghid, wup, 0)
+    weight_grad(blocks(second), ghid, wup)
     r_up = Reduce(
         place, wires, wup, h_up, False, v["c_up"], None, v["y_up"], v["z_up"], v["p_up"]
     )
@@ -902,28 +1100,26 @@
     for copy in second_copies:
         copy.wait_send()
 
-    def other_down(step, carry):
+    def other_down(step):
         block = place.g_at(step)
 
         def keep(lane, value):
             second[block, :, lane] = value.astype(LOW)
 
         loop(width // tile, lambda n: down_tile(active.at[block], keep, n))
-        return carry
-
-    lax.fori_loop(1, groups, other_down, 0)
+
+    each_group(other_down)
+    r_up.core_add(0)
+    r_up.core_add(1)
 
     def own_down(lane, value):
-        outp[:, lane] = value + vecs[5:6, lane]
+        second[g, :, lane] = value.astype(LOW)
 
     loop(width // tile, lambda n: down_tile(active.at[g], own_down, n))
-    weight_grad(active, cot_all, wdown, 0)
-    c_down = v["c_skip"] if v["c_skip"].shape == v["wdown"].shape[:2] + (h_down, width) else v["c_down"]
-    r_down = Reduce(
-        place, wires, wdown, h_down, False, c_down, None, v["y_down"], v["z_down"], v["p_down"]
-    )
-    r_down.core_send(0)
-    r_down.core_send(1)
+    if not early:
+        weight_grad(blocks(active), cot_all, wdown)
+        r_down.core_send(0)
+        r_down.core_send(1)
     sums = v["sums"]
     sums[...] = jnp.zeros_like(sums)
 
@@ -945,8 +1141,9 @@
     else:
         sums[6:7, 0:units] = ghid_sum
     sums[5:6] = column_sums(lambda i: cot_all[g, aligned(i * chunk, chunk)], per_block, width)
-    r_up.core_add(0)
-    r_up.core_add(1)
+    if not early:
+        r_down.core_add(0)
+        r_down.core_add(1)
 
     for step in range(1, groups):
         part_copy(step, second_first).wait_recv()
@@ -1000,10 +1197,8 @@
         )
         for step in range(1, groups)
     ]
-    r_down.core_add(0)
-    r_down.core_add(1)
     g_out.drain()
-    weight_grad(att_own, gb, wout, 0)
+    weight_grad([att_own], gb, wout)
     r_out = Reduce(
         place, wires, wout, h_out, True, v["c_out"], v["x_out"], v["y_out"], v["z_out"], v["p_out"]
     )
@@ -1012,15 +1207,18 @@
 
     gm = v["gm"]
 
-    dkv = v["dkv"]
+    def dkv_lanes(core, start, size):
+        return aligned(core * 2 * cols + start, size)
+
     gat, gqt, skt = vt.at[0, 0], vt.at[0, 1], vt.at[1, 0]
 
-    def back_attend(block, first):
+    def back_attend(block, first, between):
         gat[...] = ga_in[block].T
 
         def body(pair):
             lanes = aligned(pair * pair_width, pair_width)
             later = aligned(cols + pair * pair_width, pair_width)
+            starts = pair * pair_width, cols + pair * pair_width
             fixed, scores = [], []
             for half in range(2):
                 head = pair * 2 + half
@@ -1053,10 +1251,11 @@
                     value_grad = value_grad + dot(terms.astype(LOW), scaled_nat)
                     key_grad = key_grad + dot(grad_low, queries_nat)
                     done.append((shift_sum, query_grad + dot(kt[core, b, lanes], grad_low)))
-                for at, found in ((lanes, key_grad), (later, value_grad)):
+                for start, found in zip(starts, (key_grad, value_grad)):
+                    at = dkv_lanes(core, start, pair_width)
                     if not first:
-                        found = found + dkv[core, b, :, at].astype(F32)
-                    dkv[core, b, :, at] = found.astype(LOW)
+                        found = found + active[b, :, at].astype(F32)
+                    active[b, :, at] = found.astype(LOW)
                 return tuple(done)
 
             start = (jnp.zeros((1, rows), F32), jnp.zeros((pair_width, rows), F32))
@@ -1069,93 +1268,97 @@
                 gqt[at] = (0.125 * (own + shift_sum * own_keys)).astype(LOW)
                 skt[at] = (shift_sum * qt[block, at].astype(F32)).astype(LOW)
 
-        loop(heads // 2, body)
+        middle_pair = heads // 4
+        loop_from(0, middle_pair, body)
+        between()
+        loop_from(middle_pair, heads // 2, body)
         gm[block, :, 0:cols] = gqt[...].T
-        dkv[c, block, :, 0:cols] = dkv[c, block, :, 0:cols] + skt[...].T
+        at = dkv_lanes(c, 0, cols)
+        active[block, :, at] = active[block, :, at] + skt[...].T
 
     dkv_wire = wires.take(1)
 
     def dkv_copy():
         return wires.copy(
-            lambda: (dkv.at[1 - c], gm.at[:, :, cols : 3 * cols], place.c_peer()), dkv_wire
+            lambda: (
+                active.at[:, :, dkv_lanes(1 - c, 0, 2 * cols)],
+                gm.at[:, :, cols : 3 * cols],
+                place.c_peer(),
+            ),
+            dkv_wire,
         )
 
-    def back_attention():
-        fill_far(g)
-        back_attend(g, True)
+    def out_steps():
         r_out.core_add(0)
         r_out.core_add(1)
-        r_up.y_add()
-        for step in range(1, groups):
-            ga_copy(step).wait_recv()
-        for copy in cot_copies:
-            copy.wait_send()
-        for copy in out_copies:
-            copy.start()
-
-        def other(step, carry):
-            block = place.g_at(-step)
-            fill_far(block)
-            back_attend(block, False)
-            return carry
-
-        lax.fori_loop(1, groups, other, 0)
-
-        dkv_copy().start()
-        r_up.z_add()
-        r_down.y_add()
+
+    def out_x_steps():
         r_out.x_add(0)
         r_out.x_add(1)
-        dkv_copy().wait_recv()
-
-        def merge(b):
-            gm[b, :, cols : 3 * cols] = gm[b, :, cols : 3 * cols] + dkv[c, b]
-
-        loop(groups, merge)
-
-    back_attention()
+
+    up_tasks, down_tasks = r_up.y_tasks(), r_down.y_tasks()
+    tasks += down_tasks[0:2] + [out_steps] + down_tasks[2:]
+    fill_far(g)
+    work(2)
+    back_attend(g, True, lambda: work(2))
+    work(2)
+    for step in range(1, groups):
+        ga_copy(step).wait_recv()
+    for copy in cot_copies:
+        copy.wait_send()
+    for copy in out_copies:
+        copy.start()
+    tasks += up_tasks[0:1] + [out_x_steps, r_down.z_add] + up_tasks[1:3]
+
+    def other_attend(step):
+        block = place.g_at(-step)
+        fill_far(block)
+        back_attend(block, False, (lambda: work(1)) if groups == 2 else (lambda: None))
+
+    each_group(other_attend)
+    if groups > 2:
+        work()
+    r_down.y_sent()
+    dkv_copy().start()
+    work()
+    dkv_copy().wait_recv()
+
+    def merge(b):
+        gm[b, :, cols : 3 * cols] = gm[b, :, cols : 3 * cols] + active[b, :, dkv_lanes(c, 0, 2 * cols)]
+
+    loop(groups, merge)
 
     parts_sent(second_first)
     mix_first = wires.take(groups)
 
-    def other_mix(step, carry):
-        block = place.g_at(step)
-        send_part(step, gm.at[block], wqkv, mix_first)
-        return carry
-
-    lax.fori_loop(1, groups, other_mix, 0)
-    for copy in out_copies:
-        copy.wait_recv()
-    ob = second.at[g]
-
-    def out_rows(i):
-        at = aligned(i * chunk, chunk)
-        value = middle[at] + outp[at]
-        for step in range(1, groups):
-            value = value + cot_all[place.g_at(-step), at].astype(F32)
-        ob[at] = value.astype(LOW)
-
-    loop(rows // chunk, out_rows)
-    stores = [pltpu.make_async_copy(ob, v["o_out"].at[0], local.at[0])]
-    stores[0].start()
-    back_product(gm.at[g], wqkv, store_into(middle, F32))
+    each_group(lambda step: send_part(step, gm.at[place.g_at(step)], wqkv, mix_first))
+    own_parts = [far.at[i // groups, i % groups] for i in range(width // rows)]
+
+    count, per, size = row_chunks(wqkv)
+    for j in range(count):
+        value = dot_nt(gm[g], wqkv[j * per : (j + 1) * per].reshape(size, 3 * cols))
+        for i in range(size // rows):
+            own_parts[j * (size // rows) + i][...] = value[:, i * rows : (i + 1) * rows]
     g_qkv.drain()
-    weight_grad(normed, gm, wqkv, 0)
+    weight_grad(blocks(normed), gm, wqkv)
     c_qkv = v["c_up"].at[:, :, :, 0 : 3 * cols]
     r_qkv = Reduce(
         place, wires, wqkv, h_qkv, False, c_qkv, None, v["y_qkv"], v["z_qkv"], v["p_qkv"]
     )
+    tasks += up_tasks[3:]
+    work()
+    r_up.y_sent()
+    pl.semaphore_signal(v["free_sem"], inc=1, device_id=place.c_peer(), device_id_type=MESH)
+    pl.semaphore_wait(v["free_sem"], 1)
     r_qkv.core_send(0)
     r_qkv.core_send(1)
-    r_down.z_add()
-    r_out.y_add()
     r_qkv.core_add(0)
     r_qkv.core_add(1)
     for step in range(1, groups):
         part_copy(step, mix_first).wait_recv()
 
     def first_in(at):
-        t = middle[at]
+        t = jnp.concatenate([part[at] for part in own_parts], axis=1)
         for step in range(1, groups):
             t = t + p_recv[step - 1, at].astype(F32)
         return t
@@ -1175,76 +1378,101 @@
         copy.start()
         return copy
 
-    sum_core = sum_swap(0, place.c_peer())
-
-    gj = cot_all
+    stores = []
+    gj = normed
 
     def joined_back():
-        _, _, size = row_chunks(ws)
+        count, per, size = row_chunks(ws)
         span = width // size
-
-        def store(lane_index, value):
-            gj[lax.div(lane_index, span), :, aligned(lax.rem(lane_index, span) * size, size)] = value
-
-        count, per, size = row_chunks(ws)
 
         def body(j):
             value = dot_nt(gb[...], ws[pl.ds(j * per, per)].reshape(size, width))
-            store(j, value.astype(LOW))
+            at = aligned(lax.rem(j, span) * size, size)
+            gj[lax.div(j, span), :, at] = value.astype(LOW)
 
         loop(count, body)
         for half, name in enumerate(("o_frames", "o_skip")):
             stores.append(pltpu.make_async_copy(gj.at[half], v[name].at[0], local.at[1 + half]))
             stores[-1].start()
 
+    merged_copies = []
+    if sizes.pair:
+        gmx = v["gmx"]
+        merged_swap = Exchange(place, wires)
+        other_cols = aligned((1 - g) * cols, cols)
+        merged_copies = [
+            merged_swap.copy(1, lambda: gb.at[:, other_cols], lambda: gmx.at[1])
+        ]
+        merged_copies[0].start()
+        gmx[0] = gb[:, own_cols]
+    sum_core = sum_swap(0, place.c_peer())
     if lend:
         parts_sent(mix_first)
-        for store in stores:
-            store.wait()
-        stores.clear()
         for load in input_loads():
             load.start()
         for load in input_loads():
             load.wait()
-    apart = ws.shape == wdown.shape
-    grad_skip = wdown if apart else ws
     g_skip.drain()
-    r_up.drain()
-    r_down.drain()
-    if not apart:
-        joined_back()
-    weight_grad(fr_v, gb, grad_skip, 0)
-    weight_grad(sk_v, gb, grad_skip, nz // 2)
+    for copy in normed_copies:
+        copy.wait_send()
+    joined_back()
+    for copy in out_copies:
+        copy.wait_recv()
+    ob = second.at[g]
+
+    def out_rows(i):
+        at = aligned(i * chunk, chunk)
+        value = middle[at] + second[g, at].astype(F32) + vecs[5:6]
+        for step in range(1, groups):
+            value = value + cot_all[place.g_at(-step), at].astype(F32)
+        ob[at] = value.astype(LOW)
+
+    loop(rows // chunk, out_rows)
+    stores.append(pltpu.make_async_copy(ob, v["o_out"].at[0], local.at[0]))
+    stores[-1].start()
+    r_down.core_sent()
+    tasks += r_out.y_tasks()
+    sum_core.wait()
+    sums[...] = sums[...] + sum_in[0]
+    sum_x = [sum_swap(step, place.x_peer(step)) for step in range(1, groups)]
+    work()
+    qkv_tasks = r_qkv.y_tasks()
+    if sizes.pair:
+        for copy in joined_copies + merged_copies:
+            copy.wait()
+        grad_skip, c_skip = wdown.at[:, :, :, 0:cols], v["c_down"].at[:, :, :, 0:cols]
+        for half in range(2):
+            lefts = [v["io"].at[half], v["joined"].at[half]]
+            weight_grad(lefts, gmx, grad_skip, half * (nz // 2))
+    else:
+        grad_skip, c_skip = ws, v["c_skip"]
+        weight_grad([fr_v], gb, grad_skip)
+        weight_grad([sk_v], gb, grad_skip, nz // 2)
     r_skip = Reduce(
-        place, wires, grad_skip, h_skip, True, v["c_skip"], v["x_skip"], v["y_skip"], v["z_skip"],
-        v["p_skip"],
+        place, wires, grad_skip, h_skip, not sizes.pair, c_skip, v["x_skip"], v["y_skip"],
+        v["z_skip"], v["p_skip"],
     )
     r_skip.core_send(0)
     r_skip.core_send(1)
-    if apart:
-        joined_back()
-    r_skip.core_add(0)
-    r_skip.core_add(1)
-    r_qkv.y_add()
-    sum_core.wait()
-    sums[...] = sums[...] + sum_in[0]
-    sum_x = [sum_swap(step, place.x_peer(step)) for step in range(1, groups)]
-    r_out.z_add()
-    r_up.spread_on()
-    r_down.spread_on()
     for copy in sum_x:
         copy.wait()
     for step in range(1, groups):
         sums[0:6] = sums[0:6] + sum_in[step, 0:6]
     sum_y = sum_swap(groups, place.y_peer())
-    r_qkv.z_add()
-    r_skip.x_add(0)
+    r_skip.core_add(0)
+    r_skip.core_add(1)
+    if not sizes.pair:
+        r_skip.x_add(0)
+        r_skip.x_add(1)
+    tasks += [r_down.spread_on, r_up.z_add, r_out.z_add]
+    tasks += qkv_tasks + [r_up.spread_on]
+    work()
     sum_y.wait()
     sums[...] = sums[...] + sum_in[groups]
     sum_z = [sum_swap(groups + step, place.z_peer(step)) for step in range(1, nz)]
-    r_out.spread_on()
-    r_skip.x_add(1)
-    r_qkv.spread_on()
+    skip_tasks = r_skip.y_tasks()
+    tasks += [skip_tasks[0], r_out.spread_on] + skip_tasks[1:] + [r_qkv.z_add]
+    work()
     for copy in sum_z:
         copy.wait()
     for step in range(1, nz):
@@ -1256,19 +1484,18 @@
     up_copies = [up_swap.copy(step, lambda: o_up.at[g], lambda: o_up.at[g]) for step in range(1, groups)]
     for copy in up_copies:
         copy.start()
-    r_skip.y_add()
     r_skip.z_add()
+    r_qkv.spread_on()
     r_skip.spread_on()
 
     for copy in up_copies:
         copy.wait()
     for reduced in (r_up, r_down, r_out, r_qkv, r_skip):
         reduced.finish()
-    for reduced in (r_out, r_qkv, r_skip):
         reduced.drain()
-    for gathered in (g_small, g_out):
+    for gathered in [g_small] + skips[1:]:
         gathered.drain()
-    for copy in seg_copies + [seg_core] + normed_copies + kv_waits:
+    for copy in seg_copies + [seg_core] + kv_waits:
         copy.wait_send()
     for copy in out_copies:
         copy.wait_send()
@@ -1279,6 +1506,73 @@
     dkv_copy().wait_send()
     for store in stores:
         store.wait()
+
+
+def finish(sizes, *refs):
+    wholes, pieces, small, up = refs[0:3], refs[3:8], refs[8], refs[9]
+    whole_outs, outs, vectors, up_out = refs[10:13], refs[13:18], refs[18:24], refs[24]
+    held, made, passed, sems = refs[25:30], refs[30:35], refs[35], refs[36]
+    groups, cols, width = sizes.groups, sizes.cols, sizes.width
+    copies = [
+        pltpu.make_async_copy(pieces[i], held[i], sems.at[i]) for i in range(5)
+    ]
+    moves = [
+        pltpu.make_async_copy(wholes[i].at[0], passed.at[i], sems.at[5 + i]) for i in range(3)
+    ]
+    for copy in moves + copies:
+        copy.start()
+    stores = []
+    for i in range(3):
+        moves[i].wait()
+        stores.append(pltpu.make_async_copy(passed.at[i], whole_outs[i].at[0], sems.at[13 + i]))
+        stores[-1].start()
+    for i in range(5):
+        copies[i].wait()
+        half = held[i].shape[2]
+        for group in range(groups):
+            for core in range(2):
+                rows = slice(core * half, (core + 1) * half)
+                if i == 4:
+                    top = (group * 2 + core) * half
+                    made[i][top : top + half] = held[i][group, core].astype(F32)
+                elif i == 3 and sizes.direct:
+                    for s in range(sizes.n_dp):
+                        at = (s * groups + group) * sizes.part
+                        made[i][rows, at : at + sizes.part] = held[i][
+                            group, core, :, s * sizes.part : (s + 1) * sizes.part
+                        ].astype(F32)
+                elif i == 3:
+                    made[i][rows, group * sizes.units : (group + 1) * sizes.units] = held[i][
+                        group, core
+                    ].astype(F32)
+                else:
+                    for third in range(held[i].shape[3] // cols):
+                        at = third * width + group * cols
+                        made[i][rows, at : at + cols] = held[i][
+                            group, core, :, third * cols : (third + 1) * cols
+                        ].astype(F32)
+        stores.append(pltpu.make_async_copy(made[i], outs[i], sems.at[8 + i]))
+        stores[-1].start()
+    dp = lax.axis_index("dp")
+    if sizes.shard % 128 == 0 and sizes.direct:
+        own = aligned(dp * sizes.shard, sizes.shard)
+        for row in range(6):
+            vectors[row][...] = small[row : row + 1, own]
+        per_row = width // sizes.part
+        at = aligned(lax.rem(dp, per_row) * sizes.part, sizes.part)
+        for group in range(groups):
+            up_out[:, group * sizes.part : (group + 1) * sizes.part] = up[
+                group, pl.ds(6 + lax.div(dp, per_row), 1), at
+            ]
+    else:
+        for row in range(6):
+            vectors[row][...] = small[row : row + 1]
+        for group in range(groups):
+            up_out[:, group * sizes.units : (group + 1) * sizes.units] = up[
+                group, 6:7, 0 : sizes.units
+            ]
+    for copy in stores:
+        copy.wait()
 
 
 def per_device(sizes, *args):
@@ -1307,7 +1601,7 @@
     def full(*shape):
         return pltpu.VMEM(shape, F32)
 
-    same = (r_skip, width) == (r_down, width)
+    sizes.pair = groups == 2 and r_skip == r_down
     scratch = [
         low(2, rows, width), low(groups, rows, width),
         low(nz, 2, r_skip, width), low(nz, 2, depth, 3 * cols), low(nz, 2, depth, width),
@@ -1325,24 +1619,28 @@
         low(groups - 1, rows, width),
         low(rows, width), low(groups, rows, cols),
         low(groups, rows, 3 * cols),
-        low(2, groups, rows, 2 * cols),
         full(2, groups, rows, rows), low(2, groups, cols, rows),
-        low(nz, 2, r_skip // 2, width), low(nz, 2, depth // 2, width),
+        low(1, 16, 128) if sizes.pair else low(nz, 2, r_skip // 2, width),
+        low(nz, 2, depth // 2, width),
         low(nz, 2, depth // 2, units),
-        low(1, 1, 16, 128) if same else low(nz, 2, r_down // 2, width),
-        low(groups - 1, nz, 2, r_skip // 2, cols), low(groups - 1, nz, 2, depth // 2, cols),
+        low(nz, 2, r_down // 2, width),
+        low(1, 16, 128) if sizes.pair else low(groups - 1, nz, 2, r_skip // 2, cols),
+        low(groups - 1, nz, 2, depth // 2, cols),
         low(nz, r_skip // 2, cols), low(nz, depth // 2, 3 * cols), low(nz, depth // 2, cols),
         low(nz, depth // 2, units), low(nz, r_down // 2, width),
         low(nz - 1, r_skip // 2, cols), low(nz - 1, depth // 2, 3 * cols),
         low(nz - 1, depth // 2, cols), low(nz - 1, depth // 2, units),
         low(nz - 1, r_down // 2, width),
+        low(2, rows, width) if sizes.pair else low(1, 16, 128),
+        low(groups, rows, cols) if sizes.pair else low(1, 16, 128),
+        low(nz, 2, r_down, width) if 2 * r_down == 512 else low(1, 16, 128),
         full(8, width), full(groups + nz, 8, width),
-        low(512 if groups * rows <= 512 else 256, groups * rows), full(rows, width),
+        low(512 if groups * rows <= 512 else 256, groups * rows),
     ]
-    wires = 200 if groups * n_dp <= 16 else 1200
+    wires = 320 if groups * n_dp <= 16 else 1400
     scratch += [pltpu.SemaphoreType.DMA((wires,)), pltpu.SemaphoreType.DMA((wires,))]
-    scratch += [pltpu.SemaphoreType.DMA((16,))]
-    hbm, vmem = pl.BlockSpec(memory_space=pl.ANY), pl.BlockSpec(memory_space=pltpu.VMEM)
+    scratch += [pltpu.SemaphoreType.DMA((16,)), pltpu.SemaphoreType.REGULAR]
+    hbm, vmem = pl.BlockSpec(memory_space=pltpu.HBM), pl.BlockSpec(memory_space=pltpu.VMEM)
     whole = jax.ShapeDtypeStruct((1, rows, width), LOW)
 
     def piece(*shape):
@@ -1368,21 +1666,35 @@
         *[vector.reshape(1, -1) for vector in vectors],
         w_skip, w_qkv, w_out, w_up, w_down,
     )
-    output, grad_frames, grad_skip, p_skip, p_qkv, p_out, p_up, p_down, small, up = found
-
-    def joined(pieces, inner):
-        half = pieces.shape[2]
-        split = pieces.reshape(groups, 2, half, inner, -1).transpose(1, 2, 3, 0, 4)
-        return split.reshape(2 * half, -1).astype(F32)
-
-    own = lax.dynamic_slice_in_dim(small, lax.axis_index("dp") * shard, shard, 1)
-    flat = up[:, 6 : 6 + sizes.up_rows].reshape(groups, -1)
-    own_up = lax.dynamic_slice_in_dim(flat, lax.axis_index("dp") * part, part, 1).reshape(-1)
+    easy = shard % 128 == 0 and sizes.direct
+    line = jax.ShapeDtypeStruct((1, shard if easy else width), F32)
+    shapes = [w_skip.shape, w_qkv.shape, w_out.shape, w_up.shape, w_down.shape]
+    done = pl.pallas_call(
+        functools.partial(finish, sizes),
+        out_shape=(whole,) * 3
+        + tuple(jax.ShapeDtypeStruct(shape, F32) for shape in shapes)
+        + (line,) * 6
+        + (jax.ShapeDtypeStruct((1, groups * (part if easy else units)), F32),),
+        in_specs=[hbm] * 8 + [vmem] * 2,
+        out_specs=[hbm] * 8 + [vmem] * 7,
+        scratch_shapes=[pltpu.VMEM(value.shape, LOW) for value in found[3:8]]
+        + [pltpu.VMEM(shape, F32) for shape in shapes]
+        + [low(3, rows, width), pltpu.SemaphoreType.DMA((16,))],
+        compiler_params=pltpu.CompilerParams(vmem_limit_bytes=60 * 2**20),
+    )(*found)
+    output, grad_frames, grad_skip, g_skip, g_qkv, g_out, g_up, g_down = done[0:8]
+    lines = [value.reshape(-1) for value in done[8:15]]
+    if not easy:
+        at = lax.axis_index("dp")
+        lines[0:6] = [lax.dynamic_slice_in_dim(value, at * shard, shard) for value in lines[0:6]]
+        by_group = lines[6].reshape(groups, units)
+        lines[6] = lax.dynamic_slice_in_dim(by_group, at * part, part, 1).reshape(-1)
+    if not sizes.direct:
+        g_up = g_up.reshape(depth, groups, n_dp, part).transpose(0, 2, 1, 3).reshape(depth, -1)
+    g_b_skip, g_gain_a, g_bias_a, g_gain_f, g_bias_f, g_b_down, g_b_up = lines
     return (
-        output, grad_frames, grad_skip,
-        joined(p_skip, 1), own[0], own[1], own[2], joined(p_qkv, 3), joined(p_out, 1),
-        own[3], own[4], joined(p_up, n_dp), own_up,
-        p_down.reshape(-1, width).astype(F32), own[5],
+        output, grad_frames, grad_skip, g_skip, g_b_skip, g_gain_a, g_bias_a, g_qkv, g_out,
+        g_gain_f, g_bias_f, g_up, g_b_up, g_down, g_b_down,
     )
 
 

time: 315 us -> 256 us (0.81)
  Pallas kernels: 289 us -> 252 us
  local copies, waits for them, and re-layouts: 21.3 us -> 0 us
    pallas_call x1, Pallas kernels: 289 us -> 246 us  [per_device(): pl.pallas_call(functools.partial(kernel, sizes), out_shape=(whole, whole,...]
    convert_element_type x7 -> x0, local copies, waits for them, and re-layouts: 12.7 us -> none  [joined(): return split.reshape(2 * half, -1).astype(F32)]
    unnamed x24 -> x0, local copies, waits for them, and re-layouts: 7.36 us -> none
    pallas_call x0 -> x1, Pallas kernels: none -> 6.83 us  [per_device(): pl.pallas_call(functools.partial(finish, sizes), out_shape=(whole,) * 3 +...]
where the time goes in v2:
time: 256 us; the launch traced here: 253 us
  Pallas kernels  252 us (98%)
    pallas_call x1, Pallas kernels, per_device(): pl.pallas_call(functools.partial(kernel, sizes), out_shape=(whole, whole,...  246 us
    pallas_call x1, Pallas kernels, per_device(): pl.pallas_call(functools.partial(finish, sizes), out_shape=(whole,) * 3 +...  6.83 us

profile of v2, /device:TPU:0, one launch (start us, length us, event | category | flops | bytes accessed | tf_op | source)
XLA Modules:
  0.0 253.2 jit_solution(3474830355839555043)
XLA Ops:
  0.7 245.5 %shard_map.271 = (bf16[1,256,1024]{2,1,0:T(8,128)(2,1)}, bf16[1,256,1024]{2,1,0:T(8,128)(2,1)}, bf16[1,256,1024]{2,1,0:T(8,128)(2,1)}, bf16[2,2,128,512]{3,2,1,0...) custom-call(bf16[1,256,1024]{2,1,0:T(8,128)(2,1)} %refs_0_.1, ...), custom_call_target="tpu_custom_call" | custom-call | tf_op jit(solution)/shard_map/pallas_call | solution.py:1650
  246.2 6.8 %shard_map.272 = (bf16[1,256,1024]{2,1,0:T(8,128)(2,1)}, bf16[1,256,1024]{2,1,0:T(8,128)(2,1)}, bf16[1,256,1024]{2,1,0:T(8,128)(2,1)}, f32[256,1024]{1,0:T(8,128...) custom-call(bf16[1,256,1024]{2,1,0:T(8,128)(2,1)} %get-tuple-element, ...), custom_call_target="tpu_custom_call" | custom-call | tf_op jit(solution)/shard_map/pallas_call | solution.py:1672

commit v3 on v2

--- a/solution.py
+++ b/solution.py
@@ -24,12 +24,12 @@
     return lax.dot_general(left, right, (((1,), (1,)), ((), ())), preferred_element_type=F32)
 
 
-def loop(count, body):
+def loop(count, body, unroll=1):
     def visit(index, carry):
         body(index)
         return carry
 
-    lax.fori_loop(0, count, visit, 0)
+    lax.fori_loop(0, count, visit, 0, unroll=min(unroll, count))
 
 
 def loop_from(first, last, body):
@@ -456,6 +456,33 @@
     return centred * scale, scale
 
 
+ORDER = (
+    "skip_own", "small_start", "small_own", "out_own", "qkv_own", "skip_start", "rest_start",
+    "small_z1", "seg_start", "cot_share", "qkv_start", "rest_own", "qkv_y0", "skip_z1", "skip_y0",
+    "rest_z1", "seg_pass", "out_start", "skip_z2", "skip_x0", "rest_z2", "skip_y1", "small_z2",
+    "skip_z3", "qkv_z1", "rest_y0", "skip_y2", "skip_x1", "skip_x2", "small_z3", "rest_z3",
+    "skip_y3", "skip_w0", "qkv_z2", "out_y0", "rest_y1", "out_z1", "skip_w1", "skip_w2",
+    "joined_0", "joined_1", "rest_a", "skip_x3", "small_y0", "out_x0", "small_y1", "rest_y2",
+    "small_y2", "qkv_z3", "rest_y3", "skip_w3", "skip_a", "out_z2", "rest_b", "small_y3", "qkv_a",
+    "up_start", "vectors", "skip_b", "out_x1", "merge", "norm_first", "up_z1", "out_y1", "out_x2",
+    "qkv_y1", "qkv_y2", "qkv_y3", "qkv_b", "seg_turn", "up_own", "down_start", "out_w0", "out_z3",
+    "mix_own", "up_z2", "down_own", "mix_others", "turn_keys", "out_y2", "att_other_a", "out_y3",
+    "out_w1", "att_other_b", "att_own_a", "out_w2", "out_w3", "att_own_b", "up_z3", "down_z1",
+    "out_b", "out_x3", "joined_2", "out_a", "mid", "up_y0", "up_y1", "down_z2", "up_y2", "down_y0",
+    "down_z3", "joined_3", "joined_4", "joined_5", "up_a", "down_a", "up_y3", "joined_6",
+    "joined_7", "up_b", "feed_own", "feed_others", "grad_d", "down_y1", "rd_c0", "feed_a",
+    "down_y2", "down_y3", "rd_c1", "down_b", "feed_b", "part_send", "rd_y1", "part_own", "grad_u",
+    "rd_y2", "out_parts", "rd_y3", "ru_c0", "norm_second", "branch", "grad_o", "back_own_a",
+    "ro_c0", "ru_c1", "back_own_b", "ru_y1", "ga_wait", "back_other_a", "ro_c1", "back_other_b",
+    "rd_y0", "ru_y2", "ro_x0", "sums_early", "merge_keys", "mix_send", "mix_back", "rd_z", "ro_x1",
+    "ru_y3", "grad_q", "ru_y0", "up_free", "qkv_send", "ro_y1", "rq_c0", "ro_y2", "ro_y3", "rq_c1",
+    "norm_merged", "merged_send", "ru_z", "rq_y1", "rq_y2", "sum_0", "sum_1", "grad_s", "rs_c0",
+    "ro_y0", "ro_z", "out_send", "rs_c1", "rq_y3", "rs_y1", "rs_y2", "rq_y0", "rq_z", "sum_2",
+    "rs_y3", "rs_y0", "ru_f", "output", "rd_f", "sum_3", "rs_z", "rq_f", "inputs_back", "sum_4",
+    "ro_f", "rs_f",
+)
+
+
 def kernel(sizes, *refs):
     names = (
         "frames", "skip", "cot", "seg", "b_skip", "gain_a", "bias_a", "gain_f", "bias_f",
@@ -465,8 +492,9 @@
         "merged", "middle", "gmid", "normed", "second", "kv", "qt", "kt", "shift", "attt", "tot",
         "att_own", "att_send", "active", "ghid", "p_send", "p_recv", "gb", "ga_in", "gm",
         "far", "vt", "c_skip", "c_out", "c_up", "c_down", "x_skip", "x_out", "y_skip", "y_qkv",
-        "y_out", "y_up", "y_down", "z_skip", "z_qkv", "z_out", "z_up", "z_down", "joined", "gmx", "grad_down", "sums",
-        "sum_in", "turned", "send_sems", "recv_sems", "local_sems", "free_sem",
+        "y_out", "y_up", "y_down", "z_skip", "z_qkv", "z_out", "z_up", "z_down", "joined", "gmx",
+        "grad_down", "sums", "sum_in", "turned", "send_sems", "recv_sems", "local_sems",
+        "free_sem",
     )
     assert len(names) == len(refs), (len(names), len(refs))
     v = dict(zip(names, refs))
@@ -483,13 +511,6 @@
             body(1)
         else:
             loop_from(1, groups, body)
-
-    tasks = []
-
-    def work(count=None):
-        for task in tasks[:count]:
-            task()
-        del tasks[:count]
 
     barrier = pltpu.get_barrier_semaphore()
     partners = [place.z_peer(step) for step in range(1, nz)] + [place.y_peer()]
@@ -593,103 +614,133 @@
 
     pl.semaphore_wait(barrier, len(partners))
 
+    for load in loads:
+        load.wait()
+    steps = {}
+
+    def step(function):
+        steps[function.__name__] = function
+        return function
+
+    def none():
+        pass
+
+    last_reach = 3
+
+    def reaches(reach):
+        return range(reach, nz) if reach == last_reach else (reach,)
+
+    def gather_steps(name, gather):
+        many = {
+            "z": [gather.z_step, range(1, last_reach + 1)],
+            "y": [gather.y_step, range(last_reach + 1)],
+        }
+        if gather.spread:
+            many["x"] = [lambda reach: gather.x_step(reach, 0), range(last_reach + 1)]
+            many["w"] = [lambda reach: gather.x_step(reach, 1), range(last_reach + 1)]
+        steps[name + "_start"], steps[name + "_own"] = gather.start, gather.own
+
+        def run(method, reach):
+            for one in reaches(reach):
+                method(one)
+
+        for letter, (method, which) in many.items():
+            for reach in which:
+                steps[f"{name}_{letter}{reach}"] = functools.partial(run, method, reach)
+        if not gather.whole_core:
+            steps[name + "_a"] = lambda: [gather.c_wait(reach, 0) for reach in range(nz)]
+            steps[name + "_b"] = lambda: [gather.c_wait(reach, 1) for reach in range(nz)]
+
     g_small = Gather(place, wires, small, 0, whole_core=True)
     g_skip = Gather(place, wires, v["ws"], h_skip, spread=share)
-    g_rest = Gather(place, wires, v["ws"], h_skip, span=(shared, width))
     g_qkv = Gather(place, wires, v["wqkv"], h_qkv)
     g_out = Gather(place, wires, v["wout"], h_out, spread=cols)
     g_up = Gather(place, wires, v["wup"], h_up)
     g_down = Gather(place, wires, v["wdown"], h_down)
-    skips = [g_skip, g_rest] if shared < width else [g_skip]
+    gather_steps("small", g_small)
+    gather_steps("skip", g_skip)
+    gather_steps("qkv", g_qkv)
+    gather_steps("out", g_out)
+    gather_steps("up", g_up)
+    gather_steps("down", g_down)
+    gathers = [g_small, g_skip, g_qkv, g_out, g_up, g_down]
+    if shared < width:
+        g_rest = Gather(place, wires, v["ws"], h_skip, span=(shared, width))
+        gather_steps("rest", g_rest)
+        gathers.append(g_rest)
+    else:
+        for name in ("start", "own", "z1", "z2", "z3", "y0", "y1", "y2", "y3", "a", "b"):
+            steps["rest_" + name] = none
+
     seg_swap = Exchange(place, wires)
-    seg_copies = []
-    for step in range(1, groups):
-        seg_copies.append(seg_swap.copy(step, lambda: segs.at[c, g], lambda: segs.at[c, g]))
-        seg_copies[-1].start()
-    for gather in [g_small] + skips:
-        gather.start()
-    for gather in skips + [g_small, g_qkv]:
-        gather.own()
-
-    joined_copies, joined_parts = [], []
-    if sizes.pair:
-        for load in loads:
-            load.wait()
-        lines = rows // 4
-        for part in range(8):
+    seg_copies = [
+        seg_swap.copy(step, lambda: segs.at[c, g], lambda: segs.at[c, g])
+        for step in range(1, groups)
+    ]
+    seg_core = wires.copy(lambda: (segs.at[c], segs.at[c], place.c_peer()))
+
+    @step
+    def seg_start():
+        for copy in seg_copies:
+            copy.start()
+
+    @step
+    def seg_pass():
+        for copy in seg_copies:
+            copy.wait_recv()
+        seg_core.start()
+
+    joined_copies = []
+    lines = rows // 4
+    for part in range(8):
+        if sizes.pair:
             at = part // 4, pl.ds(part % 4 * lines, lines)
             copy = Exchange(place, wires).copy(
                 1, lambda at=at: v["io"].at[at], lambda at=at: v["joined"].at[at]
             )
             joined_copies.append(copy)
-            joined_parts.append(copy)
-
-    def send_joined(count):
-        for copy in joined_parts[:count]:
-            copy.start()
-        del joined_parts[:count]
-
-    send_joined(1)
-    for reach in range(1, nz):
-        g_skip.z_step(reach)
-        if reach == nz - 1:
-            g_qkv.start()
-        if reach > 1:
-            g_skip.y_step(reach - 2)
-        g_skip.x_step(reach - 1, 0)
-        send_joined(1)
-    for copy in seg_copies:
-        copy.wait_recv()
-    seg_core = wires.copy(lambda: (segs.at[c], segs.at[c], place.c_peer()))
-    seg_core.start()
-    for gather in skips[1:] + [g_small]:
-        gather.z_steps()
-    g_skip.x_step(nz - 1, 0)
-    g_skip.y_step(nz - 2)
-    g_skip.y_step(nz - 1)
-    for reach in range(nz):
-        g_skip.x_step(reach, 1)
-        for gather in skips[1:] + [g_small]:
-            gather.y_step(reach)
-    g_up.own()
-
-    if not sizes.pair:
-        for load in loads:
-            load.wait()
-    vecs = v["vecs"]
-    for row in range(6):
-        vecs[row : row + 1] = jnp.concatenate(
-            [small[s // 2, s % 2, row : row + 1, 0 : sizes.shard] for s in range(n_dp)], axis=1
+            steps[f"joined_{part}"] = copy.start
+        else:
+            steps[f"joined_{part}"] = none
+
+    vecs, segc = v["vecs"], v["segc"]
+
+    @step
+    def vectors():
+        for row in range(6):
+            vecs[row : row + 1] = jnp.concatenate(
+                [small[s // 2, s % 2, row : row + 1, 0 : sizes.shard] for s in range(n_dp)], axis=1
+            )
+        v["bup"][...] = jnp.concatenate(
+            [small[s // 2, s % 2, 6:7, 0 : sizes.part] for s in range(n_dp)], axis=1
         )
-    v["bup"][...] = jnp.concatenate(
-        [small[s // 2, s % 2, 6:7, 0 : sizes.part] for s in range(n_dp)], axis=1
-    )
-    seg_core.wait_recv()
-    segc = v["segc"]
-    for core in range(2):
-
-        def turn(block, core=core):
-            turned_ids = jnp.broadcast_to(segs[core, block, 0:1], (128, rows)).T
-            segc[core, block] = turned_ids.astype(LOW)
-
-        loop(groups, turn)
-    g_out.start()
-    g_qkv.z_step(1)
-    for gather in skips:
-        gather.finish()
+
+    @step
+    def seg_turn():
+        seg_core.wait_recv()
+        for core in range(2):
+
+            def turn(block, core=core):
+                turned_ids = jnp.broadcast_to(segs[core, block, 0:1], (128, rows)).T
+                segc[core, block] = turned_ids.astype(LOW)
+
+            loop(groups, turn)
 
     tile = min(256, width)
-
-    def merge_tile(n):
-        lane = aligned(n * tile, tile)
-        merged[:, lane] = (
-            dot(fr_v[...], ws[0 : nz // 2, :, :, lane].reshape(width, tile))
-            + dot(sk_v[...], ws[nz // 2 : nz, :, :, lane].reshape(width, tile))
-            + vecs[0:1, lane]
-        )
-
-    loop(width // tile, merge_tile)
-    g_qkv.z_step(2)
+    normed, second, cot_all = v["normed"], v["second"], v["cot_all"]
+
+    @step
+    def merge():
+        def merge_tile(n):
+            lane = aligned(n * tile, tile)
+            merged[:, lane] = (
+                dot(fr_v[...], ws[0 : nz // 2, :, :, lane].reshape(width, tile))
+                + dot(sk_v[...], ws[nz // 2 : nz, :, :, lane].reshape(width, tile))
+                + vecs[0:1, lane]
+            )
+
+        loop(width // tile, merge_tile)
+
     chunk = 64
 
     def norm_into(held, gain_row, target):
@@ -722,20 +773,36 @@
         zero = jnp.zeros((1, width), F32)
         return lax.fori_loop(0, rows // chunk, body, (zero, zero))
 
-    normed, second, cot_all = v["normed"], v["second"], v["cot_all"]
-
-    def share(buffer):
+
+    def sharing(buffer):
         swap = Exchange(place, wires)
-        copies = [
+        return [
             swap.copy(step, lambda: buffer.at[g], lambda: buffer.at[g])
             for step in range(1, groups)
         ]
+
+    def start_all(copies):
         for copy in copies:
             copy.start()
-        return copies
-
-    norm_into(merged, 1, normed.at[g])
-    normed_copies = share(normed)
+
+    def wait_all(copies):
+        for copy in copies:
+            copy.wait_recv()
+
+    def sent_all(copies):
+        for copy in copies:
+            copy.wait_send()
+
+    normed_copies, second_copies, cot_copies = sharing(normed), sharing(second), sharing(cot_all)
+
+    @step
+    def norm_first():
+        norm_into(merged, 1, normed.at[g])
+        start_all(normed_copies)
+
+    @step
+    def cot_share():
+        start_all(cot_copies)
 
     kv, qt, kt = v["kv"], v["qt"], v["kt"]
     shift = v["shift"]
@@ -778,32 +845,16 @@
         for head in range(heads):
             shift[block, head] = found[head : head + 1] * 0.125
 
-    g_up.start()
-    for step in range(3, nz):
-        g_qkv.z_step(step)
-    g_out.own()
-    g_down.own()
-    for k in range(nz - 1):
-        g_qkv.y_step(k)
-    g_out.z_steps()
-    g_qkv.y_step(nz - 1)
-    g_qkv.finish()
-    g_down.start()
-    mix(g, 0)
-    for copy in normed_copies:
-        copy.wait_recv()
-
-    def mix_other(step):
-        mix(place.g_at(-step), step)
-
-    each_group(mix_other)
-    g_up.z_step(1)
-    g_out.y_steps()
+    @step
+    def mix_own():
+        mix(g, 0)
+
+    @step
+    def mix_others():
+        wait_all(normed_copies)
+        each_group(lambda step: mix(place.g_at(-step), step))
 
     kv_waits = [kv_copy(place.g_at(-step), step) for step in range(groups)]
-    for copy in kv_waits:
-        copy.wait_recv()
-
     def slope_row(head):
         index = jnp.full((1, rows), g * heads + head, jnp.int32).astype(F32)
         return jnp.exp2((index + 1.0) * (-8.0 / H))
@@ -839,14 +890,20 @@
         def visit(index, carry):
             return body(lax.div(index, groups), lax.rem(index, groups), carry)
 
-        return lax.fori_loop(0, 2 * groups, visit, first)
+        if groups > 2:
+            return lax.fori_loop(0, 2 * groups, visit, first)
+        for index in range(2 * groups):
+            first = body(index // groups, index % groups, first)
+        return first
 
     def head_at(pair, half):
         return aligned(pair * pair_width + half * head_width, head_width)
 
     far, vt = v["far"], v["vt"]
 
-    def attend(block):
+    pairs = heads // 2
+
+    def attend(block, first, last):
         def body(pair):
             lanes = aligned(pair * pair_width, pair_width)
             fixed = []
@@ -873,7 +930,7 @@
                 own = summed[half * head_width : (half + 1) * head_width]
                 attt[block, head_at(pair, half)] = own / total
 
-        loop(heads // 2, body)
+        loop_from(first, last, body)
 
     att_own, att_send = v["att_own"], v["att_send"]
     att_first = wires.take(groups)
@@ -884,7 +941,9 @@
             att_first + step,
         )
 
-    def attention():
+    @step
+    def turn_keys():
+        wait_all(kv_waits)
         for core in range(2):
 
             def turn(b, core=core):
@@ -893,42 +952,55 @@
 
             loop(groups, turn)
 
-        def other(step, carry):
-            block = place.g_at(step)
-            fill_far(block)
-            attend(block)
-            att_send[block] = attt[block].T.astype(LOW)
-            att_copy(step, block).start()
-            return carry
-
-        lax.fori_loop(1, groups, other, 0)
-        g_up.z_step(2)
-        g_out.x_steps()
+    def attend_end(step):
+        block = place.g_at(step)
+        att_send[block] = attt[block].T.astype(LOW)
+        att_copy(step, block).start()
+
+    def attend_other(step):
+        fill_far(place.g_at(step))
+        attend(place.g_at(step), 0, pairs)
+        attend_end(step)
+
+    in_two = groups == 2
+
+    @step
+    def att_other_a():
+        if in_two:
+            fill_far(place.g_at(1))
+            attend(place.g_at(1), 0, pairs // 2)
+
+    @step
+    def att_other_b():
+        if in_two:
+            attend(place.g_at(1), pairs // 2, pairs)
+            attend_end(1)
+        else:
+            each_group(attend_other)
+
+    @step
+    def att_own_a():
         fill_far(g)
-        attend(g)
-        send_joined(1)
+        attend(g, 0, pairs // 2)
+
+    @step
+    def att_own_b():
+        attend(g, pairs // 2, pairs)
         att_own[:, own_cols] = attt[g].T.astype(LOW)
 
-    attention()
-    g_out.finish()
-    for step in range(1, groups):
-        att_copy(step, place.g_at(step)).wait_recv()
-
-    def middle_tile(n):
-        lane = aligned(n * tile, tile)
-        middle[:, lane] = merged[:, lane] + dot(
-            att_own[...], wout[:, :, :, lane].reshape(width, tile)
-        )
-
-    loop(width // tile, middle_tile)
-    norm_into(middle, 3, second.at[g])
-    second_copies = share(second)
-    cot_copies = share(cot_all)
-    for step in range(3, nz):
-        g_up.z_step(step)
-    g_up.y_steps()
-    g_down.z_step(1)
-    g_up.finish()
+    @step
+    def mid():
+        wait_all([att_copy(step, place.g_at(step)) for step in range(1, groups)])
+
+        def middle_tile(n):
+            lane = aligned(n * tile, tile)
+            middle[:, lane] = merged[:, lane] + dot(
+                att_own[...], wout[:, :, :, lane].reshape(width, tile)
+            )
+
+        loop(width // tile, middle_tile)
+        norm_into(middle, 3, second.at[g])
+        start_all(second_copies)
 
     active, ghid = v["active"], v["ghid"]
     unit_tile = 256
@@ -968,20 +1040,11 @@
 
         loop(count, body)
 
-    lend = groups > 2
-    p_send, p_recv = v["io"] if lend else v["p_send"], v["p_recv"]
-
-    def store_into(ref, kind):
-        def store(lane, value):
-            ref[:, lane] = value.astype(kind)
-
-        return store
-
     turned = v["turned"]
 
     def weight_grad(lefts, right, grad, left_at=0):
         count, per, size = row_chunks(grad, turned.shape[0])
-        step_cols = min(256, grad.shape[3])
+        step_cols = min(512, grad.shape[3])
         depth = len(lefts) * rows
         count = count * lefts[0].shape[1] // (n_dp * grad.shape[2])
 
@@ -998,81 +1061,54 @@
                     per, 2, size // per // 2, step_cols
                 )
 
-            loop(grad.shape[3] // step_cols, inner)
+            loop(grad.shape[3] // step_cols, inner, 2)
 
         loop(count, body)
 
     def blocks(ref):
         return [ref.at[b] for b in range(groups)]
 
-    feed(g)
-    g_down.z_step(2)
-    second_first = wires.take(groups)
-
-    def part_copy(step, first):
-        return wires.copy(
-            lambda: (p_send.at[part_slot(step)], p_recv.at[step - 1], place.x_peer(step)),
-            first + step,
-        )
-
-    def part_slot(step):
-        return 0 if groups == 2 else lax.rem(step, 2)
-
-    def send_part(step, left, weight, first):
-        if groups > 3:
-
-            @pl.when(step > 2)
-            def _():
-                part_copy(step - 2, first).wait_send()
-
-        back_product(left, weight, store_into(p_send.at[part_slot(step)], LOW))
-        part_copy(step, first).start()
-
-    def parts_sent(first):
-        for step in range(max(1, groups - 2), groups):
-            part_copy(step, first).wait_send()
-
-    for copy in second_copies:
-        copy.wait_recv()
-    each_group(lambda step: feed(place.g_at(step)))
-    send_joined(len(joined_parts))
+    @step
+    def feed_own():
+        feed(g)
+
+    @step
+    def feed_others():
+        wait_all(second_copies)
+        each_group(lambda step: feed(place.g_at(step)))
+
     early = shard_rows == unit_tile
     grad_down = v["grad_down"] if early else wdown
     r_down = Reduce(
         place, wires, grad_down, h_down, False, v["c_down"], None, v["y_down"], v["z_down"],
         v["p_down"],
     )
-    if early:
-
-        def feed_shard(z_index, y_index):
-            lane = aligned((z_index * 2 + y_index) * unit_tile, unit_tile)
-            feed_back(lane, wdown[z_index, y_index])
-
-        for step in range(3, nz):
-            g_down.z_step(step)
-        for copy in cot_copies:
-            copy.wait_recv()
+
+    def down_gradient():
         weight_grad(blocks(active), cot_all, grad_down)
         r_down.core_send(0)
         r_down.core_send(1)
-        for reach in range(nz - 1):
-            g_down.y_step(reach)
-        for reach in range(nz):
-            g_down.c_wait(reach, 0)
-        loop(nz, lambda z_index: feed_shard(z_index, y))
-        g_down.y_step(nz - 1)
-        r_down.core_add(0)
-        r_down.core_add(1)
-        for reach in range(nz):
-            g_down.c_wait(reach, 1)
-        loop(nz, lambda z_index: feed_shard(z_index, 1 - y))
-    else:
-        for step in range(3, nz):
-            g_down.z_step(step)
-        for copy in cot_copies:
-            copy.wait_recv()
-        g_down.y_steps()
-        g_down.finish()
+
+    @step
+    def grad_d():
+        wait_all(cot_copies)
+        if early:
+            down_gradient()
+
+    def feed_shard(z_index, y_index):
+        lane = aligned((z_index * 2 + y_index) * unit_tile, unit_tile)
+        feed_back(lane, wdown[z_index, y_index])
+
+    @step
+    def feed_a():
+        if early:
+            loop(nz, lambda z_index: feed_shard(z_index, y))
+
+    @step
+    def feed_b():
+        if early:
+            loop(nz, lambda z_index: feed_shard(z_index, 1 - y))
+            return
         per = unit_tile // (2 * shard_rows)
 
         def feed_tile(u):
@@ -1081,24 +1117,62 @@
 
         loop(units // unit_tile, feed_tile)
 
-    each_group(lambda step: send_part(step, ghid.at[place.g_at(step)], wup, second_first))
-    back_product(ghid.at[g], wup, store_into(gmid, F32))
+    lend = groups > 2
+    p_send, p_recv = v["io"] if lend else v["p_send"], v["p_recv"]
+
+    def store_into(ref, kind):
+        def store(lane, value):
+            ref[:, lane] = value.astype(kind)
+
+        return store
+
+    second_first, mix_first = wires.take(groups), wires.take(groups)
+
+    def part_copy(step, first):
+        return wires.copy(
+            lambda: (p_send.at[part_slot(step)], p_recv.at[step - 1], place.x_peer(step)),
+            first + step,
+        )
+
+    def part_slot(step):
+        return 0 if groups == 2 else lax.rem(step, 2)
+
+    def send_part(step, left, weight, first):
+        if groups > 3:
+
+            @pl.when(step > 2)
+            def _():
+                part_copy(step - 2, first).wait_send()
+
+        back_product(left, weight, store_into(p_send.at[part_slot(step)], LOW))
+        part_copy(step, first).start()
+
+    def parts_sent(first):
+        for step in range(max(1, groups - 2), groups):
+            part_copy(step, first).wait_send()
+
+    @step
+    def part_send():
+        each_group(lambda step: send_part(step, ghid.at[place.g_at(step)], wup, second_first))
+
+    @step
+    def part_own():
+        back_product(ghid.at[g], wup, store_into(gmid, F32))
 
     def down_tile(left, target, n):
         lane = aligned(n * tile, tile)
         target(lane, dot(left[...], wdown[:, :, :, lane].reshape(units, tile)))
 
-    g_up.drain()
-    g_down.drain()
-    weight_grad(blocks(second), ghid, wup)
     r_up = Reduce(
         place, wires, wup, h_up, False, v["c_up"], None, v["y_up"], v["z_up"], v["p_up"]
     )
-    r_up.core_send(0)
-    r_up.core_send(1)
-
-    for copy in second_copies:
-        copy.wait_send()
+
+    @step
+    def grad_u():
+        g_up.drain()
+        weight_grad(blocks(second), ghid, wup)
+        r_up.core_send(0)
+        r_up.core_send(1)
 
     def other_down(step):
         block = place.g_at(step)
@@ -1108,18 +1182,20 @@
 
         loop(width // tile, lambda n: down_tile(active.at[block], keep, n))
 
-    each_group(other_down)
-    r_up.core_add(0)
-    r_up.core_add(1)
-
     def own_down(lane, value):
         second[g, :, lane] = value.astype(LOW)
 
-    loop(width // tile, lambda n: down_tile(active.at[g], own_down, n))
-    if not early:
-        weight_grad(blocks(active), cot_all, wdown)
-        r_down.core_send(0)
-        r_down.core_send(1)
+    @step
+    def out_parts():
+        sent_all(second_copies)
+        each_group(other_down)
+        loop(width // tile, lambda n: down_tile(active.at[g], own_down, n))
+        g_down.drain()
+        if not early:
+            down_gradient()
+            r_down.core_add(0)
+            r_down.core_add(1)
+
     sums = v["sums"]
     sums[...] = jnp.zeros_like(sums)
 
@@ -1130,44 +1206,42 @@
         return lax.fori_loop(0, count, body, jnp.zeros((1, wide), F32))
 
     per_block = rows // chunk
-    ghid_sum = column_sums(
-        lambda i: ghid[lax.div(i, per_block), aligned(lax.rem(i, per_block) * chunk, chunk)],
-        groups * per_block,
-        units,
-    )
-    if units >= width:
-        for row in range(sizes.up_rows):
-            sums[6 + row : 7 + row] = ghid_sum[:, row * width : (row + 1) * width]
-    else:
-        sums[6:7, 0:units] = ghid_sum
-    sums[5:6] = column_sums(lambda i: cot_all[g, aligned(i * chunk, chunk)], per_block, width)
-    if not early:
-        r_down.core_add(0)
-        r_down.core_add(1)
-
-    for step in range(1, groups):
-        part_copy(step, second_first).wait_recv()
-
-    def second_in(at):
-        t = gmid[at]
-        for step in range(1, groups):
-            t = t + p_recv[step - 1, at].astype(F32)
-        return t
+    @step
+    def sums_early():
+        ghid_sum = column_sums(
+            lambda i: ghid[lax.div(i, per_block), aligned(lax.rem(i, per_block) * chunk, chunk)],
+            groups * per_block,
+            units,
+        )
+        if units >= width:
+            for row in range(sizes.up_rows):
+                sums[6 + row : 7 + row] = ghid_sum[:, row * width : (row + 1) * width]
+        else:
+            sums[6:7, 0:units] = ghid_sum
+        sums[5:6] = column_sums(lambda i: cot_all[g, aligned(i * chunk, chunk)], per_block, width)
 
     gb = v["gb"]
 
-    def second_out(at, grad):
-        total = grad + cot_all[g, at].astype(F32)
-        gmid[at] = total
-        gb[at] = total.astype(LOW)
-
-    gain_sum, bias_sum = norm_back(middle, 3, second_in, second_out)
-    sums[3:4] = gain_sum
-    sums[4:5] = bias_sum
+    @step
+    def norm_second():
+        wait_all([part_copy(step, second_first) for step in range(1, groups)])
+
+        def second_in(at):
+            t = gmid[at]
+            for step in range(1, groups):
+                t = t + p_recv[step - 1, at].astype(F32)
+            return t
+
+        def second_out(at, grad):
+            total = grad + cot_all[g, at].astype(F32)
+            gmid[at] = total
+            gb[at] = total.astype(LOW)
+
+        gain_sum, bias_sum = norm_back(middle, 3, second_in, second_out)
+        sums[3:4] = gain_sum
+        sums[4:5] = bias_sum
 
     ga_in, ga_send = v["ga_in"], att_send
-    for step in range(1, groups):
-        att_copy(step, place.g_at(step)).wait_send()
     ga_first = wires.take(groups)
 
     def ga_copy(step):
@@ -1176,20 +1250,24 @@
             lambda: (ga_send.at[block], ga_in.at[g], place.x_peer(step)), ga_first + step
         )
 
-    count, per, size = row_chunks(wout)
-
-    def branch_back(j):
-        value = dot_nt(gb[...], wout[pl.ds(j * per, per)].reshape(size, width)).astype(LOW)
-        for b in range(max(1, size // cols)):
-            if size >= cols:
-                ga_send[j * (size // cols) + b] = value[:, b * cols : (b + 1) * cols]
-            else:
-                ga_send[lax.div(j, cols // size), :, aligned(lax.rem(j, cols // size) * size, size)] = value
-
-    loop(count, branch_back)
-    for step in range(1, groups):
-        ga_copy(step).start()
-    ga_in[g] = ga_send[g]
+    @step
+    def branch():
+        sent_all([att_copy(step, place.g_at(step)) for step in range(1, groups)])
+        count, per, size = row_chunks(wout)
+
+        def branch_back(j):
+            value = dot_nt(gb[...], wout[pl.ds(j * per, per)].reshape(size, width)).astype(LOW)
+            for b in range(max(1, size // cols)):
+                if size >= cols:
+                    ga_send[j * (size // cols) + b] = value[:, b * cols : (b + 1) * cols]
+                else:
+                    lane = aligned(lax.rem(j, cols // size) * size, size)
+                    ga_send[lax.div(j, cols // size), :, lane] = value
+
+        loop(count, branch_back)
+        start_all([ga_copy(step) for step in range(1, groups)])
+        ga_in[g] = ga_send[g]
+
     out_swap = Exchange(place, wires)
     out_copies = [
         out_swap.copy(
@@ -1197,13 +1275,16 @@
         )
         for step in range(1, groups)
     ]
-    g_out.drain()
-    weight_grad([att_own], gb, wout)
     r_out = Reduce(
         place, wires, wout, h_out, True, v["c_out"], v["x_out"], v["y_out"], v["z_out"], v["p_out"]
     )
-    r_out.core_send(0)
-    r_out.core_send(1)
+
+    @step
+    def grad_o():
+        g_out.drain()
+        weight_grad([att_own], gb, wout)
+        r_out.core_send(0)
+        r_out.core_send(1)
 
     gm = v["gm"]
 
@@ -1212,9 +1293,11 @@
 
     gat, gqt, skt = vt.at[0, 0], vt.at[0, 1], vt.at[1, 0]
 
-    def back_attend(block, first, between):
+    def back_start(block):
+        fill_far(block)
         gat[...] = ga_in[block].T
 
+    def back_attend(block, fresh, first, last):
         def body(pair):
             lanes = aligned(pair * pair_width, pair_width)
             later = aligned(cols + pair * pair_width, pair_width)
@@ -1253,7 +1336,7 @@
                     done.append((shift_sum, query_grad + dot(kt[core, b, lanes], grad_low)))
                 for start, found in zip(starts, (key_grad, value_grad)):
                     at = dkv_lanes(core, start, pair_width)
-                    if not first:
+                    if not fresh:
                         found = found + active[b, :, at].astype(F32)
                     active[b, :, at] = found.astype(LOW)
                 return tuple(done)
@@ -1268,10 +1351,9 @@
                 gqt[at] = (0.125 * (own + shift_sum * own_keys)).astype(LOW)
                 skt[at] = (shift_sum * qt[block, at].astype(F32)).astype(LOW)
 
-        middle_pair = heads // 4
-        loop_from(0, middle_pair, body)
-        between()
-        loop_from(middle_pair, heads // 2, body)
+        loop_from(first, last, body)
+
+    def back_end(block):
         gm[block, :, 0:cols] = gqt[...].T
         at = dkv_lanes(c, 0, cols)
         active[block, :, at] = active[block, :, at] + skt[...].T
@@ -1288,100 +1370,182 @@
             dkv_wire,
         )
 
-    def out_steps():
-        r_out.core_add(0)
-        r_out.core_add(1)
-
-    def out_x_steps():
-        r_out.x_add(0)
-        r_out.x_add(1)
-
-    up_tasks, down_tasks = r_up.y_tasks(), r_down.y_tasks()
-    tasks += down_tasks[0:2] + [out_steps] + down_tasks[2:]
-    fill_far(g)
-    work(2)
-    back_attend(g, True, lambda: work(2))
-    work(2)
-    for step in range(1, groups):
-        ga_copy(step).wait_recv()
-    for copy in cot_copies:
-        copy.wait_send()
-    for copy in out_copies:
-        copy.start()
-    tasks += up_tasks[0:1] + [out_x_steps, r_down.z_add] + up_tasks[1:3]
-
-    def other_attend(step):
+    def back_other(step):
         block = place.g_at(-step)
-        fill_far(block)
-        back_attend(block, False, (lambda: work(1)) if groups == 2 else (lambda: None))
-
-    each_group(other_attend)
-    if groups > 2:
-        work()
-    r_down.y_sent()
-    dkv_copy().start()
-    work()
-    dkv_copy().wait_recv()
-
-    def merge(b):
-        gm[b, :, cols : 3 * cols] = gm[b, :, cols : 3 * cols] + active[b, :, dkv_lanes(c, 0, 2 * cols)]
-
-    loop(groups, merge)
-
-    parts_sent(second_first)
-    mix_first = wires.take(groups)
-
-    each_group(lambda step: send_part(step, gm.at[place.g_at(step)], wqkv, mix_first))
+        back_start(block)
+        back_attend(block, False, 0, pairs)
+        back_end(block)
+
+    @step
+    def back_own_a():
+        back_start(g)
+        back_attend(g, True, 0, pairs // 2)
+
+    @step
+    def back_own_b():
+        back_attend(g, True, pairs // 2, pairs)
+        back_end(g)
+
+    @step
+    def ga_wait():
+        wait_all([ga_copy(step) for step in range(1, groups)])
+
+    @step
+    def out_send():
+        sent_all(cot_copies)
+        start_all(out_copies)
+
+    @step
+    def back_other_a():
+        if in_two:
+            back_start(place.g_at(-1))
+            back_attend(place.g_at(-1), False, 0, pairs // 2)
+
+    @step
+    def back_other_b():
+        if in_two:
+            back_attend(place.g_at(-1), False, pairs // 2, pairs)
+            back_end(place.g_at(-1))
+        else:
+            each_group(back_other)
+        dkv_copy().start()
+
+    @step
+    def merge_keys():
+        dkv_copy().wait_recv()
+
+        def merge_block(b):
+            at = dkv_lanes(c, 0, 2 * cols)
+            gm[b, :, cols : 3 * cols] = gm[b, :, cols : 3 * cols] + active[b, :, at]
+
+        loop(groups, merge_block)
+
+    @step
+    def mix_send():
+        parts_sent(second_first)
+        each_group(lambda step: send_part(step, gm.at[place.g_at(step)], wqkv, mix_first))
+
     own_parts = [far.at[i // groups, i % groups] for i in range(width // rows)]
 
-    count, per, size = row_chunks(wqkv)
-    for j in range(count):
-        value = dot_nt(gm[g], wqkv[j * per : (j + 1) * per].reshape(size, 3 * cols))
-        for i in range(size // rows):
-            own_parts[j * (size // rows) + i][...] = value[:, i * rows : (i + 1) * rows]
-    g_qkv.drain()
-    weight_grad(blocks(normed), gm, wqkv)
+    @step
+    def mix_back():
+        count, per, size = row_chunks(wqkv)
+        for j in range(count):
+            value = dot_nt(gm[g], wqkv[j * per : (j + 1) * per].reshape(size, 3 * cols))
+            for i in range(size // rows):
+                own_parts[j * (size // rows) + i][...] = value[:, i * rows : (i + 1) * rows]
+
     c_qkv = v["c_up"].at[:, :, :, 0 : 3 * cols]
     r_qkv = Reduce(
         place, wires, wqkv, h_qkv, False, c_qkv, None, v["y_qkv"], v["z_qkv"], v["p_qkv"]
     )
-    tasks += up_tasks[3:]
-    work()
-    r_up.y_sent()
-    pl.semaphore_signal(v["free_sem"], inc=1, device_id=place.c_peer(), device_id_type=MESH)
-    pl.semaphore_wait(v["free_sem"], 1)
-    r_qkv.core_send(0)
-    r_qkv.core_send(1)
-    r_qkv.core_add(0)
-    r_qkv.core_add(1)
-    for step in range(1, groups):
-        part_copy(step, mix_first).wait_recv()
-
-    def first_in(at):
-        t = jnp.concatenate([part[at] for part in own_parts], axis=1)
-        for step in range(1, groups):
-            t = t + p_recv[step - 1, at].astype(F32)
-        return t
-
-    def first_out(at, grad):
-        gb[at] = (grad + gmid[at]).astype(LOW)
-
-    gain_sum, bias_sum = norm_back(merged, 1, first_in, first_out)
-    sums[1:2] = gain_sum
-    sums[2:3] = bias_sum
-    sums[0:1] = column_sums(lambda i: gb[aligned(i * chunk, chunk)], per_block, width)
+
+    @step
+    def grad_q():
+        g_qkv.drain()
+        weight_grad(blocks(normed), gm, wqkv)
+
+    @step
+    def up_free():
+        r_up.y_sent()
+        pl.semaphore_signal(v["free_sem"], inc=1, device_id=place.c_peer(), device_id_type=MESH)
+
+    @step
+    def qkv_send():
+        pl.semaphore_wait(v["free_sem"], 1)
+        r_qkv.core_send(0)
+        r_qkv.core_send(1)
+
+    @step
+    def norm_merged():
+        wait_all([part_copy(step, mix_first) for step in range(1, groups)])
+
+        def first_in(at):
+            t = jnp.concatenate([part[at] for part in own_parts], axis=1)
+            for step in range(1, groups):
+                t = t + p_recv[step - 1, at].astype(F32)
+            return t
+
+        def first_out(at, grad):
+            gb[at] = (grad + gmid[at]).astype(LOW)
+
+        gain_sum, bias_sum = norm_back(merged, 1, first_in, first_out)
+        sums[1:2] = gain_sum
+        sums[2:3] = bias_sum
+
+    gmx = v["gmx"]
+    merged_copies = []
+    if sizes.pair:
+        other_cols = aligned((1 - g) * cols, cols)
+        merged_copies = [
+            Exchange(place, wires).copy(1, lambda: gb.at[:, other_cols], lambda: gmx.at[1])
+        ]
+
+    @step
+    def merged_send():
+        start_all(merged_copies)
+        if sizes.pair:
+            gmx[0] = gb[:, own_cols]
 
     sum_in = v["sum_in"]
 
-    def sum_swap(slot, peer):
-        copy = wires.copy(lambda: (sums, sum_in.at[slot], peer))
-        copy.start()
-        return copy
+    def sum_copy(slot, peer):
+        return wires.copy(lambda: (sums, sum_in.at[slot], peer()))
+
+    sum_core = sum_copy(0, place.c_peer)
+    sum_x = [sum_copy(k, functools.partial(place.x_peer, k)) for k in range(1, groups)]
+    sum_y = sum_copy(groups, place.y_peer)
+    sum_z = [sum_copy(groups + k, functools.partial(place.z_peer, k)) for k in range(1, nz)]
+    o_up = v["o_up"]
+    up_swap = Exchange(place, wires)
+    up_copies = [up_swap.copy(k, lambda: o_up.at[g], lambda: o_up.at[g]) for k in range(1, groups)]
+
+    @step
+    def sum_0():
+        r_down.y_sent()
+        sums[0:1] = column_sums(lambda i: gb[aligned(i * chunk, chunk)], per_block, width)
+        sum_core.start()
+
+    @step
+    def sum_1():
+        sum_core.wait()
+        sums[...] = sums[...] + sum_in[0]
+        start_all(sum_x)
+
+    @step
+    def sum_2():
+        for copy in sum_x:
+            copy.wait()
+        for k in range(1, groups):
+            sums[0:6] = sums[0:6] + sum_in[k, 0:6]
+        sum_y.start()
+
+    @step
+    def sum_3():
+        sum_y.wait()
+        sums[...] = sums[...] + sum_in[groups]
+        start_all(sum_z)
+
+    @step
+    def sum_4():
+        for copy in sum_z:
+            copy.wait()
+        for k in range(1, nz):
+            sums[...] = sums[...] + sum_in[groups + k]
+        o_up[g] = sums[...]
+        v["o_small"][...] = sums[...]
+        start_all(up_copies)
 
     stores = []
     gj = normed
 
-    def joined_back():
+    @step
+    def inputs_back():
+        if sizes.pair:
+            give_inputs()
+
+    def give_inputs():
+        sent_all(normed_copies)
         count, per, size = row_chunks(ws)
         span = width // size
 
@@ -1395,115 +1559,94 @@
             stores.append(pltpu.make_async_copy(gj.at[half], v[name].at[0], local.at[1 + half]))
             stores[-1].start()
 
-    merged_copies = []
+    @step
+    def output():
+        wait_all(out_copies)
+        ob = second.at[g]
+
+        def out_rows(i):
+            at = aligned(i * chunk, chunk)
+            value = middle[at] + second[g, at].astype(F32) + vecs[5:6]
+            for step in range(1, groups):
+                value = value + cot_all[place.g_at(-step), at].astype(F32)
+            ob[at] = value.astype(LOW)
+
+        loop(rows // chunk, out_rows)
+        stores.append(pltpu.make_async_copy(ob, v["o_out"].at[0], local.at[0]))
+        stores[-1].start()
+
     if sizes.pair:
-        gmx = v["gmx"]
-        merged_swap = Exchange(place, wires)
-        other_cols = aligned((1 - g) * cols, cols)
-        merged_copies = [
-            merged_swap.copy(1, lambda: gb.at[:, other_cols], lambda: gmx.at[1])
-        ]
-        merged_copies[0].start()
-        gmx[0] = gb[:, own_cols]
-    sum_core = sum_swap(0, place.c_peer())
-    if lend:
-        parts_sent(mix_first)
-        for load in input_loads():
-            load.start()
-        for load in input_loads():
-            load.wait()
-    g_skip.drain()
-    for copy in normed_copies:
-        copy.wait_send()
-    joined_back()
-    for copy in out_copies:
-        copy.wait_recv()
-    ob = second.at[g]
-
-    def out_rows(i):
-        at = aligned(i * chunk, chunk)
-        value = middle[at] + second[g, at].astype(F32) + vecs[5:6]
-        for step in range(1, groups):
-            value = value + cot_all[place.g_at(-step), at].astype(F32)
-        ob[at] = value.astype(LOW)
-
-    loop(rows // chunk, out_rows)
-    stores.append(pltpu.make_async_copy(ob, v["o_out"].at[0], local.at[0]))
-    stores[-1].start()
-    r_down.core_sent()
-    tasks += r_out.y_tasks()
-    sum_core.wait()
-    sums[...] = sums[...] + sum_in[0]
-    sum_x = [sum_swap(step, place.x_peer(step)) for step in range(1, groups)]
-    work()
-    qkv_tasks = r_qkv.y_tasks()
-    if sizes.pair:
-        for copy in joined_copies + merged_copies:
-            copy.wait()
         grad_skip, c_skip = wdown.at[:, :, :, 0:cols], v["c_down"].at[:, :, :, 0:cols]
-        for half in range(2):
-            lefts = [v["io"].at[half], v["joined"].at[half]]
-            weight_grad(lefts, gmx, grad_skip, half * (nz // 2))
     else:
         grad_skip, c_skip = ws, v["c_skip"]
-        weight_grad([fr_v], gb, grad_skip)
-        weight_grad([sk_v], gb, grad_skip, nz // 2)
     r_skip = Reduce(
         place, wires, grad_skip, h_skip, not sizes.pair, c_skip, v["x_skip"], v["y_skip"],
         v["z_skip"], v["p_skip"],
     )
-    r_skip.core_send(0)
-    r_skip.core_send(1)
-    for copy in sum_x:
-        copy.wait()
-    for step in range(1, groups):
-        sums[0:6] = sums[0:6] + sum_in[step, 0:6]
-    sum_y = sum_swap(groups, place.y_peer())
-    r_skip.core_add(0)
-    r_skip.core_add(1)
-    if not sizes.pair:
-        r_skip.x_add(0)
-        r_skip.x_add(1)
-    tasks += [r_down.spread_on, r_up.z_add, r_out.z_add]
-    tasks += qkv_tasks + [r_up.spread_on]
-    work()
-    sum_y.wait()
-    sums[...] = sums[...] + sum_in[groups]
-    sum_z = [sum_swap(groups + step, place.z_peer(step)) for step in range(1, nz)]
-    skip_tasks = r_skip.y_tasks()
-    tasks += [skip_tasks[0], r_out.spread_on] + skip_tasks[1:] + [r_qkv.z_add]
-    work()
-    for copy in sum_z:
-        copy.wait()
-    for step in range(1, nz):
-        sums[...] = sums[...] + sum_in[groups + step]
-    o_up = v["o_up"]
-    o_up[g] = sums[...]
-    v["o_small"][...] = sums[...]
-    up_swap = Exchange(place, wires)
-    up_copies = [up_swap.copy(step, lambda: o_up.at[g], lambda: o_up.at[g]) for step in range(1, groups)]
-    for copy in up_copies:
-        copy.start()
-    r_skip.z_add()
-    r_qkv.spread_on()
-    r_skip.spread_on()
+
+    @step
+    def grad_s():
+        if sizes.pair:
+            for copy in joined_copies + merged_copies:
+                copy.wait()
+            for half in range(2):
+                lefts = [v["io"].at[half], v["joined"].at[half]]
+                weight_grad(lefts, gmx, grad_skip, half * (nz // 2))
+        else:
+            give_inputs()
+            parts_sent(mix_first)
+            for load in input_loads():
+                load.start()
+            for load in input_loads():
+                load.wait()
+            g_skip.drain()
+            weight_grad([fr_v], gb, grad_skip)
+            weight_grad([sk_v], gb, grad_skip, nz // 2)
+        r_skip.core_send(0)
+        r_skip.core_send(1)
+
+    def reduce_steps(name, reduced, ready=True):
+        for part in range(2):
+            add = functools.partial(reduced.core_add, part) if ready else none
+            steps[f"{name}_c{part}"] = add
+
+        def add_y(reach):
+            for one in reaches(reach):
+                reduced.y_add(one)
+
+        for reach in range(last_reach + 1):
+            steps[f"{name}_y{reach}"] = functools.partial(add_y, reach)
+        steps[name + "_z"], steps[name + "_f"] = reduced.z_add, reduced.spread_on
+
+    reduce_steps("rd", r_down, early)
+    reduce_steps("ru", r_up)
+    reduce_steps("ro", r_out)
+    reduce_steps("rq", r_qkv)
+    reduce_steps("rs", r_skip)
+    steps["ro_x0"], steps["ro_x1"] = (functools.partial(r_out.x_add, part) for part in range(2))
+    if r_skip.spread:
+        steps["rs_c1"] = lambda: [r_skip.core_add(1), r_skip.x_add(0), r_skip.x_add(1)]
+
+    assert sorted(ORDER) == sorted(steps), set(ORDER) ^ set(steps)
+    order = list(ORDER)
+    if not early:
+        cut = order.index("out_parts") + 1
+        moved = [name for name in order[:cut] if name.startswith("rd_")]
+        order[:cut] = [name for name in order[:cut] if not name.startswith("rd_")] + moved
+    for name in order:
+        steps[name]()
 
     for copy in up_copies:
         copy.wait()
     for reduced in (r_up, r_down, r_out, r_qkv, r_skip):
         reduced.finish()
         reduced.drain()
-    for gathered in [g_small] + skips[1:]:
-        gathered.drain()
-    for copy in seg_copies + [seg_core] + kv_waits:
-        copy.wait_send()
-    for copy in out_copies:
-        copy.wait_send()
-    for step in range(1, groups):
-        ga_copy(step).wait_send()
-    if not lend:
+    for gather in [g_small, *gathers[6:]] + ([g_skip] if sizes.pair else []):
+        gather.drain()
+    sent_all(seg_copies + [seg_core] + kv_waits + out_copies)
+    sent_all([ga_copy(step) for step in range(1, groups)] + [dkv_copy()])
+    if sizes.pair:
         parts_sent(mix_first)
-    dkv_copy().wait_send()
     for store in stores:
         store.wait()
 

time: 256 us -> 212 us (0.83)
  Pallas kernels: 252 us -> 211 us
    pallas_call x1, Pallas kernels: 246 us -> 204 us  [per_device(): pl.pallas_call(functools.partial(kernel, sizes), out_shape=(whole, whole,...]
where the time goes in v3:
time: 212 us; the launch traced here: 211 us
  Pallas kernels  211 us (100%)
    pallas_call x1, Pallas kernels, per_device(): pl.pallas_call(functools.partial(kernel, sizes), out_shape=(whole, whole,...  204 us
    pallas_call x1, Pallas kernels, per_device(): pl.pallas_call(functools.partial(finish, sizes), out_shape=(whole,) * 3 +...  6.83 us

profile of v3, /device:TPU:0, one launch (start us, length us, event | category | flops | bytes accessed | tf_op | source)
XLA Modules:
  0.0 211.5 jit_solution(368287805422170304)
XLA Ops:
  0.7 203.8 %shard_map.271 = (bf16[1,256,1024]{2,1,0:T(8,128)(2,1)}, bf16[1,256,1024]{2,1,0:T(8,128)(2,1)}, bf16[1,256,1024]{2,1,0:T(8,128)(2,1)}, bf16[2,2,128,512]{3,2,1,0...) custom-call(bf16[1,256,1024]{2,1,0:T(8,128)(2,1)} %refs_0_.1, ...), custom_call_target="tpu_custom_call" | custom-call | tf_op jit(solution)/shard_map/pallas_call | solution.py:1793
  204.5 6.8 %shard_map.272 = (bf16[1,256,1024]{2,1,0:T(8,128)(2,1)}, bf16[1,256,1024]{2,1,0:T(8,128)(2,1)}, bf16[1,256,1024]{2,1,0:T(8,128)(2,1)}, f32[256,1024]{1,0:T(8,128...) custom-call(bf16[1,256,1024]{2,1,0:T(8,128)(2,1)} %get-tuple-element, ...), custom_call_target="tpu_custom_call" | custom-call | tf_op jit(solution)/shard_map/pallas_call | solution.py:1815

commit v4 on v3

--- a/solution.py
+++ b/solution.py
@@ -1,5 +1,6 @@
 import functools
 import math
+import types
 
 import jax
 import jax.numpy as jnp
@@ -145,12 +146,16 @@
 
 
 class Gather:
-    def __init__(self, place, wires, ref, half, spread=0, span=None, whole_core=False):
-        self.place, self.wires, self.ref = place, wires, ref
+    def __init__(
+        self, place, wires, ref, half, spread=0, span=None, whole_core=False, across=False
+    ):
+        self.place, self.wires, self.ref, self.across = place, wires, ref, across
         self.half, self.spread, self.span, self.whole_core = half, spread, span, whole_core
         self.nz = place.sizes.nz
         self.groups = place.sizes.groups if spread else 1
-        self.z_wires = {way: wires.take(self.nz) for way in (1, -1)}
+        self.z_wires = {
+            (way, far): wires.take(self.nz) for way in (1, -1) for far in range(1 + across)
+        }
         self.y_wires = wires.take(self.nz)
         self.x_wires = {
             (step, far): wires.take(self.nz) for step in range(1, self.groups) for far in (0, 1)
@@ -182,8 +187,9 @@
 
         return self.wires.copy(ends, (first, distance))
 
-    def z_copy(self, way, distance):
-        return self.copy(self.z_wires[way], lambda: self.place.z_next(way), distance, 0)
+    def z_copy(self, way, distance, far=0):
+        first = self.z_wires[way, far]
+        return self.copy(first, lambda: self.place.z_next(way), distance, far)
 
     def y_copy(self, distance):
         return self.copy(self.y_wires, self.place.y_peer, distance, 0)
@@ -205,33 +211,39 @@
         for distance in (-reach, reach):
             self.place.if_z(distance)(functools.partial(body, distance))
 
-    def start(self):
+    def start(self, far=0):
         for way in (1, -1):
-            self.place.if_z(way)(lambda way=way: self.z_copy(way, 0).start())
+            self.place.if_z(way)(lambda way=way: self.z_copy(way, 0, far).start())
 
     def own(self):
         self.forward(0, 0)
 
     def forward(self, distance, far):
-        if not far:
+        if not far and not (self.across and distance):
             self.y_copy(distance).start()
         for step in range(1, self.groups):
             self.x_copy(step, distance, far).start()
         if not self.whole_core:
             self.c_copy(0, distance, far).start()
 
-    def z_step(self, reach):
+    def z_step(self, reach, far=0):
         def body(distance):
             way = 1 if distance < 0 else -1
-            self.z_copy(way, distance).wait_recv()
-            self.place.if_z(way)(lambda: self.z_copy(way, distance).start())
-            self.forward(distance, 0)
+            self.z_copy(way, distance, far).wait_recv()
+            self.place.if_z(way)(lambda: self.z_copy(way, distance, far).start())
+            self.forward(distance, far)
 
         self.each(reach, body)
 
     def y_step(self, reach):
+        if self.across and reach:
+            self.z_step(reach, 1)
+            return
+
         def body(distance):
             self.y_arrival(distance).wait_recv()
+            if self.across:
+                self.start(1)
             self.forward(distance, 1)
 
         self.each(reach, body)
@@ -271,9 +283,12 @@
 
     def drain(self):
         def body(distance):
-            for way in (1, -1) if distance == 0 else (1,) if distance < 0 else (-1,):
-                self.place.if_z(way)(lambda way=way: self.z_copy(way, distance).wait_send())
-            self.y_copy(distance).wait_send()
+            for way, far in self.z_wires:
+                if way * distance <= 0:
+                    copy = self.z_copy(way, distance, far)
+                    self.place.if_z(way)(copy.wait_send)
+            if not (self.across and distance):
+                self.y_copy(distance).wait_send()
             for first in self.x_wires:
                 self.x_copy(first[0], distance, first[1]).wait_send()
             if not self.whole_core:
@@ -456,51 +471,46 @@
     return centred * scale, scale
 
 
-ORDER = (
-    "skip_own", "small_start", "small_own", "out_own", "qkv_own", "skip_start", "rest_start",
-    "small_z1", "seg_start", "cot_share", "qkv_start", "rest_own", "qkv_y0", "skip_z1", "skip_y0",
-    "rest_z1", "seg_pass", "out_start", "skip_z2", "skip_x0", "rest_z2", "skip_y1", "small_z2",
-    "skip_z3", "qkv_z1", "rest_y0", "skip_y2", "skip_x1", "skip_x2", "small_z3", "rest_z3",
-    "skip_y3", "skip_w0", "qkv_z2", "out_y0", "rest_y1", "out_z1", "skip_w1", "skip_w2",
-    "joined_0", "joined_1", "rest_a", "skip_x3", "small_y0", "out_x0", "small_y1", "rest_y2",
-    "small_y2", "qkv_z3", "rest_y3", "skip_w3", "skip_a", "out_z2", "rest_b", "small_y3", "qkv_a",
-    "up_start", "vectors", "skip_b", "out_x1", "merge", "norm_first", "up_z1", "out_y1", "out_x2",
-    "qkv_y1", "qkv_y2", "qkv_y3", "qkv_b", "seg_turn", "up_own", "down_start", "out_w0", "out_z3",
-    "mix_own", "up_z2", "down_own", "mix_others", "turn_keys", "out_y2", "att_other_a", "out_y3",
-    "out_w1", "att_other_b", "att_own_a", "out_w2", "out_w3", "att_own_b", "up_z3", "down_z1",
-    "out_b", "out_x3", "joined_2", "out_a", "mid", "up_y0", "up_y1", "down_z2", "up_y2", "down_y0",
-    "down_z3", "joined_3", "joined_4", "joined_5", "up_a", "down_a", "up_y3", "joined_6",
-    "joined_7", "up_b", "feed_own", "feed_others", "grad_d", "down_y1", "rd_c0", "feed_a",
-    "down_y2", "down_y3", "rd_c1", "down_b", "feed_b", "part_send", "rd_y1", "part_own", "grad_u",
-    "rd_y2", "out_parts", "rd_y3", "ru_c0", "norm_second", "branch", "grad_o", "back_own_a",
-    "ro_c0", "ru_c1", "back_own_b", "ru_y1", "ga_wait", "back_other_a", "ro_c1", "back_other_b",
-    "rd_y0", "ru_y2", "ro_x0", "sums_early", "merge_keys", "mix_send", "mix_back", "rd_z", "ro_x1",
-    "ru_y3", "grad_q", "ru_y0", "up_free", "qkv_send", "ro_y1", "rq_c0", "ro_y2", "ro_y3", "rq_c1",
-    "norm_merged", "merged_send", "ru_z", "rq_y1", "rq_y2", "sum_0", "sum_1", "grad_s", "rs_c0",
-    "ro_y0", "ro_z", "out_send", "rs_c1", "rq_y3", "rs_y1", "rs_y2", "rq_y0", "rq_z", "sum_2",
-    "rs_y3", "rs_y0", "ru_f", "output", "rd_f", "sum_3", "rs_z", "rq_f", "inputs_back", "sum_4",
-    "ro_f", "rs_f",
-)
-
-
-def kernel(sizes, *refs):
-    names = (
-        "frames", "skip", "cot", "seg", "b_skip", "gain_a", "bias_a", "gain_f", "bias_f",
-        "b_down", "b_up", "w_skip", "w_qkv", "w_out", "w_up", "w_down", "o_out", "o_frames",
-        "o_skip", "p_skip", "p_qkv", "p_out", "p_up", "p_down", "o_small", "o_up", "io",
-        "cot_all", "ws", "wqkv", "wout", "wup", "wdown", "small", "vecs", "bup", "segs", "segc",
-        "merged", "middle", "gmid", "normed", "second", "kv", "qt", "kt", "shift", "attt", "tot",
-        "att_own", "att_send", "active", "ghid", "p_send", "p_recv", "gb", "ga_in", "gm",
-        "far", "vt", "c_skip", "c_out", "c_up", "c_down", "x_skip", "x_out", "y_skip", "y_qkv",
-        "y_out", "y_up", "y_down", "z_skip", "z_qkv", "z_out", "z_up", "z_down", "joined", "gmx",
-        "grad_down", "sums", "sum_in", "turned", "send_sems", "recv_sems", "local_sems",
-        "free_sem",
-    )
-    assert len(names) == len(refs), (len(names), len(refs))
-    v = dict(zip(names, refs))
+def in_order(
+    skip_start, skip_own, cot_share, rest_start, qkv_own, skip_z1, qkv_start, rest_own, skip_z2,
+    rest_z1, skip_z3, skip_y0, small_own, skip_y1, small_start, out_start, rest_z2, skip_x0,
+    small_z1, skip_x1, out_own, rest_z3, skip_y2, small_z2, small_z3, qkv_z1, rest_y0, skip_x2,
+    skip_y3, small_y0, out_z1, skip_x3, skip_w0, rest_a, skip_a, rest_y1, skip_w1, qkv_z2,
+    up_start, out_x0, small_y1, rest_y2, small_y2, joined_0, skip_w2, small_y3, vectors, seg_start,
+    rest_y3, out_y0, skip_w3, rest_b, skip_b, merge, norm_first, qkv_y0, out_z2, down_start,
+    qkv_z3, out_z3, up_own, qkv_y1, qkv_y2, qkv_a, down_own, seg_pass, up_z1, qkv_y3, qkv_b,
+    mix_own, mix_others, down_z1, out_y1, out_x1, out_x2, out_y2, out_y3, seg_turn, turn_keys,
+    att_other_a, att_other_b, out_w0, up_y0, out_x3, joined_1, up_z2, att_own_a, out_w1, out_w2,
+    down_y0, att_own_b, out_w3, out_b, out_a, mid, down_z2, up_z3, up_y1, down_y1, up_a, up_y2,
+    up_y3, joined_2, joined_3, down_z3, joined_4, joined_5, up_b, joined_6, feed_own, feed_others,
+    down_y2, grad_d, down_a, feed_a, rd_c0, down_y3, down_b, feed_b, part_send, rd_c1, part_own,
+    rd_y1, joined_7, grad_u, sums_early, rd_y2, out_parts, ru_c0, ru_c1, norm_second, branch,
+    grad_o, rd_y3, back_own_a, ro_c0, back_own_b, ga_wait, ru_y1, back_other_a, ro_c1, ru_y2,
+    back_other_b, ro_x0, ru_y3, merge_keys, mix_send, mix_back, ru_y0, ro_x1, up_free, grad_q,
+    qkv_send, skips_sent, rq_c0, rd_y0, rd_z, ro_y1, ro_y2, ro_y3, norm_merged, sum_0, merged_send,
+    rq_c1, rq_y1, sum_1, ro_y0, ru_z, rq_y2, out_send, rq_y3, grad_s, rs_c0, ro_z, ru_f, rq_y0,
+    rs_c1, rs_y1, rs_y2, sum_2, rs_y3, rq_z, rd_f, rd_e, inputs_back, rs_y0, output, sum_3,
+    blocks_sent, ru_e, rs_z, rq_f, ro_f, sum_4, ro_e, rq_e, parts_gone, rs_f,
+):
+    pass
+
+
+ORDER = in_order.__code__.co_varnames
+
+
+def kernel(
+    sizes, frames, skip, cot, seg, b_skip, gain_a, bias_a, gain_f, bias_f, b_down, b_up, w_skip,
+    w_qkv, w_out, w_up, w_down, o_out, o_frames, o_skip, p_skip, p_qkv, p_out, p_up, p_down,
+    o_small, o_up, io, cot_all, ws, wqkv, wout, wup, wdown, small, vecs, bup, segs, segc, merged,
+    middle, gmid, normed, second, kv, qt, kt, shift, attt, tot, att_own, att_send, active, ghid,
+    p_send, p_recv, gb, ga_in, gm, far, vt, c_skip, c_out, c_up, c_down, x_skip, x_out, y_skip,
+    y_qkv, y_out, y_up, y_down, z_skip, z_qkv, z_out, z_up, z_down, joined, gmx, grad_down, sums,
+    sum_in, turned, send_sems, recv_sems, local_sems, free_sem,
+):
+    v = types.SimpleNamespace(**locals())
     place = Place(sizes)
-    wires = Wires(place, v["send_sems"], v["recv_sems"])
-    local = v["local_sems"]
+    wires = Wires(place, v.send_sems, v.recv_sems)
+    local = v.local_sems
     nz, groups, n_dp, n_blk = sizes.nz, sizes.groups, sizes.n_dp, sizes.n_blk
     rows, width, cols, units = sizes.rows, sizes.width, sizes.cols, sizes.units
     heads = sizes.heads
@@ -518,27 +528,27 @@
     for partner in partners:
         pl.semaphore_signal(barrier, inc=1, device_id=partner, device_id_type=MESH)
 
-    fr_v, sk_v = v["io"].at[0], v["io"].at[1]
+    fr_v, sk_v = v.io.at[0], v.io.at[1]
 
     def input_loads():
         return [
-            pltpu.make_async_copy(v["frames"].at[0], fr_v, local.at[0]),
-            pltpu.make_async_copy(v["skip"].at[0], sk_v, local.at[1]),
+            pltpu.make_async_copy(v.frames.at[0], fr_v, local.at[0]),
+            pltpu.make_async_copy(v.skip.at[0], sk_v, local.at[1]),
         ]
 
     loads = input_loads() + [
-        pltpu.make_async_copy(v["cot"].at[0], v["cot_all"].at[g], local.at[2]),
+        pltpu.make_async_copy(v.cot.at[0], v.cot_all.at[g], local.at[2]),
     ]
 
-    h_skip, h_qkv = v["ws"].shape[2] // 2, v["wqkv"].shape[2] // 2
-    h_out, h_up, h_down = v["wout"].shape[2] // 2, v["wup"].shape[2] // 2, v["wdown"].shape[2] // 2
+    h_skip, h_qkv = v.ws.shape[2] // 2, v.wqkv.shape[2] // 2
+    h_out, h_up, h_down = v.wout.shape[2] // 2, v.wup.shape[2] // 2, v.wdown.shape[2] // 2
 
     stages = {}
 
     def fetch(name, start, size, tops, index):
         copies = [
             pltpu.make_async_copy(
-                v[name].at[aligned(start, size), part * width : (part + 1) * width],
+                getattr(v, name).at[aligned(start, size), part * width : (part + 1) * width],
                 buffer.at[top : top + size],
                 local.at[index + part],
             )
@@ -548,7 +558,7 @@
             copy.start()
         stages[name] = copies
 
-    merged, middle, gmid = v["merged"], v["middle"], v["gmid"]
+    merged, middle, gmid = v.merged, v.middle, v.gmid
     up_tops = [
         (middle, h_down), (middle, h_down + h_up), (merged, h_skip + h_out), (gmid, 3 * h_qkv)
     ]
@@ -559,7 +569,7 @@
     fetch("w_down", (g * 2 + c) * h_down, h_down, [(middle, 0)], 12)
     for load in loads:
         load.start()
-    ws, wqkv, wout, wup, wdown = v["ws"], v["wqkv"], v["wout"], v["wup"], v["wdown"]
+    ws, wqkv, wout, wup, wdown = v.ws, v.wqkv, v.wout, v.wup, v.wdown
     own_cols = aligned(g * cols, cols)
 
     def arrived(name):
@@ -601,16 +611,16 @@
     arrived("w_down")
     wdown[z, y, aligned(c * h_down, h_down)] = middle[0:h_down].astype(LOW)
 
-    small = v["small"]
+    small = v.small
     for row, name in enumerate(("b_skip", "gain_a", "bias_a", "gain_f", "bias_f", "b_down")):
-        small[z, y, row : row + 1, 0 : sizes.shard] = v[name][...].astype(LOW).astype(F32)
+        small[z, y, row : row + 1, 0 : sizes.shard] = getattr(v, name)[...].astype(LOW).astype(F32)
     if sizes.direct:
-        own_up = v["b_up"][:, aligned(g * sizes.part, sizes.part)]
+        own_up = v.b_up[:, aligned(g * sizes.part, sizes.part)]
     else:
-        own_up = v["b_up"][...]
+        own_up = v.b_up[...]
     small[z, y, 6:7, 0 : sizes.part] = own_up.astype(LOW).astype(F32)
-    segs = v["segs"]
-    segs[c, g] = jnp.broadcast_to(v["seg"][...].astype(F32), (8, rows))
+    segs = v.segs
+    segs[c, g] = jnp.broadcast_to(v.seg[...].astype(F32), (8, rows))
 
     pl.semaphore_wait(barrier, len(partners))
 
@@ -652,11 +662,11 @@
             steps[name + "_b"] = lambda: [gather.c_wait(reach, 1) for reach in range(nz)]
 
     g_small = Gather(place, wires, small, 0, whole_core=True)
-    g_skip = Gather(place, wires, v["ws"], h_skip, spread=share)
-    g_qkv = Gather(place, wires, v["wqkv"], h_qkv)
-    g_out = Gather(place, wires, v["wout"], h_out, spread=cols)
-    g_up = Gather(place, wires, v["wup"], h_up)
-    g_down = Gather(place, wires, v["wdown"], h_down)
+    g_skip = Gather(place, wires, v.ws, h_skip, spread=share)
+    g_qkv = Gather(place, wires, v.wqkv, h_qkv)
+    g_out = Gather(place, wires, v.wout, h_out, spread=cols)
+    g_up = Gather(place, wires, v.wup, h_up)
+    g_down = Gather(place, wires, v.wdown, h_down, across=True)
     gather_steps("small", g_small)
     gather_steps("skip", g_skip)
     gather_steps("qkv", g_qkv)
@@ -665,7 +675,7 @@
     gather_steps("down", g_down)
     gathers = [g_small, g_skip, g_qkv, g_out, g_up, g_down]
     if shared < width:
-        g_rest = Gather(place, wires, v["ws"], h_skip, span=(shared, width))
+        g_rest = Gather(place, wires, v.ws, h_skip, span=(shared, width))
         gather_steps("rest", g_rest)
         gathers.append(g_rest)
     else:
@@ -696,14 +706,14 @@
         if sizes.pair:
             at = part // 4, pl.ds(part % 4 * lines, lines)
             copy = Exchange(place, wires).copy(
-                1, lambda at=at: v["io"].at[at], lambda at=at: v["joined"].at[at]
+                1, lambda at=at: v.io.at[at], lambda at=at: v.joined.at[at]
             )
             joined_copies.append(copy)
             steps[f"joined_{part}"] = copy.start
         else:
             steps[f"joined_{part}"] = none
 
-    vecs, segc = v["vecs"], v["segc"]
+    vecs, segc = v.vecs, v.segc
 
     @step
     def vectors():
@@ -711,7 +721,7 @@
             vecs[row : row + 1] = jnp.concatenate(
                 [small[s // 2, s % 2, row : row + 1, 0 : sizes.shard] for s in range(n_dp)], axis=1
             )
-        v["bup"][...] = jnp.concatenate(
+        v.bup[...] = jnp.concatenate(
             [small[s // 2, s % 2, 6:7, 0 : sizes.part] for s in range(n_dp)], axis=1
         )
 
@@ -727,7 +737,7 @@
             loop(groups, turn)
 
     tile = min(256, width)
-    normed, second, cot_all = v["normed"], v["second"], v["cot_all"]
+    normed, second, cot_all = v.normed, v.second, v.cot_all
 
     @step
     def merge():
@@ -804,8 +814,8 @@
     def cot_share():
         start_all(cot_copies)
 
-    kv, qt, kt = v["kv"], v["qt"], v["kt"]
-    shift = v["shift"]
+    kv, qt, kt = v.kv, v.qt, v.kt
+    shift = v.shift
     pick = (
         lax.broadcasted_iota(jnp.int32, (max(8, heads), cols), 1)
         // (width // H)
@@ -880,7 +890,7 @@
 
     head_width = width // H
     pair_width = 2 * head_width
-    attt, tot = v["attt"], v["tot"]
+    attt, tot = v.attt, v.tot
 
     def score_terms(pair, core, b, queries_pad, slope, moved):
         keys = kv[core, b, :, aligned(pair * pair_width, pair_width)]
@@ -899,7 +909,7 @@
     def head_at(pair, half):
         return aligned(pair * pair_width + half * head_width, head_width)
 
-    far, vt = v["far"], v["vt"]
+    far, vt = v.far, v.vt
 
     pairs = heads // 2
 
@@ -932,7 +942,7 @@
 
         loop_from(first, last, body)
 
-    att_own, att_send = v["att_own"], v["att_send"]
+    att_own, att_send = v.att_own, v.att_send
     att_first = wires.take(groups)
 
     def att_copy(step, block):
@@ -1002,14 +1012,14 @@
         norm_into(middle, 3, second.at[g])
         start_all(second_copies)
 
-    active, ghid = v["active"], v["ghid"]
+    active, ghid = v.active, v.ghid
     unit_tile = 256
     shard_rows = wdown.shape[2]
 
     def feed(block):
         def body(u):
             lane = aligned(u * unit_tile, unit_tile)
-            pre = dot(second[block], wup[:, :, :, lane].reshape(width, unit_tile)) + v["bup"][:, lane]
+            pre = dot(second[block], wup[:, :, :, lane].reshape(width, unit_tile)) + v.bup[:, lane]
             normal = 0.5 * (1.0 + lax.erf(pre * (0.5**0.5)))
             active[block, :, lane] = (pre * normal).astype(LOW)
             slope = normal + pre * (jnp.exp(-0.5 * pre * pre) * (1.0 / math.sqrt(2.0 * math.pi)))
@@ -1040,7 +1050,7 @@
 
         loop(count, body)
 
-    turned = v["turned"]
+    turned = v.turned
 
     def weight_grad(lefts, right, grad, left_at=0):
         count, per, size = row_chunks(grad, turned.shape[0])
@@ -1078,10 +1088,10 @@
         each_group(lambda step: feed(place.g_at(step)))
 
     early = shard_rows == unit_tile
-    grad_down = v["grad_down"] if early else wdown
+    grad_down = v.grad_down if early else wdown
     r_down = Reduce(
-        place, wires, grad_down, h_down, False, v["c_down"], None, v["y_down"], v["z_down"],
-        v["p_down"],
+        place, wires, grad_down, h_down, False, v.c_down, None, v.y_down, v.z_down,
+        v.p_down,
     )
 
     def down_gradient():
@@ -1118,7 +1128,7 @@
         loop(units // unit_tile, feed_tile)
 
     lend = groups > 2
-    p_send, p_recv = v["io"] if lend else v["p_send"], v["p_recv"]
+    p_send, p_recv = v.io if lend else v.p_send, v.p_recv
 
     def store_into(ref, kind):
         def store(lane, value):
@@ -1164,7 +1174,7 @@
         target(lane, dot(left[...], wdown[:, :, :, lane].reshape(units, tile)))
 
     r_up = Reduce(
-        place, wires, wup, h_up, False, v["c_up"], None, v["y_up"], v["z_up"], v["p_up"]
+        place, wires, wup, h_up, False, v.c_up, None, v.y_up, v.z_up, v.p_up
     )
 
     @step
@@ -1196,7 +1206,7 @@
             r_down.core_add(0)
             r_down.core_add(1)
 
-    sums = v["sums"]
+    sums = v.sums
     sums[...] = jnp.zeros_like(sums)
 
     def column_sums(read, count, wide):
@@ -1220,7 +1230,7 @@
             sums[6:7, 0:units] = ghid_sum
         sums[5:6] = column_sums(lambda i: cot_all[g, aligned(i * chunk, chunk)], per_block, width)
 
-    gb = v["gb"]
+    gb = v.gb
 
     @step
     def norm_second():
@@ -1241,7 +1251,7 @@
         sums[3:4] = gain_sum
         sums[4:5] = bias_sum
 
-    ga_in, ga_send = v["ga_in"], att_send
+    ga_in, ga_send = v.ga_in, att_send
     ga_first = wires.take(groups)
 
     def ga_copy(step):
@@ -1276,7 +1286,7 @@
         for step in range(1, groups)
     ]
     r_out = Reduce(
-        place, wires, wout, h_out, True, v["c_out"], v["x_out"], v["y_out"], v["z_out"], v["p_out"]
+        place, wires, wout, h_out, True, v.c_out, v.x_out, v.y_out, v.z_out, v.p_out
     )
 
     @step
@@ -1286,7 +1296,7 @@
         r_out.core_send(0)
         r_out.core_send(1)
 
-    gm = v["gm"]
+    gm = v.gm
 
     def dkv_lanes(core, start, size):
         return aligned(core * 2 * cols + start, size)
@@ -1435,9 +1445,9 @@
             for i in range(size // rows):
                 own_parts[j * (size // rows) + i][...] = value[:, i * rows : (i + 1) * rows]
 
-    c_qkv = v["c_up"].at[:, :, :, 0 : 3 * cols]
+    c_qkv = v.c_up.at[:, :, :, 0 : 3 * cols]
     r_qkv = Reduce(
-        place, wires, wqkv, h_qkv, False, c_qkv, None, v["y_qkv"], v["z_qkv"], v["p_qkv"]
+        place, wires, wqkv, h_qkv, False, c_qkv, None, v.y_qkv, v.z_qkv, v.p_qkv
     )
 
     @step
@@ -1448,11 +1458,11 @@
     @step
     def up_free():
         r_up.y_sent()
-        pl.semaphore_signal(v["free_sem"], inc=1, device_id=place.c_peer(), device_id_type=MESH)
+        pl.semaphore_signal(v.free_sem, inc=1, device_id=place.c_peer(), device_id_type=MESH)
 
     @step
     def qkv_send():
-        pl.semaphore_wait(v["free_sem"], 1)
+        pl.semaphore_wait(v.free_sem, 1)
         r_qkv.core_send(0)
         r_qkv.core_send(1)
 
@@ -1473,7 +1483,7 @@
         sums[1:2] = gain_sum
         sums[2:3] = bias_sum
 
-    gmx = v["gmx"]
+    gmx = v.gmx
     merged_copies = []
     if sizes.pair:
         other_cols = aligned((1 - g) * cols, cols)
@@ -1487,7 +1497,7 @@
         if sizes.pair:
             gmx[0] = gb[:, own_cols]
 
-    sum_in = v["sum_in"]
+    sum_in = v.sum_in
 
     def sum_copy(slot, peer):
         return wires.copy(lambda: (sums, sum_in.at[slot], peer()))
@@ -1496,7 +1506,7 @@
     sum_x = [sum_copy(k, functools.partial(place.x_peer, k)) for k in range(1, groups)]
     sum_y = sum_copy(groups, place.y_peer)
     sum_z = [sum_copy(groups + k, functools.partial(place.z_peer, k)) for k in range(1, nz)]
-    o_up = v["o_up"]
+    o_up = v.o_up
     up_swap = Exchange(place, wires)
     up_copies = [up_swap.copy(k, lambda: o_up.at[g], lambda: o_up.at[g]) for k in range(1, groups)]
 
@@ -1533,7 +1543,7 @@
         for k in range(1, nz):
             sums[...] = sums[...] + sum_in[groups + k]
         o_up[g] = sums[...]
-        v["o_small"][...] = sums[...]
+        v.o_small[...] = sums[...]
         start_all(up_copies)
 
     stores = []
@@ -1556,7 +1566,7 @@
 
         loop(count, body)
         for half, name in enumerate(("o_frames", "o_skip")):
-            stores.append(pltpu.make_async_copy(gj.at[half], v[name].at[0], local.at[1 + half]))
+            stores.append(pltpu.make_async_copy(gj.at[half], getattr(v, name).at[0], local.at[1 + half]))
             stores[-1].start()
 
     @step
@@ -1572,16 +1582,16 @@
             ob[at] = value.astype(LOW)
 
         loop(rows // chunk, out_rows)
-        stores.append(pltpu.make_async_copy(ob, v["o_out"].at[0], local.at[0]))
+        stores.append(pltpu.make_async_copy(ob, v.o_out.at[0], local.at[0]))
         stores[-1].start()
 
     if sizes.pair:
-        grad_skip, c_skip = wdown.at[:, :, :, 0:cols], v["c_down"].at[:, :, :, 0:cols]
+        grad_skip, c_skip = wdown.at[:, :, :, 0:cols], v.c_down.at[:, :, :, 0:cols]
     else:
-        grad_skip, c_skip = ws, v["c_skip"]
+        grad_skip, c_skip = ws, v.c_skip
     r_skip = Reduce(
-        place, wires, grad_skip, h_skip, not sizes.pair, c_skip, v["x_skip"], v["y_skip"],
-        v["z_skip"], v["p_skip"],
+        place, wires, grad_skip, h_skip, not sizes.pair, c_skip, v.x_skip, v.y_skip,
+        v.z_skip, v.p_skip,
     )
 
     @step
@@ -1590,7 +1600,7 @@
             for copy in joined_copies + merged_copies:
                 copy.wait()
             for half in range(2):
-                lefts = [v["io"].at[half], v["joined"].at[half]]
+                lefts = [v.io.at[half], v.joined.at[half]]
                 weight_grad(lefts, gmx, grad_skip, half * (nz // 2))
         else:
             give_inputs()
@@ -1627,6 +1637,31 @@
     if r_skip.spread:
         steps["rs_c1"] = lambda: [r_skip.core_add(1), r_skip.x_add(0), r_skip.x_add(1)]
 
+    @step
+    def skips_sent():
+        for gather in [g_small, *gathers[6:]] + ([g_skip] if sizes.pair else []):
+            gather.drain()
+
+    @step
+    def blocks_sent():
+        sent_all(seg_copies + [seg_core] + kv_waits + [ga_copy(k) for k in range(1, groups)])
+
+    @step
+    def parts_gone():
+        if sizes.pair:
+            sent_all(out_copies)
+            parts_sent(mix_first)
+        sent_all([dkv_copy()])
+
+    def reduced_end(reduced):
+        reduced.finish()
+        reduced.drain()
+
+    steps["rd_e"] = functools.partial(reduced_end, r_down)
+    steps["ru_e"] = functools.partial(reduced_end, r_up)
+    steps["ro_e"] = functools.partial(reduced_end, r_out)
+    steps["rq_e"] = functools.partial(reduced_end, r_qkv)
+
     assert sorted(ORDER) == sorted(steps), set(ORDER) ^ set(steps)
     order = list(ORDER)
     if not early:
@@ -1638,15 +1673,10 @@
 
     for copy in up_copies:
         copy.wait()
-    for reduced in (r_up, r_down, r_out, r_qkv, r_skip):
-        reduced.finish()
-        reduced.drain()
-    for gather in [g_small, *gathers[6:]] + ([g_skip] if sizes.pair else []):
-        gather.drain()
-    sent_all(seg_copies + [seg_core] + kv_waits + out_copies)
-    sent_all([ga_copy(step) for step in range(1, groups)] + [dkv_copy()])
-    if sizes.pair:
-        parts_sent(mix_first)
+    r_skip.finish()
+    r_skip.drain()
+    if not sizes.pair:
+        sent_all(out_copies)
     for store in stores:
         store.wait()
 

time: 212 us -> 205 us (0.967)
  Pallas kernels: 211 us -> 203 us
    pallas_call x1, Pallas kernels: 204 us -> 196 us  [per_device(): pl.pallas_call(functools.partial(kernel, sizes), out_shape=(whole, whole,...]
where the time goes in v4:
time: 205 us; the launch traced here: 204 us
  Pallas kernels  203 us (99%)
    pallas_call x1, Pallas kernels, per_device(): pl.pallas_call(functools.partial(kernel, sizes), out_shape=(whole, whole,...  196 us
    pallas_call x1, Pallas kernels, per_device(): pl.pallas_call(functools.partial(finish, sizes), out_shape=(whole,) * 3 +...  6.83 us

profile of v4, /device:TPU:0, one launch (start us, length us, event | category | flops | bytes accessed | tf_op | source)
XLA Modules:
  0.0 204.2 jit_solution(1849107730444512047)
XLA Ops:
  0.7 196.5 %shard_map.271 = (bf16[1,256,1024]{2,1,0:T(8,128)(2,1)}, bf16[1,256,1024]{2,1,0:T(8,128)(2,1)}, bf16[1,256,1024]{2,1,0:T(8,128)(2,1)}, bf16[2,2,128,512]{3,2,1,0...) custom-call(bf16[1,256,1024]{2,1,0:T(8,128)(2,1)} %frames.1, ...), custom_call_target="tpu_custom_call" | custom-call | tf_op jit(solution)/shard_map/pallas_call | solution.py:1823
  197.2 6.8 %shard_map.272 = (bf16[1,256,1024]{2,1,0:T(8,128)(2,1)}, bf16[1,256,1024]{2,1,0:T(8,128)(2,1)}, bf16[1,256,1024]{2,1,0:T(8,128)(2,1)}, f32[256,1024]{1,0:T(8,128...) custom-call(bf16[1,256,1024]{2,1,0:T(8,128)(2,1)} %get-tuple-element, ...), custom_call_target="tpu_custom_call" | custom-call | tf_op jit(solution)/shard_map/pallas_call | solution.py:1845

commit v5 on v4

--- a/solution.py
+++ b/solution.py
@@ -25,7 +25,7 @@
     return lax.dot_general(left, right, (((1,), (1,)), ((), ())), preferred_element_type=F32)
 
 
-def loop(count, body, unroll=1):
+def loop(count, body, unroll=2):
     def visit(index, carry):
         body(index)
         return carry
@@ -1071,7 +1071,7 @@
                     per, 2, size // per // 2, step_cols
                 )
 
-            loop(grad.shape[3] // step_cols, inner, 2)
+            loop(grad.shape[3] // step_cols, inner)
 
         loop(count, body)
 

time: 205 us -> 201 us (0.980)
  Pallas kernels: 203 us -> 200 us
    pallas_call x1, Pallas kernels: 196 us -> 193 us  [per_device(): pl.pallas_call(functools.partial(kernel, sizes), out_shape=(whole, whole,...]
where the time goes in v5:
time: 201 us
  Pallas kernels  200 us (100%)
    pallas_call x1, Pallas kernels, per_device(): pl.pallas_call(functools.partial(kernel, sizes), out_shape=(whole, whole,...  193 us
    pallas_call x1, Pallas kernels, per_device(): pl.pallas_call(functools.partial(finish, sizes), out_shape=(whole,) * 3 +...  6.83 us

profile of v5, /device:TPU:0, one launch (start us, length us, event | category | flops | bytes accessed | tf_op | source)
XLA Modules:
  0.0 200.7 jit_solution(7341360168829626233)
XLA Ops:
  0.7 193.0 %shard_map.271 = (bf16[1,256,1024]{2,1,0:T(8,128)(2,1)}, bf16[1,256,1024]{2,1,0:T(8,128)(2,1)}, bf16[1,256,1024]{2,1,0:T(8,128)(2,1)}, bf16[2,2,128,512]{3,2,1,0...) custom-call(bf16[1,256,1024]{2,1,0:T(8,128)(2,1)} %frames.1, ...), custom_call_target="tpu_custom_call" | custom-call | tf_op jit(solution)/shard_map/pallas_call | solution.py:1823
  193.7 6.8 %shard_map.272 = (bf16[1,256,1024]{2,1,0:T(8,128)(2,1)}, bf16[1,256,1024]{2,1,0:T(8,128)(2,1)}, bf16[1,256,1024]{2,1,0:T(8,128)(2,1)}, f32[256,1024]{1,0:T(8,128...) custom-call(bf16[1,256,1024]{2,1,0:T(8,128)(2,1)} %get-tuple-element, ...), custom_call_target="tpu_custom_call" | custom-call | tf_op jit(solution)/shard_map/pallas_call | solution.py:1845
